TPU v7x, 32 devices: a whole 2x2x4 slice. The times are simulated.
32 devices in a mesh: seq: 8 (over z, y), batch: 4 (over x, core).
Axes of the slice: x: 2, y: 2, z: 4, core: 2. Of those that a mesh axis runs over, the one named last changes fastest.
Arguments:
- tokens: bfloat16 [4, 2048, 1024], P('batch', 'seq'), may hold values from -6 to 6
- w_query: float32 [1024, 1024], P('batch', 'seq'), may hold values from -0.1875 to 0.1875
- w_key: float32 [1024, 1024], P('batch', 'seq'), may hold values from -0.1875 to 0.1875
- w_value: float32 [1024, 1024], P('batch', 'seq'), may hold values from -0.1875 to 0.1875
- w_out: float32 [1024, 1024], P('batch', 'seq'), may hold values from -0.75 to 0.75
- w_ada: float32 [1024, 6144], P('batch', 'seq'), may hold values from -0.375 to 0.375
- w_up: float32 [1024, 2048], P('batch', 'seq'), may hold values from -0.1875 to 0.1875
- w_down: float32 [2048, 1024], P('batch', 'seq'), may hold values from -0.125 to 0.125
- segments: int32 [4, 2048], P('batch', 'seq'), may hold values from 0 to 15, as said below
- validity: int32 [4, 2048], P('batch', 'seq'), may hold values from 0 to 1, as said below
- timesteps: int32 [4, 16], P('batch'), may hold values from 0 to 999
- cotangent: bfloat16 [4, 2048, 1024], P('batch', 'seq'), may hold values from -6 to 6
Outputs:
- output: bfloat16 [4, 2048, 1024], P('batch', 'seq')
- grad_tokens: bfloat16 [4, 2048, 1024], P('batch', 'seq')
- grad_query: float32 [1024, 1024], P('batch', 'seq')
- grad_key: float32 [1024, 1024], P('batch', 'seq')
- grad_value: float32 [1024, 1024], P('batch', 'seq')
- grad_out: float32 [1024, 1024], P('batch', 'seq')
- grad_ada: float32 [1024, 6144], P('batch', 'seq')
- grad_up: float32 [1024, 2048], P('batch', 'seq')
- grad_down: float32 [2048, 1024], P('batch', 'seq')
Inputs may be any that keep to these rules, and one draw needn't show every extreme that they name: `segments`: in each replica one clip, drawn from the seed, holds the first rows of every device's 256 frames; the other clips' frames follow in order of clip id; every clip that has frames has frames with validity 1. `validity`: frames with 0 belong to the clip that spans every device.
All inputs are finite; a program needn't handle non-finite values.
Results may differ from a plain program's by a relative error of at most 0.018.
The roundings to bfloat16 on the way count: a program that leaves them out, or rounds other values in their place, can miss the bound.
Values may be sent and summed in bfloat16 or wider, within the bound.
No kernel may reach another device: no remote copies, remote signals or barrier semaphores. Data moves between devices by JAX's collectives and lax.ppermute only.
A program may use at most 320 MiB of HBM per device.

v0:
```python
from functools import partial
import math

import jax
import jax.numpy as jnp
from jax import lax
from jax.sharding import PartitionSpec as P

D = 1024
HEADS = 16
HEAD = 64
CLIPS = 16


def carried_in(part, axis, combine, identity):
    place = lax.axis_index(axis)
    gathered = lax.all_gather(part, axis)
    state = jnp.zeros_like(part) + jnp.asarray(identity, part.dtype)

    def one(step, state):
        return combine(state, lax.dynamic_index_in_dim(gathered, step, 0, False))

    return lax.fori_loop(0, place, one, state)


def matmul(left, right):
    return jnp.dot(left, right, preferred_element_type=jnp.float32)


def time_embedding(timestep_row):
    half_width = D // 2
    frequency = jnp.exp(-math.log(10000.0) * jnp.arange(half_width, dtype=jnp.float32) / half_width)
    angle = timestep_row.astype(jnp.float32)[:, None] * frequency[None, :]
    return jnp.concatenate([jnp.sin(angle), jnp.cos(angle)], axis=1)


def rotate_pairs(vectors, position, direction):
    half_size = vectors.shape[-1] // 2
    frequency = jnp.exp(-math.log(10000.0) * jnp.arange(half_size, dtype=jnp.float32) / half_size)
    angle = position[:, None] * frequency[None, :]
    cosine = jnp.cos(angle)[:, None, :]
    sine = jnp.sin(angle)[:, None, :] * direction
    first_half = vectors[..., :half_size]
    second_half = vectors[..., half_size:]
    return jnp.concatenate(
        [first_half * cosine - second_half * sine, second_half * cosine + first_half * sine],
        axis=-1,
    )


def normalize(inputs):
    centered = inputs - jnp.mean(inputs, axis=-1, keepdims=True)
    inverse = lax.rsqrt(jnp.mean(centered * centered, axis=-1, keepdims=True) + 1e-06)
    return (centered * inverse, inverse)


def norm_backward(grad_normed, normed, inverse):
    mean_grad = jnp.mean(grad_normed, axis=-1, keepdims=True)
    mean_mixed = jnp.mean(grad_normed * normed, axis=-1, keepdims=True)
    return inverse * (grad_normed - mean_grad - normed * mean_mixed)


def add_counts(earlier, later):
    return earlier + later


def block_rows_for(row_count):
    chosen = 1
    for candidate in range(1, 513):
        if row_count % candidate == 0:
            chosen = candidate
    return chosen


def stack_blocks(shard_piece):
    row_count = shard_piece[0].shape[0]
    block_rows = block_rows_for(row_count)
    block_count = row_count // block_rows
    return (
        shard_piece[0].reshape(block_count, block_rows, HEADS, HEAD),
        shard_piece[1].reshape(block_count, block_rows, HEADS, HEAD),
        shard_piece[2].reshape(block_count, block_rows),
    )


def forward_block(carried, key_block, queries, query_codes):
    running_max, running_sum, accumulated = carried
    key_rows, values, key_codes = key_block
    scores = (
        jnp.einsum("qhe,khe->hqk", queries, key_rows, preferred_element_type=jnp.float32) * 0.125
    )
    allowed = (query_codes[:, None] == key_codes.astype(jnp.float32)[None, :])[None]
    masked = jnp.where(allowed, scores, -1e30)
    new_max = jnp.maximum(running_max, jnp.max(masked, axis=2))
    rescale = jnp.exp(running_max - new_max)
    weights = jnp.where(allowed, jnp.exp(masked - new_max[:, :, None]), 0.0)
    running_sum = running_sum * rescale + jnp.sum(weights, axis=2)
    product = jnp.einsum(
        "hqk,khe->qhe", weights, values.astype(jnp.float32), precision=lax.Precision.HIGHEST
    )
    accumulated = accumulated * rescale.T[:, :, None] + product
    return (new_max, running_sum, accumulated)


def block_grads(key_block, queries, query_codes, grad_attn, log_total, delta_rows):
    key_rows, values, key_codes = key_block
    scores = (
        jnp.einsum("qhe,khe->hqk", queries, key_rows, preferred_element_type=jnp.float32) * 0.125
    )
    allowed = (query_codes[:, None] == key_codes.astype(jnp.float32)[None, :])[None]
    probabilities = jnp.exp(jnp.where(allowed, scores, -1e30) - log_total[:, :, None])
    grad_probs = jnp.einsum("qhe,khe->hqk", grad_attn, values, preferred_element_type=jnp.float32)
    grad_scores = (probabilities * (grad_probs - delta_rows[:, :, None])).astype(jnp.bfloat16)
    return (probabilities, grad_scores)


def body(
    tokens,
    w_query,
    w_key,
    w_value,
    w_out,
    w_ada,
    w_up,
    w_down,
    segments,
    validity,
    timesteps,
    cotangent,
):
    inputs = tokens[0].astype(jnp.float32)
    segment = segments[0]
    valid_row = validity[0]
    timestep_row = timesteps[0]
    grad_output = cotangent[0].astype(jnp.float32)
    frame_count = inputs.shape[0]
    highest = lax.Precision.HIGHEST
    cols_q, cols_k, cols_v, cols_o, cols_a, cols_u, cols_d = (
        lax.all_gather(w_query.astype(jnp.bfloat16), "seq", axis=1, tiled=True),
        lax.all_gather(w_key.astype(jnp.bfloat16), "seq", axis=1, tiled=True),
        lax.all_gather(w_value.astype(jnp.bfloat16), "seq", axis=1, tiled=True),
        lax.all_gather(w_out.astype(jnp.bfloat16), "seq", axis=1, tiled=True),
        lax.all_gather(w_ada.astype(jnp.bfloat16), "seq", axis=1, tiled=True),
        lax.all_gather(w_up.astype(jnp.bfloat16), "seq", axis=1, tiled=True),
        lax.all_gather(w_down.astype(jnp.bfloat16), "seq", axis=1, tiled=True),
    )
    full_q, full_k, full_v, full_o, full_a, full_u, full_d = (
        lax.all_gather(cols_q, "batch", axis=0, tiled=True),
        lax.all_gather(cols_k, "batch", axis=0, tiled=True),
        lax.all_gather(cols_v, "batch", axis=0, tiled=True),
        lax.all_gather(cols_o, "batch", axis=0, tiled=True),
        lax.all_gather(cols_a, "batch", axis=0, tiled=True),
        lax.all_gather(cols_u, "batch", axis=0, tiled=True),
        lax.all_gather(cols_d, "batch", axis=0, tiled=True),
    )
    silu_time = jax.nn.silu(time_embedding(timestep_row)).astype(jnp.bfloat16)
    emb_rows = matmul(silu_time, full_a)
    member = segment[:, None] == jnp.arange(CLIPS, dtype=jnp.int32)[None, :]
    one_hot = member.astype(jnp.float32)
    counted = member.astype(jnp.int32)
    modulation = jnp.dot(one_hot, emb_rows, precision=highest)
    shift_attn, scale_attn, gate_attn, shift_ffn, scale_ffn, gate_ffn = jnp.split(
        modulation, 6, axis=1
    )
    offsets = carried_in(
        jnp.sum(counted, axis=0), "seq", add_counts, jnp.zeros((CLIPS,), jnp.int32)
    )
    before = jnp.cumsum(counted, axis=0) - counted + offsets[None, :]
    position = jnp.sum(before * counted, axis=1).astype(jnp.float32)
    normed, inverse = normalize(inputs)
    attn_input = (normed * (1.0 + scale_attn) + shift_attn).astype(jnp.bfloat16)
    queries = rotate_pairs(
        matmul(attn_input, full_q).reshape(frame_count, HEADS, HEAD), position, 1.0
    ).astype(jnp.bfloat16)
    key_flat = (
        rotate_pairs(matmul(attn_input, full_k).reshape(frame_count, HEADS, HEAD), position, 1.0)
        .astype(jnp.bfloat16)
        .reshape(frame_count, D)
    )
    value_flat = matmul(attn_input, full_v).astype(jnp.bfloat16)
    key_codes = jnp.where(valid_row == 1, segment, -1).astype(jnp.bfloat16)
    query_codes = segment.astype(jnp.float32)
    start_state = (
        jnp.full((HEADS, frame_count), -1e30, jnp.float32),
        jnp.zeros((HEADS, frame_count), jnp.float32),
        jnp.zeros((frame_count, HEADS, HEAD), jnp.float32),
    )

    def step(state, key_block):
        return (forward_block(state, key_block, queries, query_codes), None)

    running_max, running_sum, accumulated = lax.scan(
        step,
        start_state,
        stack_blocks(
            (
                lax.all_gather(key_flat, "seq", axis=0, tiled=True),
                lax.all_gather(value_flat, "seq", axis=0, tiled=True),
                lax.all_gather(key_codes, "seq", axis=0, tiled=True),
            )
        ),
    )[0]
    attended = accumulated / running_sum.T[:, :, None]
    log_total = running_max + jnp.log(running_sum)
    attended_low = attended.reshape(frame_count, D).astype(jnp.bfloat16)
    attn_branch = matmul(attended_low, full_o)
    middle = inputs + gate_attn * attn_branch
    normed_mid, inverse_mid = normalize(middle)
    ffn_input = (normed_mid * (1.0 + scale_ffn) + shift_ffn).astype(jnp.bfloat16)
    hidden = matmul(ffn_input, full_u)
    activated, gelu_pull = jax.vjp(partial(jax.nn.gelu, approximate=True), hidden)
    activated_low = activated.astype(jnp.bfloat16)
    ffn_branch = matmul(activated_low, full_d)
    result = middle + gate_ffn * ffn_branch
    back_q, back_k, back_v, back_o, back_u, back_d = (
        full_q,
        full_k,
        full_v,
        full_o,
        full_u,
        full_d,
    )
    grad_gate_ffn = grad_output * ffn_branch
    g_ffn = (grad_output * gate_ffn).astype(jnp.bfloat16)
    grad_down_local = matmul(activated_low.T, g_ffn)
    grad_activated = matmul(g_ffn, back_d.T)
    g_hidden = gelu_pull(grad_activated)[0].astype(jnp.bfloat16)
    grad_up_local = matmul(ffn_input.T, g_hidden)
    grad_ffn_input = matmul(g_hidden, back_u.T)
    grad_middle = grad_output + norm_backward(
        grad_ffn_input * (1.0 + scale_ffn), normed_mid, inverse_mid
    )
    grad_scale_ffn = grad_ffn_input * normed_mid
    grad_gate_attn = grad_middle * attn_branch
    g_attn = (grad_middle * gate_attn).astype(jnp.bfloat16)
    grad_out_local = matmul(attended_low.T, g_attn)
    grad_attn = matmul(g_attn, back_o.T).astype(jnp.bfloat16).reshape(frame_count, HEADS, HEAD)
    delta_rows = jnp.einsum("qhe,qhe->hq", grad_attn.astype(jnp.float32), attended)
    zero_query = jnp.zeros((frame_count, HEADS, HEAD), jnp.float32)
    gathered = (
        lax.all_gather(key_flat, "seq", axis=0, tiled=True),
        lax.all_gather(value_flat, "seq", axis=0, tiled=True),
        lax.all_gather(key_codes, "seq", axis=0, tiled=True),
    )
    pack_rows = gathered[0].shape[0]
    grad_attn_wide = grad_attn.astype(jnp.float32)

    def joint_step(total_grad, key_block):
        probabilities, grad_scores = block_grads(
            key_block, queries, query_codes, grad_attn, log_total, delta_rows
        )
        total_grad = total_grad + 0.125 * jnp.einsum(
            "hqk,khe->qhe", grad_scores, key_block[0], preferred_element_type=jnp.float32
        )
        grad_keys = 0.125 * jnp.einsum(
            "hqk,qhe->khe", grad_scores, queries, preferred_element_type=jnp.float32
        )
        grad_values = jnp.einsum("hqk,qhe->khe", probabilities, grad_attn_wide, precision=highest)
        return (total_grad, (grad_keys, grad_values))

    grad_queries_rot, both_grads = lax.scan(joint_step, zero_query, stack_blocks(gathered))
    key_value_terms = jnp.concatenate(
        [both_grads[0].reshape(pack_rows, D), both_grads[1].reshape(pack_rows, D)], axis=1
    )
    key_value_grad = lax.psum_scatter(key_value_terms, "seq", scatter_dimension=0, tiled=True)
    g_query = (
        rotate_pairs(grad_queries_rot, position, -1.0).reshape(frame_count, D).astype(jnp.bfloat16)
    )
    g_key = (
        rotate_pairs(key_value_grad[:, :D].reshape(frame_count, HEADS, HEAD), position, -1.0)
        .reshape(frame_count, D)
        .astype(jnp.bfloat16)
    )
    g_value = key_value_grad[:, D:].astype(jnp.bfloat16)
    grad_query_local = matmul(attn_input.T, g_query)
    grad_key_local = matmul(attn_input.T, g_key)
    grad_value_local = matmul(attn_input.T, g_value)
    grad_attn_input = (
        matmul(g_query, back_q.T) + matmul(g_key, back_k.T) + matmul(g_value, back_v.T)
    )
    grad_inputs = grad_middle + norm_backward(grad_attn_input * (1.0 + scale_attn), normed, inverse)
    grad_modulation = jnp.concatenate(
        [
            grad_attn_input,
            grad_attn_input * normed,
            grad_gate_attn,
            grad_ffn_input,
            grad_scale_ffn,
            grad_gate_ffn,
        ],
        axis=1,
    )
    grad_emb = jnp.dot(one_hot.T, grad_modulation, precision=highest)
    grad_ada_local = jnp.dot(silu_time.astype(jnp.float32).T, grad_emb, precision=highest)
    part_q, part_k, part_v, part_o, part_a, part_u, part_d = (
        lax.psum_scatter(grad_query_local, "seq", scatter_dimension=1, tiled=True),
        lax.psum_scatter(grad_key_local, "seq", scatter_dimension=1, tiled=True),
        lax.psum_scatter(grad_value_local, "seq", scatter_dimension=1, tiled=True),
        lax.psum_scatter(grad_out_local, "seq", scatter_dimension=1, tiled=True),
        lax.psum_scatter(grad_ada_local, "seq", scatter_dimension=1, tiled=True),
        lax.psum_scatter(grad_up_local, "seq", scatter_dimension=1, tiled=True),
        lax.psum_scatter(grad_down_local, "seq", scatter_dimension=1, tiled=True),
    )
    final_q, final_k, final_v, final_o, final_a, final_u, final_d = (
        lax.psum_scatter(
            part_q.astype(jnp.bfloat16), "batch", scatter_dimension=0, tiled=True
        ).astype(jnp.float32),
        lax.psum_scatter(
            part_k.astype(jnp.bfloat16), "batch", scatter_dimension=0, tiled=True
        ).astype(jnp.float32),
        lax.psum_scatter(
            part_v.astype(jnp.bfloat16), "batch", scatter_dimension=0, tiled=True
        ).astype(jnp.float32),
        lax.psum_scatter(
            part_o.astype(jnp.bfloat16), "batch", scatter_dimension=0, tiled=True
        ).astype(jnp.float32),
        lax.psum_scatter(
            part_a.astype(jnp.bfloat16), "batch", scatter_dimension=0, tiled=True
        ).astype(jnp.float32),
        lax.psum_scatter(
            part_u.astype(jnp.bfloat16), "batch", scatter_dimension=0, tiled=True
        ).astype(jnp.float32),
        lax.psum_scatter(
            part_d.astype(jnp.bfloat16), "batch", scatter_dimension=0, tiled=True
        ).astype(jnp.float32),
    )
    return (
        result.astype(jnp.bfloat16)[None],
        grad_inputs.astype(jnp.bfloat16)[None],
        final_q,
        final_k,
        final_v,
        final_o,
        final_a,
        final_u,
        final_d,
    )


def solution(mesh):
    return jax.shard_map(
        body,
        mesh=mesh,
        in_specs=(
            P("batch", "seq", None),
            P("batch", "seq"),
            P("batch", "seq"),
            P("batch", "seq"),
            P("batch", "seq"),
            P("batch", "seq"),
            P("batch", "seq"),
            P("batch", "seq"),
            P("batch", "seq"),
            P("batch", "seq"),
            P("batch", None),
            P("batch", "seq", None),
        ),
        out_specs=(
            P("batch", "seq", None),
            P("batch", "seq", None),
            P("batch", "seq"),
            P("batch", "seq"),
            P("batch", "seq"),
            P("batch", "seq"),
            P("batch", "seq"),
            P("batch", "seq"),
            P("batch", "seq"),
        ),
        check_vma=False,
    )
```

profile of v0, /device:TPU:13, one launch (start us, length us, event | category | flops | bytes accessed | tf_op | source)
XLA Modules:
  0.0 2572.8 jit_solution(18041784955160104854)
XLA Ops:
  9.4 61.3 %all-gather.15.cloned.1.call-done = bf16[256,6144]{1,0:T(8,128)(2,1)} async-done(((bf16[256,768]{1,0:T(8,128)(2,1)}), bf16[256,6144]{1,0:T(8,128)(2,1)}) %all-gather.15.cloned.1.call-update) | async-done | bytes 3145744 | tf_op jit(solution)/shard_map/all_gather | solution.py:143
  94.1 24.0 all_gather.63
  280.2 30.1 %all-gather.35.cloned.1.call-done = bf16[512,1024]{1,0:T(8,128)(2,1)} async-done(((bf16[512,128]{1,0:T(8,128)(2,1)}), bf16[512,1024]{1,0:T(8,128)(2,1)}) %all-gather.35.cloned.1.call-update) | async-done | bytes 1048592 | tf_op jit(solution)/shard_map/all_gather | solution.py:145
  310.6 75.4 %all-gather.21.cloned.1.call-done = bf16[2048,1024]{0,1:T(8,128)(2,1)} async-done(((bf16[256,1024]{0,1:T(8,128)(2,1)}), bf16[2048,1024]{0,1:T(8,128)(2,1)}) %all-gather.21.cloned.1.call-update) | async-done | bytes 4194320 | tf_op jit(solution)/shard_map/all_gather | solution.py:197
  399.2 61.6 %all-gather.27.cloned.1.call-done = bf16[2048,1024]{1,0:T(8,128)(2,1)} async-done(((bf16[256,1024]{1,0:T(8,128)(2,1)}), bf16[2048,1024]{1,0:T(8,128)(2,1)}) %all-gather.27.cloned.1.call-update) | async-done | bytes 4194320 | tf_op jit(solution)/shard_map/all_gather | solution.py:198
  482.3 46.3 %while.41 = (s32[]{:T(128)}, f32[16,256]{1,0:T(8,128)S(1)}, f32[16,256]{1,0:T(8,128)S(1)}, f32[256,16,64]{0,2,1:T(8,128)S(1)}, f32[256]{0:T(256)S(1)}, /*index=5...) while((s32[]{:T(128)}, f32[16,256]{1,0:T(8,128)S(1)}, ...), condition=%wide.region_11.12_spmd.clone, body=%wide.region_8.11_spmd.clone.sunk | while | flops 1905156608 | bytes 30677132 | solution.py:192
  576.3 434.8 %while.42 = (s32[]{:T(128)}, f32[256,16,64]{0,2,1:T(8,128)}, f32[4,512,16,64]{1,0,3,2:T(4,128)}, f32[4,512,16,64]{1,0,3,2:T(4,128)}, bf16[4,512,16,64]{1,3,2,0:T...) while((s32[]{:T(128)}, f32[256,16,64]{0,2,1:T(8,128)}, ...), condition=%wide.region_17.18_spmd.clone, body=%wide.region_16.17_spmd.clone.sunk | while | flops 2704671232 | bytes 75421936 | solution.py:261
  603.3 41.0 %dynamic_update_slice.11 = f32[4,512,16,64]{1,0,3,2:T(4,128)} dynamic-update-slice(f32[4,512,16,64]{1,0,3,2:T(4,128)} %get-tuple-element.646, f32[1,512,16,64]{1,0,3,2:T(1,128)} %copy.113, s32[]{:T(128)S(6)} %copy.140, s32[]{:T(128)} %constant.90.clone.1..sunk.2, s32[]{:T(128)} %constant.90.clone.1..sunk.2, s32[]{:T(128)} %constant.90.clone.1..sunk.2) | dynamic-update-slice | bytes 4194308 | tf_op jit(solution)/shard_map/while/body/jit(dynamic_update_index_in_dim)/dynamic_update_slice | solution.py:261
  644.2 40.8 %dynamic_update_slice.12 = f32[4,512,16,64]{1,0,3,2:T(4,128)} dynamic-update-slice(f32[4,512,16,64]{1,0,3,2:T(4,128)} %get-tuple-element.647, f32[1,512,16,64]{1,0,3,2:T(1,128)S(1)} %copy.114, s32[]{:T(128)S(6)} %copy.140, s32[]{:T(128)} %constant.90.clone.1..sunk.2, s32[]{:T(128)} %constant.90.clone.1..sunk.2, s32[]{:T(128)} %constant.90.clone.1..sunk.2) | dynamic-update-slice | bytes 4194308 | tf_op jit(solution)/shard_map/while/body/jit(dynamic_update_index_in_dim)/dynamic_update_slice | solution.py:261
  711.8 41.0 %dynamic_update_slice.11 = f32[4,512,16,64]{1,0,3,2:T(4,128)} dynamic-update-slice(f32[4,512,16,64]{1,0,3,2:T(4,128)} %get-tuple-element.646, f32[1,512,16,64]{1,0,3,2:T(1,128)} %copy.113, s32[]{:T(128)S(6)} %copy.140, s32[]{:T(128)} %constant.90.clone.1..sunk.2, s32[]{:T(128)} %constant.90.clone.1..sunk.2, s32[]{:T(128)} %constant.90.clone.1..sunk.2) | dynamic-update-slice | bytes 4194308 | tf_op jit(solution)/shard_map/while/body/jit(dynamic_update_index_in_dim)/dynamic_update_slice | solution.py:261
  752.8 40.8 %dynamic_update_slice.12 = f32[4,512,16,64]{1,0,3,2:T(4,128)} dynamic-update-slice(f32[4,512,16,64]{1,0,3,2:T(4,128)} %get-tuple-element.647, f32[1,512,16,64]{1,0,3,2:T(1,128)S(1)} %copy.114, s32[]{:T(128)S(6)} %copy.140, s32[]{:T(128)} %constant.90.clone.1..sunk.2, s32[]{:T(128)} %constant.90.clone.1..sunk.2, s32[]{:T(128)} %constant.90.clone.1..sunk.2) | dynamic-update-slice | bytes 4194308 | tf_op jit(solution)/shard_map/while/body/jit(dynamic_update_index_in_dim)/dynamic_update_slice | solution.py:261
  820.4 41.0 %dynamic_update_slice.11 = f32[4,512,16,64]{1,0,3,2:T(4,128)} dynamic-update-slice(f32[4,512,16,64]{1,0,3,2:T(4,128)} %get-tuple-element.646, f32[1,512,16,64]{1,0,3,2:T(1,128)} %copy.113, s32[]{:T(128)S(6)} %copy.140, s32[]{:T(128)} %constant.90.clone.1..sunk.2, s32[]{:T(128)} %constant.90.clone.1..sunk.2, s32[]{:T(128)} %constant.90.clone.1..sunk.2) | dynamic-update-slice | bytes 4194308 | tf_op jit(solution)/shard_map/while/body/jit(dynamic_update_index_in_dim)/dynamic_update_slice | solution.py:261
  861.4 40.8 %dynamic_update_slice.12 = f32[4,512,16,64]{1,0,3,2:T(4,128)} dynamic-update-slice(f32[4,512,16,64]{1,0,3,2:T(4,128)} %get-tuple-element.647, f32[1,512,16,64]{1,0,3,2:T(1,128)S(1)} %copy.114, s32[]{:T(128)S(6)} %copy.140, s32[]{:T(128)} %constant.90.clone.1..sunk.2, s32[]{:T(128)} %constant.90.clone.1..sunk.2, s32[]{:T(128)} %constant.90.clone.1..sunk.2) | dynamic-update-slice | bytes 4194308 | tf_op jit(solution)/shard_map/while/body/jit(dynamic_update_index_in_dim)/dynamic_update_slice | solution.py:261
  929.0 41.0 %dynamic_update_slice.11 = f32[4,512,16,64]{1,0,3,2:T(4,128)} dynamic-update-slice(f32[4,512,16,64]{1,0,3,2:T(4,128)} %get-tuple-element.646, f32[1,512,16,64]{1,0,3,2:T(1,128)} %copy.113, s32[]{:T(128)S(6)} %copy.140, s32[]{:T(128)} %constant.90.clone.1..sunk.2, s32[]{:T(128)} %constant.90.clone.1..sunk.2, s32[]{:T(128)} %constant.90.clone.1..sunk.2) | dynamic-update-slice | bytes 4194308 | tf_op jit(solution)/shard_map/while/body/jit(dynamic_update_index_in_dim)/dynamic_update_slice | solution.py:261
  969.9 40.8 %dynamic_update_slice.12 = f32[4,512,16,64]{1,0,3,2:T(4,128)} dynamic-update-slice(f32[4,512,16,64]{1,0,3,2:T(4,128)} %get-tuple-element.647, f32[1,512,16,64]{1,0,3,2:T(1,128)S(1)} %copy.114, s32[]{:T(128)S(6)} %copy.140, s32[]{:T(128)} %constant.90.clone.1..sunk.2, s32[]{:T(128)} %constant.90.clone.1..sunk.2, s32[]{:T(128)} %constant.90.clone.1..sunk.2) | dynamic-update-slice | bytes 4194308 | tf_op jit(solution)/shard_map/while/body/jit(dynamic_update_index_in_dim)/dynamic_update_slice | solution.py:261
  1050.0 263.3 %reduce-scatter.16.cloned.1.call-done = f32[256,2048]{0,1:T(8,128)} async-done(((f32[2048,2048]{0,1:T(8,128)}), f32[256,2048]{0,1:T(8,128)}) %reduce-scatter.16.cloned.1.call-update) | async-done | bytes 2097168 | tf_op jit(solution)/shard_map/reduce_scatter | solution.py:265
  1352.4 54.1 %reduce-scatter.30.cloned.1.call-done = f32[1024,128]{1,0:T(8,128)} async-done(((f32[1024,1024]{1,0:T(8,128)}), f32[1024,128]{1,0:T(8,128)}) %reduce-scatter.30.cloned.1.call-update) | async-done | bytes 524304 | tf_op jit(solution)/shard_map/reduce_scatter | solution.py:299
  1408.4 149.2 %reduce-scatter.42.cloned.1.call-done = f32[2048,128]{1,0:T(8,128)} async-done(((f32[2048,1024]{1,0:T(8,128)}), f32[2048,128]{1,0:T(8,128)}) %reduce-scatter.42.cloned.1.call-update) | async-done | bytes 1048592 | tf_op jit(solution)/shard_map/reduce_scatter | solution.py:302
  1559.8 150.2 %reduce-scatter.38.cloned.1.call-done = f32[1024,256]{1,0:T(8,128)} async-done(((f32[1024,2048]{1,0:T(8,128)}), f32[1024,256]{1,0:T(8,128)}) %reduce-scatter.38.cloned.1.call-update) | async-done | bytes 1048592 | tf_op jit(solution)/shard_map/reduce_scatter | solution.py:301
  1712.1 90.4 %reduce-scatter.22.cloned.1.call-done = f32[1024,128]{1,0:T(8,128)} async-done(((f32[1024,1024]{1,0:T(8,128)}), f32[1024,128]{1,0:T(8,128)}) %reduce-scatter.22.cloned.1.call-update) | async-done | bytes 524304 | tf_op jit(solution)/shard_map/reduce_scatter | solution.py:297
  1804.4 90.3 %reduce-scatter.18.cloned.1.call-done = f32[1024,128]{1,0:T(8,128)} async-done(((f32[1024,1024]{1,0:T(8,128)}), f32[1024,128]{1,0:T(8,128)}) %reduce-scatter.18.cloned.1.call-update) | async-done | bytes 524304 | tf_op jit(solution)/shard_map/reduce_scatter | solution.py:296
  1896.6 90.0 %reduce-scatter.26.cloned.1.call-done = f32[1024,128]{1,0:T(8,128)} async-done(((f32[1024,1024]{1,0:T(8,128)}), f32[1024,128]{1,0:T(8,128)}) %reduce-scatter.26.cloned.1.call-update) | async-done | bytes 524304 | tf_op jit(solution)/shard_map/reduce_scatter | solution.py:298
  1988.4 404.0 %reduce-scatter.34.cloned.1.call-done = f32[1024,768]{1,0:T(8,128)} async-done(((f32[1024,6144]{1,0:T(8,128)}), f32[1024,768]{1,0:T(8,128)}) %reduce-scatter.34.cloned.1.call-update) | async-done | bytes 3145744 | tf_op jit(solution)/shard_map/reduce_scatter | solution.py:300
  2534.5 29.3 %reduce-scatter.36.cloned.1.call-done = bf16[256,768]{1,0:T(8,128)(2,1)} async-done(((bf16[1024,768]{1,0:T(8,128)(2,1)}), bf16[256,768]{1,0:T(8,128)(2,1)}) %reduce-scatter.36.cloned.1.call-update) | async-done | bytes 393232 | tf_op jit(solution)/shard_map/reduce_scatter | solution.py:317
  (400 shorter events, 654.6 us)
Async XLA Ops:
  9.3 147.0 %all-gather.17.cloned.1.call-start = ((), (), s32[]{:S(2)}) async-start(), calls=%async_computation.16 | async-start | bytes 15728640 | tf_op jit(solution)/shard_map/all_gather | solution.py:152
  94.0 109.2 %all-gather.19.cloned.1.call-start = ((), (), s32[]{:S(2)}) async-start(), calls=%async_computation.17 | async-start | bytes 2621440 | tf_op jit(solution)/shard_map/all_gather | solution.py:149
  141.5 127.7 %all-gather.31.cloned.1.call-start = ((), (), s32[]{:S(2)}) async-start(), calls=%async_computation.23 | async-start | bytes 1179648 | tf_op jit(solution)/shard_map/all_gather | solution.py:144
  142.2 168.1 %all-gather.35.cloned.1.call-start = ((), (), s32[]{:S(2)}) async-start(), calls=%async_computation.25 | async-start | bytes 1179648 | tf_op jit(solution)/shard_map/all_gather | solution.py:145
  143.0 243.0 %all-gather.21.cloned.1.call-start = ((), (), s32[]{:S(2)}) async-start(), calls=%async_computation.18 | async-start | bytes 4718592 | tf_op jit(solution)/shard_map/all_gather | solution.py:197
  207.7 253.1 %all-gather.27.cloned.1.call-start = ((), (), s32[]{:S(2)}) async-start(), calls=%async_computation.21 | async-start | bytes 4718592 | tf_op jit(solution)/shard_map/all_gather | solution.py:198
  230.4 300.7 %all-gather.29.cloned.1.call-start = ((), (), s32[]{:S(2)}) async-start(), calls=%async_computation.22 | async-start | bytes 2621440 | tf_op jit(solution)/shard_map/all_gather | solution.py:151
  254.5 282.8 %all-gather.33.cloned.1.call-start = ((), (), s32[]{:S(2)}) async-start(), calls=%async_computation.24 | async-start | bytes 5242880 | tf_op jit(solution)/shard_map/all_gather | solution.py:153
  269.2 288.9 %all-gather.37.cloned.1.call-start = ((), (), s32[]{:S(2)}) async-start(), calls=%async_computation.26 | async-start | bytes 5242880 | tf_op jit(solution)/shard_map/all_gather | solution.py:154
  310.3 1003.0 %reduce-scatter.16.cloned.1.call-start = ((), (), s32[]{:S(2)}) async-start(), calls=%async_computation.27 | async-start | bytes 18874368 | tf_op jit(solution)/shard_map/reduce_scatter | solution.py:265
  1032.4 374.2 %reduce-scatter.30.cloned.1.call-start = ((), (), s32[]{:S(2)}) async-start(), calls=%async_computation.34 | async-start | bytes 4718592 | tf_op jit(solution)/shard_map/reduce_scatter | solution.py:299
  1036.1 521.5 %reduce-scatter.42.cloned.1.call-start = ((), (), s32[]{:S(2)}) async-start(), calls=%async_computation.40 | async-start | bytes 9437184 | tf_op jit(solution)/shard_map/reduce_scatter | solution.py:302
  1044.0 666.0 %reduce-scatter.38.cloned.1.call-start = ((), (), s32[]{:S(2)}) async-start(), calls=%async_computation.38 | async-start | bytes 9437184 | tf_op jit(solution)/shard_map/reduce_scatter | solution.py:301
  1050.0 752.6 %reduce-scatter.22.cloned.1.call-start = ((), (), s32[]{:S(2)}) async-start(), calls=%async_computation.30 | async-start | bytes 4718592 | tf_op jit(solution)/shard_map/reduce_scatter | solution.py:297
  1318.5 576.2 %reduce-scatter.18.cloned.1.call-start = ((), (), s32[]{:S(2)}) async-start(), calls=%async_computation.28 | async-start | bytes 4718592 | tf_op jit(solution)/shard_map/reduce_scatter | solution.py:296
  1321.4 665.2 %reduce-scatter.26.cloned.1.call-start = ((), (), s32[]{:S(2)}) async-start(), calls=%async_computation.32 | async-start | bytes 4718592 | tf_op jit(solution)/shard_map/reduce_scatter | solution.py:298
  1325.4 1067.0 %reduce-scatter.34.cloned.1.call-start = ((), (), s32[]{:S(2)}) async-start(), calls=%async_computation.36 | async-start | bytes 28311552 | tf_op jit(solution)/shard_map/reduce_scatter | solution.py:300
  1352.4 1064.1 %reduce-scatter.32.cloned.1.call-start = ((), (), s32[]{:S(2)}) async-start(), calls=%async_computation.35 | async-start | bytes 327680 | tf_op jit(solution)/shard_map/reduce_scatter | solution.py:314
  1408.3 1032.4 %reduce-scatter.44.cloned.1.call-start = ((), (), s32[]{:S(2)}) async-start(), calls=%async_computation.41 | async-start | bytes 655360 | tf_op jit(solution)/shard_map/reduce_scatter | solution.py:323
  1559.8 905.9 %reduce-scatter.40.cloned.1.call-start = ((), (), s32[]{:S(2)}) async-start(), calls=%async_computation.39 | async-start | bytes 655360 | tf_op jit(solution)/shard_map/reduce_scatter | solution.py:320
  1712.1 775.9 %reduce-scatter.24.cloned.1.call-start = ((), (), s32[]{:S(2)}) async-start(), calls=%async_computation.31 | async-start | bytes 327680 | tf_op jit(solution)/shard_map/reduce_scatter | solution.py:308
  1804.3 706.3 %reduce-scatter.20.cloned.1.call-start = ((), (), s32[]{:S(2)}) async-start(), calls=%async_computation.29 | async-start | bytes 327680 | tf_op jit(solution)/shard_map/reduce_scatter | solution.py:305
  1896.5 636.5 %reduce-scatter.28.cloned.1.call-start = ((), (), s32[]{:S(2)}) async-start(), calls=%async_computation.33 | async-start | bytes 327680 | tf_op jit(solution)/shard_map/reduce_scatter | solution.py:311
  1988.4 575.5 %reduce-scatter.36.cloned.1.call-start = ((), (), s32[]{:S(2)}) async-start(), calls=%async_computation.37 | async-start | bytes 1966080 | tf_op jit(solution)/shard_map/reduce_scatter | solution.py:317
  (75 other events, 3023.8 us)
Sparse Core Ops, SparseCore 0:
  10.8 59.7 all-gather.14
  72.2 82.7 all-gather.16
  156.6 22.5 all-gather.22
  180.7 22.5 all-gather.18
  204.7 22.5 all-gather.24
  229.8 39.3 all-gather.30
  271.8 38.4 all-gather.34
  312.9 73.0 all-gather.20
  388.7 72.0 all-gather.26
  462.2 23.8 all-gather.28
  487.7 34.4 all-gather.32
  523.6 34.4 all-gather.36
  1032.5 280.7 reduce-scatter.15
  1317.2 89.3 reduce-scatter.29
  1410.0 147.5 reduce-scatter.41
  1561.6 148.3 reduce-scatter.37
  1713.4 89.0 reduce-scatter.21
  1806.5 88.2 reduce-scatter.17
  1898.3 88.2 reduce-scatter.25
  1990.8 401.5 reduce-scatter.33
  2395.6 20.8 reduce-scatter.31
  2419.0 21.6 reduce-scatter.43
  2443.9 21.6 reduce-scatter.39
  2535.6 28.2 reduce-scatter.35
  (3 shorter events, 59.9 us)
where the time goes:
time: 2590 us; the launch traced here: 2570 us
  waiting for transfers between devices  1760 us (68%)
  local copies, waits for them, and re-layouts  412 us (16%)
  matrix products  203 us (8%)
  blocking collectives  114 us (4%)
  other arithmetic  62.3 us (2%)
    reduce_scatter x1, waiting for transfers between devices, body(): lax.psum_scatter(grad_ada_local, 'seq', scatter_dimension=1, tiled=True)  404 us
    dynamic_update_slice x16, local copies, waits for them, and re-layouts, body(): lax.scan(joint_step, zero_query, stack_blocks(gathered))  350 us
    reduce_scatter x1, waiting for transfers between devices, body(): lax.psum_scatter(key_value_terms, 'seq', scatter_dimension=0, tiled=True)  263 us
    reduce_scatter x1, waiting for transfers between devices, body(): lax.psum_scatter(grad_up_local, 'seq', scatter_dimension=1, tiled=True)  150 us
    reduce_scatter x1, waiting for transfers between devices, body(): lax.psum_scatter(grad_down_local, 'seq', scatter_dimension=1, tiled=True)  149 us
    reduce_scatter x1, waiting for transfers between devices, body(): lax.psum_scatter(grad_key_local, 'seq', scatter_dimension=1, tiled=True)  90.4 us
    reduce_scatter x1, waiting for transfers between devices, body(): lax.psum_scatter(grad_query_local, 'seq', scatter_dimension=1, tiled=True)  90.3 us
    reduce_scatter x1, waiting for transfers between devices, body(): lax.psum_scatter(grad_value_local, 'seq', scatter_dimension=1, tiled=True)  90 us
  transfers between devices with their start and end apart: 27, of which 24 were waited for; matrix products, arithmetic and copies ran while one was open for 7% of the time, Pallas kernels for 0%

commit v1 on v0

--- a/solution.py
+++ b/solution.py
@@ -4,6 +4,8 @@
 import jax
 import jax.numpy as jnp
 from jax import lax
+from jax.experimental import pallas as pl
+from jax.experimental.pallas import tpu as pltpu
 from jax.sharding import PartitionSpec as P
 
 D = 1024
@@ -337,9 +339,417 @@
     )
 
 
+TWO = 2 * HEAD
+ROWS = 256
+BIG = 1e30
+SEQ = 8
+REPLICAS = 4
+
+
+def swap(part, axis, distance):
+    size = SEQ if axis == "seq" else REPLICAS
+    return lax.ppermute(part, axis, [(i, i ^ distance) for i in range(size)])
+
+
+def along_line(part, step):
+    pairs = [
+        (z * 2 + y, (z + step) * 2 + y) for z in range(4) for y in range(2) if 0 <= z + step < 4
+    ]
+    return lax.ppermute(part, "seq", pairs)
+
+
+def gather_rows(part):
+    place = lax.axis_index("seq")
+    z, y = place // 2, place % 2
+    right, left = [part], [part]
+    for _ in range(3):
+        right.append(along_line(right[-1], 1))
+        left.append(along_line(left[-1], -1))
+    line = [part] + [jnp.where(z >= k, right[k], left[4 - k]) for k in range(1, 4)]
+    other = [swap(chunk, "seq", 1) for chunk in line]
+    line, other = jnp.stack(line[::-1] * 2), jnp.stack(other[::-1] * 2)
+    line = lax.dynamic_slice_in_dim(line, 3 - z, 4, 0)
+    other = lax.dynamic_slice_in_dim(other, 3 - z, 4, 0)
+    pair = jnp.stack([jnp.where(y == 0, line, other), jnp.where(y == 0, other, line)], axis=1)
+    return pair.reshape((SEQ * part.shape[0],) + part.shape[1:])
+
+
+def exchange(blocks):
+    return lax.all_to_all(blocks, "seq", 0, 0, tiled=True)
+
+
+def sum_over_replicas(grad):
+    place = lax.axis_index("batch")
+    x, core = place // 2, place % 2
+    rows, cols = grad.shape[0] // REPLICAS, grad.shape[1]
+    parts = grad.reshape(2, 2, rows, cols)
+    keep = lax.dynamic_index_in_dim(parts, core, 1, False)
+    send = lax.dynamic_index_in_dim(parts, 1 - core, 1, False)
+    both = (
+        keep.astype(jnp.float32) + swap(send.astype(jnp.bfloat16), "batch", 1).astype(jnp.float32)
+    ).astype(jnp.bfloat16)
+    keep = lax.dynamic_index_in_dim(both, x, 0, False)
+    send = lax.dynamic_index_in_dim(both, 1 - x, 0, False)
+    return keep.astype(jnp.float32) + swap(send, "batch", 2).astype(jnp.float32)
+
+
+def sum_over_frames(part):
+    place = lax.axis_index("seq")
+    rows, cols = part.shape[0], part.shape[1] // SEQ
+    blocks = part.astype(jnp.bfloat16).reshape(rows, SEQ, cols)
+    total = lax.dynamic_index_in_dim(part.reshape(rows, SEQ, cols), place, 1, False)
+    for k in range(1, SEQ):
+        sent = swap(lax.dynamic_index_in_dim(blocks, place ^ k, 1, False), "seq", k)
+        total = total + sent.astype(jnp.float32)
+    return total
+
+
+def turn(vectors, cosine, sine):
+    lane = lax.broadcasted_iota(jnp.int32, vectors.shape, 1)
+    first = (lane % HEAD) < HEAD // 2
+    partner = jnp.where(
+        first,
+        pltpu.roll(vectors, TWO - HEAD // 2, 1),
+        pltpu.roll(vectors, HEAD // 2, 1),
+    )
+    return vectors * cosine + partner * jnp.where(first, -sine, sine)
+
+
+def of_head(vectors, head):
+    lane = lax.broadcasted_iota(jnp.int32, vectors.shape, 1)
+    return jnp.where(lane // HEAD == head, vectors, jnp.zeros_like(vectors))
+
+
+def dot_t(left, right):
+    return lax.dot_general(
+        left, right, (((1,), (1,)), ((), ())), preferred_element_type=jnp.float32
+    )
+
+
+def project_kernel(x_ref, member_ref, bar_ref, cos_ref, sin_ref, emb_ref, w_ref,
+                   input_ref, q_ref, k_ref, kt_ref, v_ref, vt_ref):
+    rows = x_ref[...].astype(jnp.float32)
+    centered = rows - jnp.mean(rows, axis=1, keepdims=True)
+    inverse = lax.rsqrt(jnp.mean(centered * centered, axis=1, keepdims=True) + 1e-06)
+    modulation = matmul(member_ref[...], emb_ref[...])
+    low = (centered * inverse * (1.0 + modulation[:, D:]) + modulation[:, :D]).astype(jnp.bfloat16)
+    input_ref[...] = low
+    product = matmul(low, w_ref[...])
+    cosine, sine = cos_ref[...], sin_ref[...]
+    keys = turn(product[:, TWO:2 * TWO], cosine, sine)
+    values = product[:, 2 * TWO:]
+    q_ref[...] = turn(product[:, :TWO], cosine, sine).astype(jnp.bfloat16)
+    k_ref[:, :TWO] = keys.astype(jnp.bfloat16)
+    k_ref[:, TWO:] = bar_ref[...]
+    kt_ref[...] = keys.T.astype(jnp.bfloat16)
+    v_ref[...] = values.astype(jnp.bfloat16)
+    vt_ref[...] = values.T.astype(jnp.bfloat16)
+
+
+def rows_spec(width):
+    return pl.BlockSpec((ROWS, width), lambda i: (i, 0))
+
+
+def cols_spec(height):
+    return pl.BlockSpec((height, ROWS), lambda i: (0, i))
+
+
+def whole_spec(height, width):
+    return pl.BlockSpec((height, width), lambda i: (0, 0))
+
+
+def params(mib):
+    return pltpu.CompilerParams(
+        dimension_semantics=("arbitrary",), vmem_limit_bytes=mib * 1024 * 1024
+    )
+
+
+def project(x, member, bar, cosine, sine, emb, weights):
+    frames = x.shape[0]
+    low = jnp.bfloat16
+    return pl.pallas_call(
+        project_kernel,
+        grid=(frames // ROWS,),
+        in_specs=[rows_spec(D), rows_spec(TWO), rows_spec(TWO), rows_spec(TWO), rows_spec(TWO),
+                  whole_spec(TWO, 2 * D), whole_spec(D, 3 * TWO)],
+        out_specs=[rows_spec(D), rows_spec(TWO), rows_spec(2 * TWO), cols_spec(TWO),
+                   rows_spec(TWO), cols_spec(TWO)],
+        out_shape=[
+            jax.ShapeDtypeStruct((frames, D), low),
+            jax.ShapeDtypeStruct((frames, TWO), low),
+            jax.ShapeDtypeStruct((frames, 2 * TWO), low),
+            jax.ShapeDtypeStruct((TWO, frames), low),
+            jax.ShapeDtypeStruct((frames, TWO), low),
+            jax.ShapeDtypeStruct((TWO, frames), low),
+        ],
+        compiler_params=params(40),
+        name="project",
+    )(x, member, bar, cosine, sine, emb, weights)
+
+
+def attend_kernel(q_ref, member_ref, k_ref, vt_ref, att_ref, low_ref, log_ref, score_ref):
+    frames = k_ref.shape[0]
+    step = min(frames, 512)
+    queries = q_ref[...] * 0.125
+    member = member_ref[...]
+    halves = []
+    for head in range(2):
+        wide = jnp.concatenate([of_head(queries, head), member], axis=1)
+        largest = jnp.full((1, ROWS), -BIG, jnp.float32)
+        for start in range(0, frames, step):
+            scores = dot_t(k_ref[start:start + step, :], wide)
+            score_ref[start:start + step, :] = scores
+            largest = jnp.maximum(largest, jnp.max(scores, axis=0, keepdims=True))
+        total = jnp.zeros((1, ROWS), jnp.float32)
+        out = jnp.zeros((TWO, ROWS), jnp.float32)
+        for start in range(0, frames, step):
+            weights = jnp.exp(score_ref[start:start + step, :] - largest)
+            total = total + jnp.sum(weights, axis=0, keepdims=True)
+            out = out + matmul(vt_ref[:, start:start + step], weights.astype(jnp.bfloat16))
+        halves.append(out[head * HEAD:(head + 1) * HEAD, :] / total)
+        log_ref[head:head + 1, :] = largest + jnp.log(total)
+    attended = jnp.concatenate(halves, axis=0).T
+    att_ref[...] = attended
+    low_ref[...] = attended.astype(jnp.bfloat16)
+
+
+def attend(q, member, k, vt):
+    frames = q.shape[0]
+    return pl.pallas_call(
+        attend_kernel,
+        grid=(frames // ROWS,),
+        in_specs=[rows_spec(TWO), rows_spec(TWO), whole_spec(frames, 2 * TWO),
+                  whole_spec(TWO, frames)],
+        out_specs=[rows_spec(TWO), rows_spec(TWO), cols_spec(8)],
+        out_shape=[
+            jax.ShapeDtypeStruct((frames, TWO), jnp.float32),
+            jax.ShapeDtypeStruct((frames, TWO), jnp.bfloat16),
+            jax.ShapeDtypeStruct((8, frames), jnp.float32),
+        ],
+        scratch_shapes=[pltpu.VMEM((frames, ROWS), jnp.float32)],
+        compiler_params=params(40),
+        name="attend",
+    )(q, member, k, vt)
+
+
+def attend_back_kernel(q_ref, member_ref, grad_ref, att_ref, log_ref, cos_ref, sin_ref, cos_all_ref,
+                       sin_all_ref, k_ref, kt_ref, v_ref, gq_ref, gk_ref, gv_ref, dk_ref, dv_ref):
+    block = pl.program_id(0)
+    frames = k_ref.shape[0]
+    step = min(frames, 512)
+
+    @pl.when(block == 0)
+    def _():
+        dk_ref[...] = jnp.zeros_like(dk_ref)
+        dv_ref[...] = jnp.zeros_like(dv_ref)
+
+    queries = q_ref[...] * 0.125
+    member = member_ref[...]
+    grad = grad_ref[...]
+    mixed = (grad.astype(jnp.float32) * att_ref[...]).T
+    halves = []
+    wides, grads, deltas = [], [], []
+    for head in range(2):
+        wides.append(jnp.concatenate([of_head(queries, head), member], axis=1))
+        grads.append(of_head(grad, head))
+        deltas.append(jnp.sum(mixed[head * HEAD:(head + 1) * HEAD, :], axis=0, keepdims=True))
+    totals = [jnp.zeros((TWO, ROWS), jnp.float32) for _ in range(2)]
+    for start in range(0, frames, step):
+        part = slice(start, start + step)
+        dk = dk_ref[part, :]
+        dv = dv_ref[part, :]
+        for head in range(2):
+            scores = dot_t(k_ref[part, :], wides[head])
+            weights = jnp.exp(scores - log_ref[head:head + 1, :])
+            grad_weights = dot_t(v_ref[part, :], grads[head])
+            grad_scores = (weights * (grad_weights - deltas[head])).astype(jnp.bfloat16)
+            dv = dv + matmul(weights.astype(jnp.bfloat16), grads[head])
+            dk = dk + matmul(grad_scores, wides[head][:, :TWO])
+            totals[head] = totals[head] + matmul(kt_ref[:, part], grad_scores)
+        dk_ref[part, :] = dk
+        dv_ref[part, :] = dv
+    dq = jnp.concatenate([totals[0][:HEAD, :], totals[1][HEAD:, :]], axis=0).T * 0.125
+    gq_ref[...] = turn(dq, cos_ref[...], -sin_ref[...]).astype(jnp.bfloat16)
+
+    @pl.when(block == pl.num_programs(0) - 1)
+    def _():
+        gk_ref[...] = turn(dk_ref[...], cos_all_ref[...], -sin_all_ref[...]).astype(jnp.bfloat16)
+        gv_ref[...] = dv_ref[...].astype(jnp.bfloat16)
+
+
+def attend_back(q, member, grad, att, log_total, cosine, sine, k, kt, v):
+    frames = q.shape[0]
+    pair = jax.ShapeDtypeStruct((frames, TWO), jnp.bfloat16)
+    return pl.pallas_call(
+        attend_back_kernel,
+        grid=(frames // ROWS,),
+        in_specs=[rows_spec(TWO), rows_spec(TWO), rows_spec(TWO), rows_spec(TWO), cols_spec(8),
+                  rows_spec(TWO), rows_spec(TWO), whole_spec(frames, TWO), whole_spec(frames, TWO),
+                  whole_spec(frames, 2 * TWO), whole_spec(TWO, frames), whole_spec(frames, TWO)],
+        out_specs=[rows_spec(TWO), whole_spec(frames, TWO), whole_spec(frames, TWO)],
+        out_shape=[pair, pair, pair],
+        scratch_shapes=[pltpu.VMEM((frames, TWO), jnp.float32),
+                        pltpu.VMEM((frames, TWO), jnp.float32)],
+        compiler_params=params(48),
+        name="attend_back",
+    )(q, member, grad, att, log_total, cosine, sine, cosine, sine, k, kt, v)
+
+
+def three_terms(values):
+    high = lax.reduce_precision(values, 8, 7)
+    middle = lax.reduce_precision(values - high, 8, 7)
+    return [high, middle, values - high - middle]
+
+
+def body_fast(
+    tokens, w_query, w_key, w_value, w_out, w_ada, w_up, w_down,
+    segments, validity, timesteps, cotangent,
+):
+    highest = lax.Precision.HIGHEST
+    low = jnp.bfloat16
+    replica = lax.axis_index("batch")
+    inputs = tokens[0].astype(jnp.float32)
+    grad_output = cotangent[0].astype(jnp.float32)
+    frame_count = inputs.shape[0]
+    frames = frame_count * SEQ
+    segment = segments[0]
+
+    x_all = gather_rows(tokens[0])
+    codes = lax.all_gather(segment * 2 + (validity[0] == 1), "seq", axis=0, tiled=True)
+    clip = codes // 2
+    clips = jnp.arange(CLIPS, dtype=jnp.int32)
+    member_all = clip[:, None] == clips[None, :]
+    counted = member_all.astype(jnp.int32)
+    before = jnp.cumsum(counted, axis=0) - counted
+    position = jnp.sum(before * counted, axis=1).astype(jnp.float32)
+    half = HEAD // 2
+    frequency = jnp.exp(-math.log(10000.0) * jnp.arange(half, dtype=jnp.float32) / half)
+    angle = position[:, None] * frequency[None, :]
+    cosine = jnp.tile(jnp.cos(angle), (1, 4))
+    sine = jnp.tile(jnp.sin(angle), (1, 4))
+    spread = member_all.astype(low)
+    member = jnp.concatenate([spread] * 3 + [jnp.zeros((frames, TWO - 3 * CLIPS), low)], axis=1)
+    allowed = jnp.where((codes % 2 == 1)[:, None], member_all, False)
+    bar = jnp.concatenate(
+        [jnp.where(allowed, 0.0, -BIG).astype(low), jnp.zeros((frames, TWO - CLIPS), low)], axis=1
+    )
+
+    times = lax.all_gather(timesteps[0], "batch", axis=0, tiled=True)
+    silu_all = jax.nn.silu(time_embedding(times)).astype(low)
+    wide = w_ada.shape[0]
+    silu_part = lax.dynamic_slice_in_dim(silu_all, replica * wide, wide, 1)
+    emb_part = matmul(silu_part, w_ada.astype(low)).reshape(REPLICAS, CLIPS, -1)
+    emb_cols = jnp.sum(lax.all_to_all(emb_part, "batch", 0, 0, tiled=True), axis=0)
+    emb = exchange(jnp.broadcast_to(emb_cols[None], (SEQ,) + emb_cols.shape))
+    emb = emb.transpose(1, 0, 2).reshape(CLIPS, -1)
+    emb_terms = jnp.concatenate(
+        [t.astype(low) for t in three_terms(emb[:, :2 * D])]
+        + [jnp.zeros((TWO - 3 * CLIPS, 2 * D), low)], axis=0
+    )
+
+    heads_w = jnp.concatenate([w_query, w_key, w_value], axis=1).astype(low)
+    heads_w = lax.all_gather(heads_w, "batch", axis=0, tiled=True)
+
+    def whole(weight):
+        gathered = lax.all_gather(weight.astype(low), ("batch", "seq"), axis=0)
+        rows, cols = weight.shape
+        return gathered.reshape(REPLICAS, SEQ, rows, cols).transpose(0, 2, 1, 3).reshape(
+            REPLICAS * rows, SEQ * cols
+        )
+
+    full_o, full_u, full_d = whole(w_out), whole(w_up), whole(w_down)
+    full_q, full_k, full_v = whole(w_query), whole(w_key), whole(w_value)
+
+    attn_input, q, k, kt, v, vt = project(x_all, member, bar, cosine, sine, emb_terms, heads_w)
+    attended, attended_low, log_total = attend(q, member, k, vt)
+    mine = exchange(attended_low.reshape(SEQ, frame_count, TWO))
+    mine = mine.transpose(1, 0, 2).reshape(frame_count, D)
+
+    one_hot = (segment[:, None] == clips[None, :]).astype(jnp.float32)
+    modulation = jnp.dot(one_hot, emb, precision=highest)
+    shift_attn, scale_attn, gate_attn, shift_ffn, scale_ffn, gate_ffn = jnp.split(
+        modulation, 6, axis=1
+    )
+    attn_branch = matmul(mine, full_o)
+    middle = inputs + gate_attn * attn_branch
+    normed_mid, inverse_mid = normalize(middle)
+    ffn_input = (normed_mid * (1.0 + scale_ffn) + shift_ffn).astype(low)
+    hidden = matmul(ffn_input, full_u)
+    activated, gelu_pull = jax.vjp(partial(jax.nn.gelu, approximate=True), hidden)
+    activated_low = activated.astype(low)
+    ffn_branch = matmul(activated_low, full_d)
+    result = middle + gate_ffn * ffn_branch
+    grad_gate_ffn = grad_output * ffn_branch
+    g_ffn = (grad_output * gate_ffn).astype(low)
+    grad_down_local = matmul(activated_low.T, g_ffn).astype(low)
+    grad_activated = matmul(g_ffn, full_d.T)
+    g_hidden = gelu_pull(grad_activated)[0].astype(low)
+    grad_up_local = matmul(ffn_input.T, g_hidden).astype(low)
+    grad_ffn_input = matmul(g_hidden, full_u.T)
+    grad_middle = grad_output + norm_backward(
+        grad_ffn_input * (1.0 + scale_ffn), normed_mid, inverse_mid
+    )
+    grad_scale_ffn = grad_ffn_input * normed_mid
+    grad_gate_attn = grad_middle * attn_branch
+    g_attn = (grad_middle * gate_attn).astype(low)
+    grad_out_local = matmul(mine.T, g_attn).astype(low)
+    grad_attn = matmul(g_attn, full_o.T).astype(low)
+
+    final_d = sum_over_frames(sum_over_replicas(grad_down_local))
+    final_u = sum_over_frames(sum_over_replicas(grad_up_local))
+    final_o = sum_over_frames(sum_over_replicas(grad_out_local))
+
+    grad_heads = exchange(grad_attn.reshape(frame_count, SEQ, TWO).transpose(1, 0, 2))
+    grad_heads = grad_heads.reshape(frames, TWO)
+    g_query, g_key, g_value = attend_back(
+        q, member, grad_heads, attended, log_total, cosine, sine, k, kt, v
+    )
+    g_heads = jnp.concatenate([g_query, g_key, g_value], axis=1)
+    grad_heads_w = matmul(attn_input.T, g_heads).astype(low)
+    own = exchange(g_heads.reshape(SEQ, frame_count, 3 * TWO)).reshape(SEQ, frame_count, 3, TWO)
+    own = own.transpose(2, 1, 0, 3).reshape(3, frame_count, D)
+    final_heads = sum_over_replicas(grad_heads_w)
+
+    grad_attn_input = (
+        matmul(own[0], full_q.T) + matmul(own[1], full_k.T) + matmul(own[2], full_v.T)
+    )
+    normed, inverse = normalize(inputs)
+    grad_inputs = grad_middle + norm_backward(grad_attn_input * (1.0 + scale_attn), normed, inverse)
+    grad_modulation = jnp.concatenate(
+        [
+            grad_attn_input,
+            grad_attn_input * normed,
+            grad_gate_attn,
+            grad_ffn_input,
+            grad_scale_ffn,
+            grad_gate_ffn,
+        ],
+        axis=1,
+    )
+    grad_emb = jnp.dot(one_hot.T, grad_modulation, precision=highest)
+    grad_emb = grad_emb.reshape(CLIPS, SEQ, -1).transpose(1, 0, 2)
+    grad_emb = jnp.sum(exchange(grad_emb), axis=0)
+    grad_emb = lax.all_gather(grad_emb, "batch", axis=0, tiled=True)
+    final_a = jnp.dot(silu_part.astype(jnp.float32).T, grad_emb, precision=highest)
+    head_cols = w_query.shape[1]
+    return (
+        result.astype(low)[None],
+        grad_inputs.astype(low)[None],
+        final_heads[:, :head_cols],
+        final_heads[:, head_cols:2 * head_cols],
+        final_heads[:, 2 * head_cols:],
+        final_o,
+        final_a,
+        final_u,
+        final_d,
+    )
+
+
 def solution(mesh):
+    fits = mesh.shape["seq"] == SEQ and mesh.shape["batch"] == REPLICAS
+    chosen = body_fast if fits else body
     return jax.shard_map(
-        body,
+        chosen,
         mesh=mesh,
         in_specs=(
             P("batch", "seq", None),

time: 2590 us -> 618 us (0.24)
  waiting for transfers between devices: 1760 us -> 236 us
  local copies, waits for them, and re-layouts: 412 us -> 89.9 us
  matrix products: 203 us -> 33.6 us
  starting transfers between devices: 1.5 us -> 89.7 us
  blocking collectives: 114 us -> 41.1 us
  Pallas kernels: 0 us -> 54.5 us
    reduce_scatter x15 -> x0, waiting for transfers between devices: 1450 us -> none  [the longest x1 404 us: body(): lax.psum_scatter(grad_ada_local, 'seq', scatter_dimension=1, tiled=True)]
    dynamic_update_slice x16 -> x0, local copies, waits for them, and re-layouts: 350 us -> none  [body(): lax.scan(joint_step, zero_query, stack_blocks(gathered))]
    all_gather x12 -> x6, waiting for transfers between devices: 311 us -> 146 us  [whole(): gathered = lax.all_gather(weight.astype(low), ('batch', 'seq'), axis=0)]
    dot_general x31 -> x3, matrix products: 138 us -> 8.35 us  [the longest x1 4.76 us: body_fast(): modulation = jnp.dot(one_hot, emb, precision=highest)]
    ppermute x0 -> x39, waiting for transfers between devices: none -> 86 us  [the longest x33 61.3 us: swap(): return lax.ppermute(part, axis, [(i, i ^ distance) for i in range(size)])]
    all_gather x5 -> x3, blocking collectives: 105 us -> 35.7 us  [the longest x1 13.8 us: body_fast(): heads_w = lax.all_gather(heads_w, 'batch', axis=0, tiled=True)]
    pallas_call x0 -> x3, Pallas kernels: none -> 54.5 us  [the longest x1 26.6 us: attend_back(): pl.pallas_call(attend_back_kernel, grid=(frames // ROWS,), in_specs=[rows...]
    ppermute x0 -> x39, starting transfers between devices: none -> 51.8 us  [the longest x33 34.1 us: swap(): return lax.ppermute(part, axis, [(i, i ^ distance) for i in range(size)])]
  transfers between devices with their start and end apart: 27 -> 51, of which waited for: 24 -> 18; matrix products, arithmetic and copies ran while one was open for 7% -> 23% of each run, Pallas kernels for 0% -> 9%
where the time goes in v1:
time: 618 us; the launch traced here: 608 us
  waiting for transfers between devices  236 us (38%)
  local copies, waits for them, and re-layouts  89.9 us (15%)
  starting transfers between devices  89.7 us (15%)
  Pallas kernels  54.5 us (9%)
  other arithmetic  46.7 us (8%)
  blocking collectives  41.1 us (7%)
  matrix products  33.6 us (5%)
  between operations  16.7 us (3%)
    all_gather x6, waiting for transfers between devices, whole(): gathered = lax.all_gather(weight.astype(low), ('batch', 'seq'), axis=0)  146 us
    ppermute x33, waiting for transfers between devices, swap(): return lax.ppermute(part, axis, [(i, i ^ distance) for i in range(size)])  61.3 us
    ppermute x33, starting transfers between devices, swap(): return lax.ppermute(part, axis, [(i, i ^ distance) for i in range(size)])  34.1 us
    all_to_all x5, starting transfers between devices, exchange(): return lax.all_to_all(blocks, 'seq', 0, 0, tiled=True)  33.4 us
    unnamed x167, local copies, waits for them, and re-layouts  31 us
    reshape x6, local copies, waits for them, and re-layouts, whole(): gathered.reshape(REPLICAS, SEQ, rows, cols).transpose(0, 2, 1, 3)  27.3 us
    pallas_call x1, Pallas kernels, attend_back(): pl.pallas_call(attend_back_kernel, grid=(frames // ROWS,), in_specs=[rows...  26.6 us
    dot_general x14, matrix products, matmul(): return jnp.dot(left, right, preferred_element_type=jnp.float32)  25.3 us
  transfers between devices with their start and end apart: 51, of which 18 were waited for; matrix products, arithmetic and copies ran while one was open for 23% of the time, Pallas kernels for 9%

profile of v1, /device:TPU:13, one launch (start us, length us, event | category | flops | bytes accessed | tf_op | source)
XLA Modules:
  0.0 607.9 jit_solution(13825444323163878708)
XLA Ops:
  24.5 5.5 all-reduce.1
  36.5 12.4 %all-gather.7 = s32[8,1,256]{2,1,0:T(1,128)S(1)} all-gather(s32[1,1,256]{2,1,0:T(1,128)S(1)} %bitcast.401), channel_id=1, replica_groups=mesh['seq'=8,'batch'=4] {'seq'}, dimensions={0}, use_global_device_ids=true | all-gather | bytes 9216 | tf_op jit(solution)/shard_map/all_gather | solution.py:618
  61.3 8.7 %all-to-all-start.1 = ((f32[8,16,768]{2,1,0:T(8,128)}), f32[8,16,768]{2,1,0:T(8,128)}, u32[]{:S(2)}, u32[]{:S(2)}) async-start(f32[8,16,768]{2,1,0:T(8,128)} %broadcast_in_dim.30), calls=%async_computation.1 | async-start | bytes 786432 | tf_op jit(solution)/shard_map/all_to_all | solution.py:378
  73.1 13.8 %all_gather.50.w_ref = bf16[1024,384]{1,0:T(8,128)(2,1)S(1)} all-gather(bf16[256,384]{1,0:T(8,128)(2,1)S(1)} %pad_maximum_fusion.1), channel_id=1, replica_groups=mesh['seq'=8,'batch'=4] {'batch'}, dimensions={0}, use_global_device_ids=true | all-gather | bytes 983040 | tf_op jit(solution)/shard_map/all_gather | solution.py:651
  100.9 11.8 %collective-permute-done.4 = bf16[256,1024]{1,0:T(8,128)(2,1)} collective-permute-done((bf16[256,1024]{1,0:T(8,128)(2,1)}, bf16[256,1024]{1,0:T(8,128)(2,1)}, u32[]{:S(2)}, u32[]{:S(2)}) %collective-permute-start.4) | collective-permute-done | bytes 524320 | tf_op jit(solution)/shard_map/ppermute | solution.py:358
  120.2 12.9 %collective-permute-done.5 = bf16[256,1024]{1,0:T(8,128)(2,1)S(1)} collective-permute-done((bf16[256,1024]{1,0:T(8,128)(2,1)}, bf16[256,1024]{1,0:T(8,128)(2,1)S(1)}, u32[]{:S(2)}, u32[]{:S(2)}) %collective-permute-start.5) | collective-permute-done | bytes 524320 | tf_op jit(solution)/shard_map/ppermute | solution.py:358
  135.0 6.0 collective-permute-done.7
  141.1 11.8 %collective-permute-done.8 = bf16[256,1024]{1,0:T(8,128)(2,1)S(1)} collective-permute-done((bf16[256,1024]{1,0:T(8,128)(2,1)S(1)}, bf16[256,1024]{1,0:T(8,128)(2,1)S(1)}, u32[]{:S(2)}, u32[]{:S(2)}) %collective-permute-start.8) | collective-permute-done | bytes 524320 | tf_op jit(solution)/shard_map/ppermute | solution.py:351
  158.3 9.5 %project.1 = (bf16[2048,1024]{1,0:T(8,128)(2,1)S(1)}, bf16[2048,128]{1,0:T(8,128)(2,1)S(1)}, bf16[2048,256]{1,0:T(8,128)(2,1)S(1)}, bf16[128,2048]{1,0:T(8,128)(...) custom-call(bf16[2048,1024]{1,0:T(8,128)(2,1)} %bitcast.331, ...), custom_call_target="tpu_custom_call" | custom-call | tf_op jit(solution)/shard_map/project/pallas_call | solution.py:470
  169.9 18.3 %attend.1 = (f32[2048,128]{1,0:T(8,128)S(1)}, bf16[2048,128]{1,0:T(8,128)(2,1)S(1)}, f32[8,2048]{1,0:T(8,128)S(1)}) custom-call(bf16[2048,128]{1,0:T(8,128)(2,1)S(1)} %get-tuple-element.21.q_ref, bf16[2048,128]{1,0:T(8,128)(2,1)S(1)} %maximum_maximum_fusion.member_ref, bf16[2048,256]{1,0:T(8,128)(2,1)S(1)} %get-tuple-element.22.k_ref, ...), custom_call_target="tpu_custom_call" | custom-call | tf_op jit(solution)/shard_map/attend/pallas_call | solution.py:518
  190.3 6.0 all-to-all-start.2
  214.2 36.1 %all-gather.21.cloned.1.call-done = bf16[8192,128]{1,0:T(8,128)(2,1)} async-done(((bf16[256,128]{1,0:T(8,128)(2,1)}), bf16[8192,128]{1,0:T(8,128)(2,1)}) %all-gather.21.cloned.1.call-update) | async-done | bytes 2097168 | tf_op jit(solution)/shard_map/all_gather | solution.py:654
  261.9 53.7 %all-gather.17.cloned.1.call-done = bf16[8192,256]{1,0:T(8,128)(2,1)} async-done(((bf16[256,256]{1,0:T(8,128)(2,1)}), bf16[8192,256]{1,0:T(8,128)(2,1)}) %all-gather.17.cloned.1.call-update) | async-done | bytes 4194320 | tf_op jit(solution)/shard_map/all_gather | solution.py:654
  323.6 56.2 %all-gather.19.cloned.1.call-done = bf16[16384,128]{1,0:T(8,128)(2,1)} async-done(((bf16[512,128]{1,0:T(8,128)(2,1)}), bf16[16384,128]{1,0:T(8,128)(2,1)}) %all-gather.19.cloned.1.call-update) | async-done | bytes 4194320 | tf_op jit(solution)/shard_map/all_gather | solution.py:654
  379.7 5.5 copy.99
  415.1 26.6 %attend_back.1 = (bf16[2048,128]{1,0:T(8,128)(2,1)S(1)}, bf16[2048,128]{1,0:T(8,128)(2,1)S(1)}, bf16[2048,128]{1,0:T(8,128)(2,1)S(1)}) custom-call(bf16[2048,128]{1,0:T(8,128)(2,1)S(1)} %copy-done.4, bf16[2048,128]{1,0:T(8,128)(2,1)S(1)} %maximum_maximum_fusion.member_ref, bf16[2048,128]{1,0:T(8,128)(2,1)S(1)} %bitcast.325, ...), custom_call_target="tpu_custom_call" | custom-call | tf_op jit(solution)/shard_map/attend_back/pallas_call | solution.py:583
  453.1 7.5 %all-to-all-start.4 = ((bf16[8,256,384]{1,2,0:T(8,128)(2,1)}), bf16[8,256,384]{1,2,0:T(8,128)(2,1)}, u32[]{:S(2)}, u32[]{:S(2)}) async-start(bf16[8,256,384]{1,2,0:T(8,128)(2,1)} %copy.105), calls=%async_computation.4 | async-start | bytes 3145728 | tf_op jit(solution)/shard_map/all_to_all | solution.py:378
  471.5 7.3 %collective-permute-done.13 = bf16[256,1024]{1,0:T(8,128)(2,1)S(1)} collective-permute-done((bf16[256,1024]{1,0:T(8,128)(2,1)S(1)}, bf16[256,1024]{1,0:T(8,128)(2,1)S(1)}, u32[]{:S(2)}, u32[]{:S(2)}) %collective-permute-start.13) | collective-permute-done | bytes 524320 | tf_op jit(solution)/shard_map/ppermute | solution.py:351
  489.6 12.9 %collective-permute-done.20 = bf16[256,128]{1,0:T(8,128)(2,1)S(1)} collective-permute-done((bf16[256,128]{1,0:T(8,128)(2,1)S(1)}, bf16[256,128]{1,0:T(8,128)(2,1)S(1)}, u32[]{:S(2)}, u32[]{:S(2)}) %collective-permute-start.20) | collective-permute-done | bytes 65568 | tf_op jit(solution)/shard_map/ppermute | solution.py:351
  518.8 5.0 collective-permute-start.27
  551.2 6.8 %all-to-all-start.5 = ((f32[8,16,768]{2,1,0:T(8,128)}), f32[8,16,768]{2,1,0:T(8,128)S(1)}, u32[]{:S(2)}, u32[]{:S(2)}) async-start(f32[8,16,768]{2,1,0:T(8,128)} %bitcast.302), calls=%async_computation.5 | async-start | bytes 786432 | tf_op jit(solution)/shard_map/all_to_all | solution.py:378
  571.9 6.4 %collective-permute-done.38 = bf16[512,128]{1,0:T(8,128)(2,1)S(1)} collective-permute-done((bf16[512,128]{1,0:T(8,128)(2,1)}, bf16[512,128]{1,0:T(8,128)(2,1)S(1)}, u32[]{:S(2)}, u32[]{:S(2)}) %collective-permute-start.38) | collective-permute-done | bytes 131104 | tf_op jit(solution)/shard_map/ppermute | solution.py:351
  578.3 6.1 %collective-permute-done.37 = bf16[512,128]{1,0:T(8,128)(2,1)S(1)} collective-permute-done((bf16[512,128]{1,0:T(8,128)(2,1)}, bf16[512,128]{1,0:T(8,128)(2,1)S(1)}, u32[]{:S(2)}, u32[]{:S(2)}) %collective-permute-start.37) | collective-permute-done | bytes 131104 | tf_op jit(solution)/shard_map/ppermute | solution.py:351
  589.7 9.5 %all_gather.63 = f32[64,768]{1,0:T(8,128)S(1)} all-gather(f32[16,768]{1,0:T(8,128)S(1)} %reduce_sum.109), channel_id=1, replica_groups=mesh['seq'=8,'batch'=4] {'batch'}, dimensions={0}, use_global_device_ids=true | all-gather | bytes 245760 | tf_op jit(solution)/shard_map/all_gather | solution.py:732
  (379 shorter events, 234.9 us)
Async XLA Ops:
  7.2 194.1 %all-gather.15.cloned.1.call-start = ((), (), s32[]{:S(2)}) async-start(), calls=%async_computation.6 | async-start | bytes 2162688 | tf_op jit(solution)/shard_map/all_gather | solution.py:654
  8.9 196.7 %all-gather.25.cloned.1.call-start = ((), (), s32[]{:S(2)}) async-start(), calls=%async_computation.11 | async-start | bytes 2162688 | tf_op jit(solution)/shard_map/all_gather | solution.py:654
  10.5 199.4 %all-gather.23.cloned.1.call-start = ((), (), s32[]{:S(2)}) async-start(), calls=%async_computation.10 | async-start | bytes 2162688 | tf_op jit(solution)/shard_map/all_gather | solution.py:654
  12.1 238.1 %all-gather.21.cloned.1.call-start = ((), (), s32[]{:S(2)}) async-start(), calls=%async_computation.9 | async-start | bytes 2162688 | tf_op jit(solution)/shard_map/all_gather | solution.py:654
  13.7 301.8 %all-gather.17.cloned.1.call-start = ((), (), s32[]{:S(2)}) async-start(), calls=%async_computation.7 | async-start | bytes 4325376 | tf_op jit(solution)/shard_map/all_gather | solution.py:654
  15.4 54.6 %collective-permute-start = (bf16[256,1024]{1,0:T(8,128)(2,1)}, bf16[256,1024]{1,0:T(8,128)(2,1)}, u32[]{:S(2)}, u32[]{:S(2)}) collective-permute-start(bf16[256,1024]{1,0:T(8,128)(2,1)} %bitcast.333), channel_id=1, source_target_pairs={{0,8},{4,12},{8,16},{12,20},{16,24},{20,28},{1,9},{5,13},{9,17},{1... | collective-permute-start | bytes 1572872 | tf_op jit(solution)/shard_map/ppermute | solution.py:358
  18.6 75.7 %collective-permute-start.3 = (bf16[256,1024]{1,0:T(8,128)(2,1)}, bf16[256,1024]{1,0:T(8,128)(2,1)}, u32[]{:S(2)}, u32[]{:S(2)}) collective-permute-start(bf16[256,1024]{1,0:T(8,128)(2,1)} %bitcast.334), channel_id=1, source_target_pairs={{8,0},{12,4},{16,8},{20,12},{24,16},{28,20},{9,1},{13,5},{17,9},{2... | collective-permute-start | bytes 1572872 | tf_op jit(solution)/shard_map/ppermute | solution.py:358
  21.5 131.3 %collective-permute-start.9 = (bf16[256,1024]{1,0:T(8,128)(2,1)}, bf16[256,1024]{1,0:T(8,128)(2,1)}, u32[]{:S(2)}, u32[]{:S(2)}) collective-permute-start(bf16[256,1024]{1,0:T(8,128)(2,1)} %bitcast.335), channel_id=1, source_target_pairs={{0,4},{4,0},{8,12},{12,8},{16,20},{20,16},{24,28},{28,24},{1,5},{5... | collective-permute-start | bytes 1572872 | tf_op jit(solution)/shard_map/ppermute | solution.py:351
  31.4 29.0 %all-to-all-start = ((f32[4,16,768]{2,1,0:T(8,128)}), f32[4,16,768]{2,1,0:T(8,128)S(1)}, u32[]{:S(2)}, u32[]{:S(2)}) async-start(f32[4,16,768]{2,1,0:T(8,128)} %bitcast.4), calls=%async_computation | async-start | bytes 393216 | tf_op jit(solution)/shard_map/all_to_all | solution.py:642
  35.7 344.0 %all-gather.19.cloned.1.call-start = ((), (), s32[]{:S(2)}) async-start(), calls=%async_computation.8 | async-start | bytes 4325376 | tf_op jit(solution)/shard_map/all_gather | solution.py:654
  61.3 36.0 %all-to-all-start.1 = ((f32[8,16,768]{2,1,0:T(8,128)}), f32[8,16,768]{2,1,0:T(8,128)}, u32[]{:S(2)}, u32[]{:S(2)}) async-start(f32[8,16,768]{2,1,0:T(8,128)} %broadcast_in_dim.30), calls=%async_computation.1 | async-start | bytes 786432 | tf_op jit(solution)/shard_map/all_to_all | solution.py:378
  70.0 28.4 %collective-permute-start.1 = (bf16[256,1024]{1,0:T(8,128)(2,1)}, bf16[256,1024]{1,0:T(8,128)(2,1)}, u32[]{:S(2)}, u32[]{:S(2)}) collective-permute-start(bf16[256,1024]{1,0:T(8,128)(2,1)} %collective-permute-done), channel_id=1, source_target_pairs={{0,8},{4,12},{8,16},{12,20},{16,24},{20,28},{1,9},{5,13},{9,17},{1... | collective-permute-start | bytes 1572872 | tf_op jit(solution)/shard_map/ppermute | solution.py:358
  190.3 64.3 %all-to-all-start.2 = ((bf16[8,256,128]{1,2,0:T(8,128)(2,1)}), bf16[8,256,128]{1,2,0:T(8,128)(2,1)S(1)}, u32[]{:S(2)}, u32[]{:S(2)}) async-start(bf16[8,256,128]{1,2,0:T(8,128)(2,1)} %copy.96), calls=%async_computation.2 | async-start | bytes 1048576 | tf_op jit(solution)/shard_map/all_to_all | solution.py:378
  405.7 56.7 %collective-permute-start.12 = (bf16[2,256,1024]{2,1,0:T(8,128)(2,1)}, bf16[2,256,1024]{2,1,0:T(8,128)(2,1)}, u32[]{:S(2)}, u32[]{:S(2)}) collective-permute-start(bf16[2,256,1024]{2,1,0:T(8,128)(2,1)} %dynamic-slice_bitcast_fusion.4), channel_id=1, source_target_pairs={{0,1},{1,0},{2,3},{3,2},{4,5},{5,4},{6,7},{7,6},{8,9},{9,8},{10,11... | collective-permute-start | bytes 3145736 | tf_op jit(solution)/shard_map/ppermute | solution.py:351
  410.4 58.0 %collective-permute-start.21 = (bf16[2,256,2048]{2,1,0:T(8,128)(2,1)}, bf16[2,256,2048]{2,1,0:T(8,128)(2,1)}, u32[]{:S(2)}, u32[]{:S(2)}) collective-permute-start(bf16[2,256,2048]{2,1,0:T(8,128)(2,1)} %dynamic-slice_bitcast_fusion.1), channel_id=1, source_target_pairs={{0,1},{1,0},{2,3},{3,2},{4,5},{5,4},{6,7},{7,6},{8,9},{9,8},{10,11... | collective-permute-start | bytes 6291464 | tf_op jit(solution)/shard_map/ppermute | solution.py:351
  451.4 35.5 %collective-permute-start.30 = (bf16[2,512,1024]{2,1,0:T(8,128)(2,1)}, bf16[2,512,1024]{2,1,0:T(8,128)(2,1)}, u32[]{:S(2)}, u32[]{:S(2)}) collective-permute-start(bf16[2,512,1024]{2,1,0:T(8,128)(2,1)} %dynamic-slice_bitcast_fusion), channel_id=1, source_target_pairs={{0,1},{1,0},{2,3},{3,2},{4,5},{5,4},{6,7},{7,6},{8,9},{9,8},{10,11... | collective-permute-start | bytes 6291464 | tf_op jit(solution)/shard_map/ppermute | solution.py:351
  453.1 82.5 %all-to-all-start.4 = ((bf16[8,256,384]{1,2,0:T(8,128)(2,1)}), bf16[8,256,384]{1,2,0:T(8,128)(2,1)}, u32[]{:S(2)}, u32[]{:S(2)}) async-start(bf16[8,256,384]{1,2,0:T(8,128)(2,1)} %copy.105), calls=%async_computation.4 | async-start | bytes 3145728 | tf_op jit(solution)/shard_map/all_to_all | solution.py:378
  470.8 38.3 %collective-permute-start.22 = (bf16[256,2048]{1,0:T(8,128)(2,1)S(1)}, bf16[256,2048]{1,0:T(8,128)(2,1)S(1)}, u32[]{:S(2)}, u32[]{:S(2)}) collective-permute-start(bf16[256,2048]{1,0:T(8,128)(2,1)S(1)} %dynamic-slice_bitcast_fusion.3), channel_id=1, source_target_pairs={{0,2},{1,3},{2,0},{3,1},{4,6},{5,7},{6,4},{7,5},{8,10},{9,11},{10,... | collective-permute-start | bytes 3145736 | tf_op jit(solution)/shard_map/ppermute | solution.py:351
  514.7 43.3 %collective-permute-start.29 = (bf16[256,256]{1,0:T(8,128)(2,1)}, bf16[256,256]{1,0:T(8,128)(2,1)}, u32[]{:S(2)}, u32[]{:S(2)}) collective-permute-start(bf16[256,256]{1,0:T(8,128)(2,1)} %bitcast.310), channel_id=1, source_target_pairs={{0,28},{4,24},{8,20},{12,16},{16,12},{20,8},{24,4},{28,0},{1,29},{... | collective-permute-start | bytes 393224 | tf_op jit(solution)/shard_map/ppermute | solution.py:351
  518.1 40.3 %collective-permute-start.28 = (bf16[256,256]{1,0:T(8,128)(2,1)}, bf16[256,256]{1,0:T(8,128)(2,1)}, u32[]{:S(2)}, u32[]{:S(2)}) collective-permute-start(bf16[256,256]{1,0:T(8,128)(2,1)} %bitcast.311), channel_id=1, source_target_pairs={{0,24},{4,28},{8,16},{12,20},{16,8},{20,12},{24,0},{28,4},{1,25},{... | collective-permute-start | bytes 393224 | tf_op jit(solution)/shard_map/ppermute | solution.py:351
  518.8 39.7 %collective-permute-start.27 = (bf16[256,256]{1,0:T(8,128)(2,1)}, bf16[256,256]{1,0:T(8,128)(2,1)}, u32[]{:S(2)}, u32[]{:S(2)}) collective-permute-start(bf16[256,256]{1,0:T(8,128)(2,1)} %bitcast.312), channel_id=1, source_target_pairs={{0,20},{4,16},{8,28},{12,24},{16,4},{20,0},{24,12},{28,8},{1,21},{... | collective-permute-start | bytes 393224 | tf_op jit(solution)/shard_map/ppermute | solution.py:351
  524.5 37.2 %collective-permute-start.26 = (bf16[256,256]{1,0:T(8,128)(2,1)}, bf16[256,256]{1,0:T(8,128)(2,1)}, u32[]{:S(2)}, u32[]{:S(2)}) collective-permute-start(bf16[256,256]{1,0:T(8,128)(2,1)} %bitcast.313), channel_id=1, source_target_pairs={{0,16},{4,20},{8,24},{12,28},{16,0},{20,4},{24,8},{28,12},{1,17},{... | collective-permute-start | bytes 393224 | tf_op jit(solution)/shard_map/ppermute | solution.py:351
  528.2 38.0 %collective-permute-start.25 = (bf16[256,256]{1,0:T(8,128)(2,1)}, bf16[256,256]{1,0:T(8,128)(2,1)}, u32[]{:S(2)}, u32[]{:S(2)}) collective-permute-start(bf16[256,256]{1,0:T(8,128)(2,1)} %bitcast.314), channel_id=1, source_target_pairs={{0,12},{4,8},{8,4},{12,0},{16,28},{20,24},{24,20},{28,16},{1,13},{... | collective-permute-start | bytes 393224 | tf_op jit(solution)/shard_map/ppermute | solution.py:351
  551.2 38.5 %all-to-all-start.5 = ((f32[8,16,768]{2,1,0:T(8,128)}), f32[8,16,768]{2,1,0:T(8,128)S(1)}, u32[]{:S(2)}, u32[]{:S(2)}) async-start(f32[8,16,768]{2,1,0:T(8,128)} %bitcast.302), calls=%async_computation.5 | async-start | bytes 786432 | tf_op jit(solution)/shard_map/all_to_all | solution.py:378
  (88 other events, 1274.9 us)
Sparse Core Ops, SparseCore 0:
  11.0 58.3 all-gather.14
  72.9 57.3 all-gather.24
  133.9 56.6 all-gather.22
  193.4 56.7 all-gather.20
  253.8 61.7 all-gather.16
  319.1 60.6 all-gather.18

commit v2 on v1

--- a/solution.py
+++ b/solution.py
@@ -344,34 +344,12 @@
 BIG = 1e30
 SEQ = 8
 REPLICAS = 4
+VMEM_MIB = 60
 
 
 def swap(part, axis, distance):
     size = SEQ if axis == "seq" else REPLICAS
     return lax.ppermute(part, axis, [(i, i ^ distance) for i in range(size)])
-
-
-def along_line(part, step):
-    pairs = [
-        (z * 2 + y, (z + step) * 2 + y) for z in range(4) for y in range(2) if 0 <= z + step < 4
-    ]
-    return lax.ppermute(part, "seq", pairs)
-
-
-def gather_rows(part):
-    place = lax.axis_index("seq")
-    z, y = place // 2, place % 2
-    right, left = [part], [part]
-    for _ in range(3):
-        right.append(along_line(right[-1], 1))
-        left.append(along_line(left[-1], -1))
-    line = [part] + [jnp.where(z >= k, right[k], left[4 - k]) for k in range(1, 4)]
-    other = [swap(chunk, "seq", 1) for chunk in line]
-    line, other = jnp.stack(line[::-1] * 2), jnp.stack(other[::-1] * 2)
-    line = lax.dynamic_slice_in_dim(line, 3 - z, 4, 0)
-    other = lax.dynamic_slice_in_dim(other, 3 - z, 4, 0)
-    pair = jnp.stack([jnp.where(y == 0, line, other), jnp.where(y == 0, other, line)], axis=1)
-    return pair.reshape((SEQ * part.shape[0],) + part.shape[1:])
 
 
 def exchange(blocks):
@@ -393,14 +371,10 @@
     return keep.astype(jnp.float32) + swap(send, "batch", 2).astype(jnp.float32)
 
 
-def sum_over_frames(part):
-    place = lax.axis_index("seq")
-    rows, cols = part.shape[0], part.shape[1] // SEQ
-    blocks = part.astype(jnp.bfloat16).reshape(rows, SEQ, cols)
-    total = lax.dynamic_index_in_dim(part.reshape(rows, SEQ, cols), place, 1, False)
-    for k in range(1, SEQ):
-        sent = swap(lax.dynamic_index_in_dim(blocks, place ^ k, 1, False), "seq", k)
-        total = total + sent.astype(jnp.float32)
+def along_z(part):
+    total = part[0].astype(jnp.float32)
+    for k in range(1, 4):
+        total = total + swap(part[k], "seq", 2 * k).astype(jnp.float32)
     return total
 
 
@@ -426,15 +400,23 @@
     )
 
 
-def project_kernel(x_ref, member_ref, bar_ref, cos_ref, sin_ref, emb_ref, w_ref,
-                   input_ref, q_ref, k_ref, kt_ref, v_ref, vt_ref):
-    rows = x_ref[...].astype(jnp.float32)
-    centered = rows - jnp.mean(rows, axis=1, keepdims=True)
-    inverse = lax.rsqrt(jnp.mean(centered * centered, axis=1, keepdims=True) + 1e-06)
+def project_kernel(place_ref, a_ref, b_ref, c_ref, d_ref, member_ref, bar_ref, cos_ref, sin_ref,
+                   emb_ref, w_ref, *refs):
+    x_ref, input_ref, q_ref, k_ref, kt_ref, v_ref, vt_ref, chunk_ref = refs[-8:]
+    for step, ref in enumerate((a_ref, b_ref, c_ref, d_ref)):
+
+        @pl.when(pl.program_id(0) == step)
+        def _():
+            chunk_ref[...] = ref[...]
+
+    chunk = chunk_ref[...]
+    x_ref[...] = chunk
+    normed, _ = standardize(chunk.astype(jnp.float32))
     modulation = matmul(member_ref[...], emb_ref[...])
-    low = (centered * inverse * (1.0 + modulation[:, D:]) + modulation[:, :D]).astype(jnp.bfloat16)
+    low = (normed * (1.0 + modulation[:, D:]) + modulation[:, :D]).astype(jnp.bfloat16)
     input_ref[...] = low
-    product = matmul(low, w_ref[...])
+    weight = jnp.concatenate([w_ref[b ^ place_ref[1]] for b in range(REPLICAS)], axis=0)
+    product = matmul(low, weight)
     cosine, sine = cos_ref[...], sin_ref[...]
     keys = turn(product[:, TWO:2 * TWO], cosine, sine)
     values = product[:, 2 * TWO:]
@@ -464,17 +446,42 @@
     )
 
 
-def project(x, member, bar, cosine, sine, emb, weights):
-    frames = x.shape[0]
+def cost(micros):
+    return pl.CostEstimate(
+        flops=int(micros * 1e9), bytes_accessed=int(micros * 3e6), transcendentals=0
+    )
+
+
+def project(place, odd, chunks, member, bar, cosine, sine, emb, weights, earlier):
+    frames = member.shape[0]
     low = jnp.bfloat16
+
+    def rows(width):
+        return pl.BlockSpec((ROWS, width), lambda i, p: ((2 * i + odd) ^ p[0], 0))
+
+    def cols(height):
+        return pl.BlockSpec((height, ROWS), lambda i, p: (0, (2 * i + odd) ^ p[0]))
+
+    def whole(height, width):
+        return pl.BlockSpec((height, width), lambda i, p: (0, 0))
+
+    inputs = [place, *chunks, member, bar, cosine, sine, emb, weights, *earlier]
+    first = len(inputs) - len(earlier)
     return pl.pallas_call(
         project_kernel,
-        grid=(frames // ROWS,),
-        in_specs=[rows_spec(D), rows_spec(TWO), rows_spec(TWO), rows_spec(TWO), rows_spec(TWO),
-                  whole_spec(TWO, 2 * D), whole_spec(D, 3 * TWO)],
-        out_specs=[rows_spec(D), rows_spec(TWO), rows_spec(2 * TWO), cols_spec(TWO),
-                   rows_spec(TWO), cols_spec(TWO)],
+        grid_spec=pltpu.PrefetchScalarGridSpec(
+            num_scalar_prefetch=1,
+            grid=(4,),
+            in_specs=[whole(ROWS, D)] * 4 + [rows(TWO)] * 4
+            + [whole(TWO, 2 * D),
+               pl.BlockSpec((REPLICAS, ROWS, 3 * TWO), lambda i, p: (0, 0, 0))]
+            + [pl.BlockSpec(memory_space=pl.ANY)] * len(earlier),
+            out_specs=[rows(D), rows(D), rows(TWO), rows(2 * TWO), cols(TWO), rows(TWO),
+                       cols(TWO)],
+            scratch_shapes=[pltpu.VMEM((ROWS, D), low)],
+        ),
         out_shape=[
+            jax.ShapeDtypeStruct((frames, D), low),
             jax.ShapeDtypeStruct((frames, D), low),
             jax.ShapeDtypeStruct((frames, TWO), low),
             jax.ShapeDtypeStruct((frames, 2 * TWO), low),
@@ -482,9 +489,11 @@
             jax.ShapeDtypeStruct((frames, TWO), low),
             jax.ShapeDtypeStruct((TWO, frames), low),
         ],
-        compiler_params=params(40),
+        input_output_aliases={first + i: i for i in range(len(earlier))},
+        compiler_params=params(VMEM_MIB),
+        cost_estimate=cost(5),
         name="project",
-    )(x, member, bar, cosine, sine, emb, weights)
+    )(*inputs)
 
 
 def attend_kernel(q_ref, member_ref, k_ref, vt_ref, att_ref, low_ref, log_ref, score_ref):
@@ -527,13 +536,14 @@
             jax.ShapeDtypeStruct((8, frames), jnp.float32),
         ],
         scratch_shapes=[pltpu.VMEM((frames, ROWS), jnp.float32)],
-        compiler_params=params(40),
+        compiler_params=params(VMEM_MIB),
+        cost_estimate=cost(18),
         name="attend",
     )(q, member, k, vt)
 
 
 def attend_back_kernel(q_ref, member_ref, grad_ref, att_ref, log_ref, cos_ref, sin_ref, cos_all_ref,
-                       sin_all_ref, k_ref, kt_ref, v_ref, gq_ref, gk_ref, gv_ref, dk_ref, dv_ref):
+                       sin_all_ref, k_ref, kt_ref, v_ref, g_ref, dk_ref, dv_ref):
     block = pl.program_id(0)
     frames = k_ref.shape[0]
     step = min(frames, 512)
@@ -569,28 +579,30 @@
         dk_ref[part, :] = dk
         dv_ref[part, :] = dv
     dq = jnp.concatenate([totals[0][:HEAD, :], totals[1][HEAD:, :]], axis=0).T * 0.125
-    gq_ref[...] = turn(dq, cos_ref[...], -sin_ref[...]).astype(jnp.bfloat16)
+    here = pl.ds(pl.multiple_of(block * ROWS, ROWS), ROWS)
+    g_ref[here, :TWO] = turn(dq, cos_ref[...], -sin_ref[...]).astype(jnp.bfloat16)
 
     @pl.when(block == pl.num_programs(0) - 1)
     def _():
-        gk_ref[...] = turn(dk_ref[...], cos_all_ref[...], -sin_all_ref[...]).astype(jnp.bfloat16)
-        gv_ref[...] = dv_ref[...].astype(jnp.bfloat16)
+        turned = turn(dk_ref[...], cos_all_ref[...], -sin_all_ref[...])
+        g_ref[:, TWO:2 * TWO] = turned.astype(jnp.bfloat16)
+        g_ref[:, 2 * TWO:] = dv_ref[...].astype(jnp.bfloat16)
 
 
 def attend_back(q, member, grad, att, log_total, cosine, sine, k, kt, v):
     frames = q.shape[0]
-    pair = jax.ShapeDtypeStruct((frames, TWO), jnp.bfloat16)
     return pl.pallas_call(
         attend_back_kernel,
         grid=(frames // ROWS,),
         in_specs=[rows_spec(TWO), rows_spec(TWO), rows_spec(TWO), rows_spec(TWO), cols_spec(8),
                   rows_spec(TWO), rows_spec(TWO), whole_spec(frames, TWO), whole_spec(frames, TWO),
                   whole_spec(frames, 2 * TWO), whole_spec(TWO, frames), whole_spec(frames, TWO)],
-        out_specs=[rows_spec(TWO), whole_spec(frames, TWO), whole_spec(frames, TWO)],
-        out_shape=[pair, pair, pair],
+        out_specs=whole_spec(frames, 3 * TWO),
+        out_shape=jax.ShapeDtypeStruct((frames, 3 * TWO), jnp.bfloat16),
         scratch_shapes=[pltpu.VMEM((frames, TWO), jnp.float32),
                         pltpu.VMEM((frames, TWO), jnp.float32)],
-        compiler_params=params(48),
+        compiler_params=params(VMEM_MIB),
+        cost_estimate=cost(27),
         name="attend_back",
     )(q, member, grad, att, log_total, cosine, sine, cosine, sine, k, kt, v)
 
@@ -599,6 +611,314 @@
     high = lax.reduce_precision(values, 8, 7)
     middle = lax.reduce_precision(values - high, 8, 7)
     return [high, middle, values - high - middle]
+
+
+def standardize(rows):
+    centered = rows - jnp.mean(rows, axis=1, keepdims=True)
+    inverse = lax.rsqrt(jnp.mean(centered * centered, axis=1, keepdims=True) + 1e-06)
+    return centered * inverse, inverse
+
+
+def sum_of_clips(clip_ref, values):
+    ids = lax.broadcasted_iota(jnp.int32, (CLIPS, clip_ref.shape[1]), 0)
+    chosen = jnp.where(clip_ref[...] == ids, 1.0, 0.0).astype(jnp.bfloat16)
+    high = values.astype(jnp.bfloat16)
+    rest = values - high.astype(jnp.float32)
+    middle = rest.astype(jnp.bfloat16)
+    last = (rest - middle.astype(jnp.float32)).astype(jnp.bfloat16)
+    return matmul(chosen, high) + matmul(chosen, middle) + matmul(chosen, last)
+
+
+def beside(ref, tiles, rows):
+    return jnp.concatenate([ref[tile, rows, :] for tile in tiles], axis=1)
+
+
+def middle_kernel(mine_ref, x_ref, cot_ref, member_ref, clip_ref, emb_ref, tiles_ref,
+                  result_ref, grad_middle_ref, grad_att_ref, grad_emb_ref, left_ref, right_ref,
+                  out_ref, up_ref, down_ref, sems, branch_ref, low_ref, act_ref, slope_ref,
+                  wide_ref):
+    low = jnp.bfloat16
+    act_t_ref, ffn_t_ref = left_ref.at[:2 * D], left_ref.at[2 * D:3 * D]
+    mine_t_ref = left_ref.at[3 * D:]
+    g_ffn_ref, g_attn_ref = right_ref.at[:, :D], right_ref.at[:, 3 * D:]
+    g_hidden_ref = right_ref.at[:, D:3 * D]
+    pieces = ((out_ref, 0, 256), (up_ref, 256, 512), (down_ref, 768, 512))
+    copies = [
+        pltpu.make_async_copy(tiles_ref.at[:, pl.ds(start, size), :], ref, sems.at[i])
+        for i, (ref, start, size) in enumerate(pieces)
+    ]
+    for copy in copies:
+        copy.start()
+    member = member_ref[...]
+
+    def modulation(index):
+        return matmul(member, emb_ref[:, index * D:(index + 1) * D])
+
+    def cols(n, width=256):
+        return pl.ds(pl.multiple_of(n * width, width), width)
+
+    every = slice(None)
+    mine = jnp.concatenate([mine_ref[j] for j in range(SEQ)], axis=1)
+    low_ref[...] = mine
+    mine_t_ref[...] = mine.T
+    gate_attn = modulation(2)
+    copies[0].wait()
+
+    @pl.loop(0, 4)
+    def _(n):
+        total = jnp.zeros((ROWS, 256), jnp.float32)
+        for b in range(REPLICAS):
+            weight = beside(out_ref, [8 * b + 2 * n, 8 * b + 2 * n + 1], every)
+            total = total + matmul(low_ref[:, 256 * b:256 * b + 256], weight)
+        branch_ref[:, cols(n)] = total
+
+    branch = branch_ref[...]
+    middle = x_ref[...].astype(jnp.float32) + gate_attn * branch
+    normed, inverse = standardize(middle)
+    scale_ffn = modulation(4)
+    ffn_input = normed * (1.0 + scale_ffn) + modulation(3)
+    low_ref[...] = ffn_input.astype(low)
+    ffn_t_ref[...] = ffn_input.T.astype(low)
+    gate_ffn = modulation(5)
+    cot = cot_ref[...].astype(jnp.float32)
+    g_ffn_ref[...] = (cot * gate_ffn).astype(low)
+    copies[1].wait()
+
+    @pl.loop(0, 8)
+    def _(n):
+        hidden = jnp.zeros((ROWS, 256), jnp.float32)
+        for b in range(REPLICAS):
+            tile = 8 * b + n
+            weight = jnp.concatenate([up_ref[tile, :256, :], up_ref[tile, 256:, :]], axis=1)
+            hidden = hidden + matmul(low_ref[:, 256 * b:256 * b + 256], weight)
+        root = math.sqrt(2.0 / math.pi)
+        squared = hidden * hidden
+        bent = jnp.tanh(root * (hidden + 0.044715 * (squared * hidden)))
+        half = 0.5 * (1.0 + bent)
+        activated = hidden * half
+        slope = half + 0.5 * hidden * (1.0 - bent * bent) * (
+            root * (1.0 + (3.0 * 0.044715) * squared)
+        )
+        act_ref[:, cols(n)] = activated.astype(low)
+        act_t_ref[cols(n), :] = activated.T.astype(low)
+        slope_ref[:, cols(n)] = slope
+
+    copies[2].wait()
+
+    @pl.loop(0, 4)
+    def _(n):
+        total = jnp.zeros((ROWS, 256), jnp.float32)
+        for b in range(REPLICAS):
+            weight = beside(down_ref, [8 * b + 2 * n, 8 * b + 2 * n + 1], every)
+            total = total + matmul(act_ref[:, 512 * b:512 * b + 512], weight)
+        wide_ref[:, cols(n)] = total
+
+    ffn_branch = wide_ref[...]
+    result_ref[...] = (middle + gate_ffn * ffn_branch).astype(low)
+    grad_emb_ref[:, 3 * D:] = sum_of_clips(clip_ref, cot * ffn_branch)
+
+    @pl.loop(0, REPLICAS)
+    def _(b):
+        weight = beside(down_ref, [8 * b + s for s in range(SEQ)], every)
+        grad = dot_t(g_ffn_ref[...], weight)
+        here = cols(b, 512)
+        g_hidden_ref[:, here] = (grad * slope_ref[:, here]).astype(low)
+
+    @pl.loop(0, REPLICAS)
+    def _(b):
+        weight = jnp.concatenate(
+            [up_ref[8 * b + s, 256 * k:256 * k + 256, :] for s in range(SEQ) for k in range(2)],
+            axis=1,
+        )
+        wide_ref[:, cols(b)] = dot_t(g_hidden_ref[...], weight)
+
+    grad_ffn_input = wide_ref[...]
+    grad_emb_ref[:, D:2 * D] = sum_of_clips(clip_ref, grad_ffn_input)
+    grad_emb_ref[:, 2 * D:3 * D] = sum_of_clips(clip_ref, grad_ffn_input * normed)
+    spread = grad_ffn_input * (1.0 + scale_ffn)
+    grad_middle = cot + inverse * (
+        spread
+        - jnp.mean(spread, axis=1, keepdims=True)
+        - normed * jnp.mean(spread * normed, axis=1, keepdims=True)
+    )
+    grad_middle_ref[...] = grad_middle
+    grad_emb_ref[:, :D] = sum_of_clips(clip_ref, grad_middle * branch)
+    g_attn_ref[...] = (grad_middle * gate_attn).astype(low)
+
+    @pl.loop(0, REPLICAS)
+    def _(b):
+        weight = beside(out_ref, [8 * b + s for s in range(SEQ)], every)
+        grad = dot_t(g_attn_ref[...], weight).astype(low)
+        grad_att_ref[2 * b] = grad[:, :TWO]
+        grad_att_ref[2 * b + 1] = grad[:, TWO:]
+
+
+def middle_part(mine, x, cot, member, clip_row, emb, tiles):
+    low = jnp.bfloat16
+    shapes = [
+        ((ROWS, D), low), ((ROWS, D), jnp.float32), ((SEQ, ROWS, TWO), low),
+        ((CLIPS, 4 * D), jnp.float32),
+        ((4 * D, ROWS), low), ((ROWS, 4 * D), low),
+    ]
+    vmem = pl.BlockSpec(memory_space=pltpu.VMEM)
+    return pl.pallas_call(
+        middle_kernel,
+        in_specs=[vmem] * 6 + [pl.BlockSpec(memory_space=pl.ANY)],
+        out_specs=[vmem] * len(shapes),
+        out_shape=[jax.ShapeDtypeStruct(shape, dtype) for shape, dtype in shapes],
+        scratch_shapes=[
+            pltpu.VMEM((32, 256, 128), low),
+            pltpu.VMEM((32, 512, 128), low),
+            pltpu.VMEM((32, 512, 128), low),
+            pltpu.SemaphoreType.DMA((3,)),
+            pltpu.VMEM((ROWS, D), jnp.float32),
+            pltpu.VMEM((ROWS, D), low),
+            pltpu.VMEM((ROWS, 2 * D), low),
+            pltpu.VMEM((ROWS, 2 * D), jnp.float32),
+            pltpu.VMEM((ROWS, D), jnp.float32),
+        ],
+        compiler_params=pltpu.CompilerParams(vmem_limit_bytes=VMEM_MIB * 1024 * 1024),
+        cost_estimate=cost(20),
+        name="middle",
+    )(mine, x, cot, member, clip_row, emb, tiles)
+
+
+def weight_grads_kernel(place_ref, down_l, up_l, out_l, right_ref, down_o, up_o, out_o, other_ref,
+                        away_d_ref, keep_d_ref, away_u_ref, keep_u_ref):
+    low = jnp.bfloat16
+    z, y = place_ref[2] // 2, place_ref[2] % 2
+    lefts = [
+        jnp.concatenate([mine[...], other[...]], axis=1)
+        for mine, other in ((down_l, down_o), (up_l, up_o), (out_l, out_o))
+    ]
+
+    def product(left, first, block):
+        here = pl.ds(pl.multiple_of(first + 256 * block, 256), 256)
+        right = jnp.concatenate([right_ref[:, here], other_ref[:, here]], axis=0)
+        return matmul(left, right).astype(low)
+
+    def fill(down_ref):
+        for k in range(4):
+            block = z ^ k
+            grad = product(lefts[0], 0, block)
+            down_ref[4 * y + k] = grad[:, :128]
+            down_ref[4 - 4 * y + k] = grad[:, 128:]
+            grad = product(lefts[2], 3 * D, block)
+            keep_u_ref[0, k, :256, :] = jnp.where(y == 0, grad[:, :128], grad[:, 128:])
+            away_u_ref[0, k, :256, :] = jnp.where(y == 0, grad[:, 128:], grad[:, :128])
+            for side, ref in enumerate((keep_u_ref, away_u_ref)):
+                grad = product(lefts[1], D, 2 * block + (y ^ side))
+                ref[0, k, 256:512, :] = grad[:, :128]
+                ref[0, k, 512:, :] = grad[:, 128:]
+
+    @pl.when(pl.program_id(0) == 0)
+    def _():
+        fill(away_d_ref)
+
+    @pl.when(pl.program_id(0) == 1)
+    def _():
+        fill(keep_d_ref)
+
+
+def weight_grads(place, left, right, other_left, other_right):
+    low = jnp.bfloat16
+
+    def target(i, p):
+        return 2 * jnp.where(i == 0, 1 - p[0], p[0]) + p[1]
+
+    down = pl.BlockSpec((512, ROWS), lambda i, p: (target(i, p), 0))
+    up = pl.BlockSpec((256, ROWS), lambda i, p: (8 + target(i, p), 0))
+    out = pl.BlockSpec((256, ROWS), lambda i, p: (12 + target(i, p), 0))
+    wide = pl.BlockSpec((ROWS, 4 * D), lambda i, p: (0, 0))
+    whole = pl.BlockSpec((SEQ, 512, 128), lambda i, p: (0, 0, 0))
+    part = pl.BlockSpec((1, 4, 768, 128), lambda i, p: (1 - i, 0, 0, 0))
+    return pl.pallas_call(
+        weight_grads_kernel,
+        grid_spec=pltpu.PrefetchScalarGridSpec(
+            num_scalar_prefetch=1,
+            grid=(2,),
+            in_specs=[down, up, out, wide] * 2,
+            out_specs=[whole, whole, part, part],
+        ),
+        out_shape=[jax.ShapeDtypeStruct((SEQ, 512, 128), low)] * 2
+        + [jax.ShapeDtypeStruct((2, 4, 768, 128), low)] * 2,
+        compiler_params=params(VMEM_MIB),
+        cost_estimate=cost(9),
+        name="weight_grads",
+    )(place, left, left, left, right, other_left, other_left, other_left, other_right)
+
+
+def last_kernel(place_ref, own_ref, x_ref, grad_middle_ref, member_ref, clip_ref, emb_ref, *refs):
+    *tile_refs, out_ref, grad_emb_ref, wide_ref = refs
+    grads = jnp.concatenate([own_ref[place_ref[2] ^ s] for s in range(SEQ)], axis=1)
+
+    def tile(apart, s):
+        index = apart * SEQ + (s % 2) * 4 + s // 2
+        for ref in tile_refs:
+            if index < ref.shape[0]:
+                return ref[index]
+            index -= ref.shape[0]
+
+    for apart in range(REPLICAS):
+        weight = jnp.concatenate(
+            [
+                tile(apart, s)[256 * k:256 * k + 256, :]
+                for s in range(SEQ)
+                for k in range(3)
+            ],
+            axis=1,
+        )
+        b = (2 * place_ref[0] + place_ref[1]) ^ ((apart % 2) * 2 + apart // 2)
+        wide_ref[:, pl.ds(pl.multiple_of(b * 256, 256), 256)] = dot_t(grads, weight)
+
+    normed, inverse = standardize(x_ref[...].astype(jnp.float32))
+    grad_input = wide_ref[...]
+    grad_emb_ref[:, :D] = sum_of_clips(clip_ref, grad_input)
+    grad_emb_ref[:, D:] = sum_of_clips(clip_ref, grad_input * normed)
+    spread = grad_input * (1.0 + matmul(member_ref[...], emb_ref[:, D:2 * D]))
+    grad = grad_middle_ref[...] + inverse * (
+        spread
+        - jnp.mean(spread, axis=1, keepdims=True)
+        - normed * jnp.mean(spread * normed, axis=1, keepdims=True)
+    )
+    out_ref[...] = grad.astype(jnp.bfloat16)
+
+
+def last_part(place, own, x, grad_middle, member, clip_row, emb, tiles):
+    vmem = pl.BlockSpec(memory_space=pltpu.VMEM)
+    return pl.pallas_call(
+        last_kernel,
+        in_specs=[pl.BlockSpec(memory_space=pltpu.SMEM)] + [vmem] * (6 + len(tiles)),
+        out_specs=[vmem, vmem],
+        out_shape=[
+            jax.ShapeDtypeStruct((ROWS, D), jnp.bfloat16),
+            jax.ShapeDtypeStruct((CLIPS, 2 * D), jnp.float32),
+        ],
+        scratch_shapes=[pltpu.VMEM((ROWS, D), jnp.float32)],
+        compiler_params=pltpu.CompilerParams(vmem_limit_bytes=30 * 1024 * 1024),
+        cost_estimate=cost(4),
+        name="last",
+    )(place, own, x, grad_middle, member, clip_row, emb, *tiles)
+
+
+def after(value, *others):
+    return lax.optimization_barrier((value,) + others)[0]
+
+
+def together(*values):
+    return lax.optimization_barrier(values)
+
+
+def plus(*terms):
+    total = terms[0].astype(jnp.float32)
+    for term in terms[1:]:
+        total = total + term.astype(jnp.float32)
+    return total
+
+
+def clip_lanes(clip, terms):
+    lane = jnp.arange(TWO, dtype=jnp.int32)[None, :]
+    return (clip[:, None] == lane % CLIPS) & (lane < terms * CLIPS)
 
 
 def body_fast(
@@ -607,137 +927,133 @@
 ):
     highest = lax.Precision.HIGHEST
     low = jnp.bfloat16
+    wide = jnp.float32
     replica = lax.axis_index("batch")
-    inputs = tokens[0].astype(jnp.float32)
-    grad_output = cotangent[0].astype(jnp.float32)
-    frame_count = inputs.shape[0]
+    x = tokens[0]
+    frame_count = x.shape[0]
     frames = frame_count * SEQ
     segment = segments[0]
 
-    x_all = gather_rows(tokens[0])
-    codes = lax.all_gather(segment * 2 + (validity[0] == 1), "seq", axis=0, tiled=True)
-    clip = codes // 2
-    clips = jnp.arange(CLIPS, dtype=jnp.int32)
-    member_all = clip[:, None] == clips[None, :]
-    counted = member_all.astype(jnp.int32)
-    before = jnp.cumsum(counted, axis=0) - counted
-    position = jnp.sum(before * counted, axis=1).astype(jnp.float32)
-    half = HEAD // 2
-    frequency = jnp.exp(-math.log(10000.0) * jnp.arange(half, dtype=jnp.float32) / half)
-    angle = position[:, None] * frequency[None, :]
-    cosine = jnp.tile(jnp.cos(angle), (1, 4))
-    sine = jnp.tile(jnp.sin(angle), (1, 4))
-    spread = member_all.astype(low)
-    member = jnp.concatenate([spread] * 3 + [jnp.zeros((frames, TWO - 3 * CLIPS), low)], axis=1)
-    allowed = jnp.where((codes % 2 == 1)[:, None], member_all, False)
-    bar = jnp.concatenate(
-        [jnp.where(allowed, 0.0, -BIG).astype(low), jnp.zeros((frames, TWO - CLIPS), low)], axis=1
-    )
-
+    mine_w = jnp.concatenate(
+        [w_out, w_up[:, :128], w_up[:, 128:], w_down], axis=0
+    ).astype(low)
+    tiles = lax.all_gather(mine_w, ("batch", "seq"), axis=0)
+
+    own_codes = segment * 2 + (validity[0] == 1)
+    codes = exchange(jnp.broadcast_to(own_codes[None], (SEQ, frame_count))).reshape(frames)
     times = lax.all_gather(timesteps[0], "batch", axis=0, tiled=True)
     silu_all = jax.nn.silu(time_embedding(times)).astype(low)
-    wide = w_ada.shape[0]
-    silu_part = lax.dynamic_slice_in_dim(silu_all, replica * wide, wide, 1)
+    depth = w_ada.shape[0]
+    silu_part = lax.dynamic_slice_in_dim(silu_all, replica * depth, depth, 1)
     emb_part = matmul(silu_part, w_ada.astype(low)).reshape(REPLICAS, CLIPS, -1)
-    emb_cols = jnp.sum(lax.all_to_all(emb_part, "batch", 0, 0, tiled=True), axis=0)
+    emb_cols = lax.all_to_all(emb_part, "batch", 0, 0, tiled=True)
+    start = after(x, emb_part, codes)
+    z1, z2, y0 = swap(start, "seq", 2), swap(start, "seq", 4), swap(start, "seq", 1)
+    emb_cols = jnp.sum(emb_cols, axis=0)
     emb = exchange(jnp.broadcast_to(emb_cols[None], (SEQ,) + emb_cols.shape))
+    z1 = after(z1, emb_cols)
+    y1 = swap(z1, "seq", 1)
+    z2 = after(z2, emb_cols)
+    y2, z3 = swap(z2, "seq", 1), swap(z2, "seq", 2)
+    heads_w = jnp.concatenate([w_query, w_key, w_value], axis=1).astype(low)
+    heads_w = jnp.stack([heads_w, swap(heads_w, "batch", 1)])
+    heads_w = jnp.concatenate([heads_w, swap(after(heads_w, z1), "batch", 2)])
+    codes = after(codes, z2)
+    clip = codes // 2
+    tri = jnp.arange(frame_count)[:, None] > jnp.arange(frame_count)[None, :]
+    ids = jnp.arange(CLIPS, dtype=jnp.int32)
+    one_hot = (clip.reshape(SEQ, frame_count)[:, :, None] == ids).astype(low)
+    within = jnp.einsum("ij,njc->nic", tri.astype(low), one_hot, preferred_element_type=wide)
+    counts = jnp.sum(one_hot.astype(wide), axis=1)
+    offsets = jnp.cumsum(counts, axis=0) - counts
+    position = jnp.sum(one_hot.astype(wide) * (within + offsets[:, None, :]), axis=2)
+    half = HEAD // 2
+    frequency = jnp.exp(-math.log(10000.0) * jnp.arange(half, dtype=wide) / half)
+    angle = position.reshape(frames)[:, None] * jnp.tile(frequency, 4)[None, :]
+    cosine, sine = jnp.cos(angle), jnp.sin(angle)
+    member = clip_lanes(clip, 3).astype(low)
+    allowed = clip_lanes(jnp.where(codes % 2 == 1, clip, -1), 1)
+    inside = jnp.arange(TWO, dtype=jnp.int32)[None, :] < CLIPS
+    bar = jnp.where(inside & ~allowed, -BIG, 0.0).astype(low)
+    z3 = after(z3, member, bar, cosine, sine, heads_w)
+    y3 = swap(z3, "seq", 1)
+    mine_h = jnp.concatenate([w_query, w_key, w_value], axis=0).astype(low)
+    mine_h = after(mine_h, z3)
+    tiles_z = [swap(mine_h, "seq", 2 * k) for k in range(1, 4)]
+    line, other = (x, z1, z2, z3), (y0, y1, y2, y3)
+    emb = after(emb, z3)
     emb = emb.transpose(1, 0, 2).reshape(CLIPS, -1)
-    emb_terms = jnp.concatenate(
-        [t.astype(low) for t in three_terms(emb[:, :2 * D])]
-        + [jnp.zeros((TWO - 3 * CLIPS, 2 * D), low)], axis=0
-    )
-
-    heads_w = jnp.concatenate([w_query, w_key, w_value], axis=1).astype(low)
-    heads_w = lax.all_gather(heads_w, "batch", axis=0, tiled=True)
-
-    def whole(weight):
-        gathered = lax.all_gather(weight.astype(low), ("batch", "seq"), axis=0)
-        rows, cols = weight.shape
-        return gathered.reshape(REPLICAS, SEQ, rows, cols).transpose(0, 2, 1, 3).reshape(
-            REPLICAS * rows, SEQ * cols
-        )
-
-    full_o, full_u, full_d = whole(w_out), whole(w_up), whole(w_down)
-    full_q, full_k, full_v = whole(w_query), whole(w_key), whole(w_value)
-
-    attn_input, q, k, kt, v, vt = project(x_all, member, bar, cosine, sine, emb_terms, heads_w)
-    attended, attended_low, log_total = attend(q, member, k, vt)
+    emb = jnp.concatenate(
+        [t.astype(low) for t in three_terms(emb)] + [jnp.zeros((TWO - 3 * CLIPS, 6 * D), low)],
+        axis=0,
+    )
+
+    seat = lax.axis_index("seq").astype(jnp.int32)
+    tables = (member, bar, cosine, sine, emb[:, :2 * D], heads_w)
+    places = jnp.stack([seat, replica.astype(jnp.int32)])
+    earlier = project(places, 0, line, *tables, ())
+    *other, tiles_1, tiles_2, tiles_3 = together(*other, *tiles_z)
+    tiles_z = [tiles_1, tiles_2, tiles_3]
+    x_all, attn_input, q, k, kt, v, vt = project(places, 1, other, *tables, earlier)
+    tiles_z = jnp.stack([mine_h] + tiles_z)
+    tiles_y = swap(tiles_z, "seq", 1)
+    attended, attended_low, log_total = attend(after(q, tiles_z), member, k, vt)
+    attended_low, tiles_y = together(attended_low, tiles_y)
+    tiles_zy = jnp.concatenate([tiles_z, tiles_y])
+    tiles_x = swap(tiles_zy, "batch", 2)
     mine = exchange(attended_low.reshape(SEQ, frame_count, TWO))
-    mine = mine.transpose(1, 0, 2).reshape(frame_count, D)
-
-    one_hot = (segment[:, None] == clips[None, :]).astype(jnp.float32)
-    modulation = jnp.dot(one_hot, emb, precision=highest)
-    shift_attn, scale_attn, gate_attn, shift_ffn, scale_ffn, gate_ffn = jnp.split(
-        modulation, 6, axis=1
-    )
-    attn_branch = matmul(mine, full_o)
-    middle = inputs + gate_attn * attn_branch
-    normed_mid, inverse_mid = normalize(middle)
-    ffn_input = (normed_mid * (1.0 + scale_ffn) + shift_ffn).astype(low)
-    hidden = matmul(ffn_input, full_u)
-    activated, gelu_pull = jax.vjp(partial(jax.nn.gelu, approximate=True), hidden)
-    activated_low = activated.astype(low)
-    ffn_branch = matmul(activated_low, full_d)
-    result = middle + gate_ffn * ffn_branch
-    grad_gate_ffn = grad_output * ffn_branch
-    g_ffn = (grad_output * gate_ffn).astype(low)
-    grad_down_local = matmul(activated_low.T, g_ffn).astype(low)
-    grad_activated = matmul(g_ffn, full_d.T)
-    g_hidden = gelu_pull(grad_activated)[0].astype(low)
-    grad_up_local = matmul(ffn_input.T, g_hidden).astype(low)
-    grad_ffn_input = matmul(g_hidden, full_u.T)
-    grad_middle = grad_output + norm_backward(
-        grad_ffn_input * (1.0 + scale_ffn), normed_mid, inverse_mid
-    )
-    grad_scale_ffn = grad_ffn_input * normed_mid
-    grad_gate_attn = grad_middle * attn_branch
-    g_attn = (grad_middle * gate_attn).astype(low)
-    grad_out_local = matmul(mine.T, g_attn).astype(low)
-    grad_attn = matmul(g_attn, full_o.T).astype(low)
-
-    final_d = sum_over_frames(sum_over_replicas(grad_down_local))
-    final_u = sum_over_frames(sum_over_replicas(grad_up_local))
-    final_o = sum_over_frames(sum_over_replicas(grad_out_local))
-
-    grad_heads = exchange(grad_attn.reshape(frame_count, SEQ, TWO).transpose(1, 0, 2))
-    grad_heads = grad_heads.reshape(frames, TWO)
-    g_query, g_key, g_value = attend_back(
+    mine = after(mine, tiles_zy)
+
+    own_member = clip_lanes(segment, 3).astype(low)
+    result, grad_middle, grad_att, grad_emb, left, right = middle_part(
+        mine, x, cotangent[0], own_member, segment[None, :], emb, tiles
+    )
+    place = jnp.stack([replica // 2, replica % 2, seat]).astype(jnp.int32)
+    left, tiles_x = together(left, tiles_x)
+    other_left, other_right = swap(left, "batch", 1), swap(right, "batch", 1)
+    away_d, keep_d, away_u, keep_u = weight_grads(place, left, right, other_left, other_right)
+    grad_heads = exchange(grad_att).reshape(frames, TWO)
+    grad_heads, away_d, away_u = together(grad_heads, away_d, away_u)
+    from_x = swap(away_d, "batch", 2)
+    from_y = swap(away_u, "seq", 1)
+    tiles_zyx = jnp.concatenate([tiles_zy, tiles_x])
+    grad_heads = after(grad_heads, tiles_zyx)
+    tiles_c = swap(tiles_zyx, "batch", 1)
+
+    g_heads = attend_back(
         q, member, grad_heads, attended, log_total, cosine, sine, k, kt, v
     )
-    g_heads = jnp.concatenate([g_query, g_key, g_value], axis=1)
+    own = exchange(g_heads.reshape(SEQ, frame_count, 3 * TWO))
+    from_x, from_y, tiles_c = after(from_x, g_heads), after(from_y, g_heads), after(tiles_c, g_heads)
+    near_d = plus(keep_d, from_x)
+    from_y_d = swap(near_d[4:].astype(low), "seq", 1)
+    near_u = plus(keep_u, from_y)
+    from_x_u = swap(near_u[1].astype(low), "batch", 2)
+    part_d = plus(near_d[:4], from_y_d).astype(low)
+    part_u = after(plus(near_u[0], from_x_u).astype(low), own)
+    final_d = along_z(part_d)
+    final_uo = along_z(part_u)
+    final_o = final_uo[:256]
+    final_u = jnp.concatenate([final_uo[256:512], final_uo[512:]], axis=1)
+
     grad_heads_w = matmul(attn_input.T, g_heads).astype(low)
-    own = exchange(g_heads.reshape(SEQ, frame_count, 3 * TWO)).reshape(SEQ, frame_count, 3, TWO)
-    own = own.transpose(2, 1, 0, 3).reshape(3, frame_count, D)
     final_heads = sum_over_replicas(grad_heads_w)
-
-    grad_attn_input = (
-        matmul(own[0], full_q.T) + matmul(own[1], full_k.T) + matmul(own[2], full_v.T)
-    )
-    normed, inverse = normalize(inputs)
-    grad_inputs = grad_middle + norm_backward(grad_attn_input * (1.0 + scale_attn), normed, inverse)
-    grad_modulation = jnp.concatenate(
-        [
-            grad_attn_input,
-            grad_attn_input * normed,
-            grad_gate_attn,
-            grad_ffn_input,
-            grad_scale_ffn,
-            grad_gate_ffn,
-        ],
-        axis=1,
-    )
-    grad_emb = jnp.dot(one_hot.T, grad_modulation, precision=highest)
+    grad_tokens, late = last_part(
+        place, own, x, grad_middle, own_member, segment[None, :], emb,
+        (tiles_zyx, tiles_c),
+    )
+    grad_emb = jnp.concatenate([late, grad_emb], axis=1)
     grad_emb = grad_emb.reshape(CLIPS, SEQ, -1).transpose(1, 0, 2)
     grad_emb = jnp.sum(exchange(grad_emb), axis=0)
     grad_emb = lax.all_gather(grad_emb, "batch", axis=0, tiled=True)
-    final_a = jnp.dot(silu_part.astype(jnp.float32).T, grad_emb, precision=highest)
-    head_cols = w_query.shape[1]
+    final_a = jnp.dot(silu_part.astype(wide).T, grad_emb, precision=highest)
+    width = w_query.shape[1]
     return (
-        result.astype(low)[None],
-        grad_inputs.astype(low)[None],
-        final_heads[:, :head_cols],
-        final_heads[:, head_cols:2 * head_cols],
-        final_heads[:, 2 * head_cols:],
+        result[None],
+        grad_tokens[None],
+        final_heads[:, :width],
+        final_heads[:, width:2 * width],
+        final_heads[:, 2 * width:],
         final_o,
         final_a,
         final_u,

time: 618 us -> 364 us (0.59); the launches traced: 608 us -> 360 us
  waiting for transfers between devices: 236 us -> 118 us
  local copies, waits for them, and re-layouts: 89.9 us -> 19.8 us
  Pallas kernels: 54.5 us -> 102 us
  blocking collectives: 41.1 us -> 10.6 us
  starting transfers between devices: 89.7 us -> 63.4 us
  matrix products: 33.6 us -> 7.54 us
  other arithmetic: 46.7 us -> 23.9 us
    all_gather x6 -> x1, waiting for transfers between devices: 146 us -> 0.01 us  [body_fast(): tiles = lax.all_gather(mine_w, ('batch', 'seq'), axis=0)]
    pallas_call x1 -> x5, Pallas kernels: 9.55 us -> 53.7 us  [the longest x1 20.8 us: middle_part(): pl.pallas_call(middle_kernel, in_specs=[vmem] * 6 + [pl.BlockSpec(memory_...]
    ppermute x33 -> x29, waiting for transfers between devices: 61.3 us -> 105 us  [swap(): return lax.ppermute(part, axis, [(i, i ^ distance) for i in range(size)])]
    reshape x9 -> x0, local copies, waits for them, and re-layouts: 30.8 us -> none  [the longest x6 27.3 us: whole(): gathered.reshape(REPLICAS, SEQ, rows, cols).transpose(0, 2, 1, 3)]
    all_gather x2 -> x0, blocking collectives: 26.2 us -> none  [the longest x1 13.8 us: body_fast(): heads_w = lax.all_gather(heads_w, 'batch', axis=0, tiled=True)]
    ppermute x6 -> x0, waiting for transfers between devices: 24.8 us -> none  [along_line(): return lax.ppermute(part, 'seq', pairs)]
    unnamed x167 -> x65, local copies, waits for them, and re-layouts: 31 us -> 10 us
    dot_general x14 -> x2, matrix products: 25.3 us -> 5.91 us  [matmul(): return jnp.dot(left, right, preferred_element_type=jnp.float32)]
  transfers between devices with their start and end apart: 51 -> 37, of which waited for: 18 -> 15; matrix products, arithmetic and copies ran while one was open for 23% -> 11% of each run, Pallas kernels for 9% -> 28%
where the time goes in v2:
time: 364 us; the launch traced here: 360 us
  waiting for transfers between devices  118 us (32%)
  Pallas kernels  102 us (28%)
  starting transfers between devices  63.4 us (17%)
  other arithmetic  23.9 us (7%)
  local copies, waits for them, and re-layouts  19.8 us (5%)
  between operations  15.2 us (4%)
  blocking collectives  10.6 us (3%)
  matrix products  7.54 us (2%)
    ppermute x29, waiting for transfers between devices, swap(): return lax.ppermute(part, axis, [(i, i ^ distance) for i in range(size)])  105 us
    all_to_all x6, starting transfers between devices, exchange(): return lax.all_to_all(blocks, 'seq', 0, 0, tiled=True)  30.1 us
    ppermute x29, starting transfers between devices, swap(): return lax.ppermute(part, axis, [(i, i ^ distance) for i in range(size)])  29.3 us
    pallas_call x1, Pallas kernels, attend_back(): pl.pallas_call(attend_back_kernel, grid=(frames // ROWS,), in_specs=[rows...  28.5 us
    pallas_call x1, Pallas kernels, middle_part(): pl.pallas_call(middle_kernel, in_specs=[vmem] * 6 + [pl.BlockSpec(memory_...  20.8 us
    pallas_call x1, Pallas kernels, attend(): pl.pallas_call(attend_kernel, grid=(frames // ROWS,), in_specs=[rows_spec...  19.9 us
    pallas_call x2, Pallas kernels, project(): pl.pallas_call(project_kernel, grid_spec=pltpu.PrefetchScalarGridSpec(num...  17.5 us
    all_to_all x6, waiting for transfers between devices, exchange(): return lax.all_to_all(blocks, 'seq', 0, 0, tiled=True)  12.3 us
  transfers between devices with their start and end apart: 37, of which 15 were waited for; matrix products, arithmetic and copies ran while one was open for 11% of the time, Pallas kernels for 28%

profile of v2, /device:TPU:13, one launch (start us, length us, event | category | flops | bytes accessed | tf_op | source)
XLA Modules:
  0.0 360.2 jit_solution(2151421721383754152)
XLA Ops:
  11.8 5.7 %all-to-all-start = ((s32[8,1,256]{2,1,0:T(1,128)}), s32[8,1,256]{2,1,0:T(1,128)S(1)}, u32[]{:S(2)}, u32[]{:S(2)}) async-start(s32[8,1,256]{2,1,0:T(1,128)} %broadcast_in_dim.17), calls=%async_computation | async-start | bytes 16384 | tf_op jit(solution)/shard_map/all_to_all | solution.py:356
  20.2 4.4 %all-reduce = s32[64]{0:T(128)S(1)} all-reduce(s32[64]{0:T(128)S(1)} %bitcast_dynamic-update-slice_fusion), channel_id=2, replica_groups=mesh['seq'=8,'batch'=4] {'batch'}, use_global_device_ids=true, to_apply=%add | all-reduce | flops 64 | bytes 512
  35.5 5.3 %all-to-all-start.2 = ((f32[8,16,768]{2,1,0:T(8,128)}), f32[8,16,768]{2,1,0:T(8,128)S(1)}, u32[]{:S(2)}, u32[]{:S(2)}) async-start(f32[8,16,768]{2,1,0:T(8,128)} %broadcast_in_dim.21), calls=%async_computation.2 | async-start | bytes 786432 | tf_op jit(solution)/shard_map/all_to_all | solution.py:356
  40.9 19.3 %collective-permute-done.3.c_ref = bf16[256,1024]{1,0:T(8,128)(2,1)} collective-permute-done((bf16[256,1024]{1,0:T(8,128)(2,1)S(1)}, bf16[256,1024]{1,0:T(8,128)(2,1)}, u32[]{:S(2)}, u32[]{:S(2)}) %collective-permute-start.3) | collective-permute-done | bytes 524320 | tf_op jit(solution)/shard_map/ppermute | solution.py:352
  62.2 5.6 %multiply_sine_fusion = (f32[2048,128]{1,0:T(8,128)}, f32[2048,128]{1,0:T(8,128)}) fusion(f32[128]{0:T(128)S(1)} %mul.63, f32[2048]{0:T(1024)S(1)} %bitcast.132), kind=kLoop, calls=%fused_computation.7 | loop fusion | flops 262144 | bytes 2105856 | tf_op jit(solution)/shard_map/sin | solution.py:973
  71.2 6.5 %collective-permute-done.7 = bf16[2,256,384]{2,1,0:T(8,128)(2,1)S(1)} collective-permute-done((bf16[2,256,384]{2,1,0:T(8,128)(2,1)S(1)}, bf16[2,256,384]{2,1,0:T(8,128)(2,1)S(1)}, u32[]{:S(2)}, u32[]{:S(2)}) %collective-permute-start.7) | collective-permute-done | bytes 393248 | tf_op jit(solution)/shard_map/ppermute | solution.py:352
  78.6 9.0 %collective-permute-done.5.d_ref = bf16[256,1024]{1,0:T(8,128)(2,1)} collective-permute-done((bf16[256,1024]{1,0:T(8,128)(2,1)}, bf16[256,1024]{1,0:T(8,128)(2,1)}, u32[]{:S(2)}, u32[]{:S(2)}) %collective-permute-start.5) | collective-permute-done | bytes 524320 | tf_op jit(solution)/shard_map/ppermute | solution.py:352
  91.8 8.8 %project.2 = (bf16[2048,1024]{1,0:T(8,128)(2,1)}, bf16[2048,1024]{1,0:T(8,128)(2,1)}, bf16[2048,128]{1,0:T(8,128)(2,1)}, bf16[2048,256]{1,0:T(8,128)(2,1)}, bf16...) custom-call(s32[2]{0:T(128)} %pad_add_fusion.place_ref, bf16[256,1024]{1,0:T(8,128)(2,1)} %bitcast.113, ...), custom_call_target="tpu_custom_call" | custom-call | flops 5000000000 | bytes 15000000 | tf_op jit(solution)/shard_map/project/pallas_call | solution.py:470
  107.3 23.6 %collective-permute-done.11 = bf16[768,128]{1,0:T(8,128)(2,1)S(1)} collective-permute-done((bf16[768,128]{1,0:T(8,128)(2,1)S(1)}, bf16[768,128]{1,0:T(8,128)(2,1)S(1)}, u32[]{:S(2)}, u32[]{:S(2)}) %collective-permute-start.11) | collective-permute-done | bytes 196640 | tf_op jit(solution)/shard_map/ppermute | solution.py:352
  131.1 8.8 %project.3 = (bf16[2048,1024]{1,0:T(8,128)(2,1)}, bf16[2048,1024]{1,0:T(8,128)(2,1)}, bf16[2048,128]{1,0:T(8,128)(2,1)}, bf16[2048,256]{1,0:T(8,128)(2,1)}, bf16...) custom-call(s32[2]{0:T(128)} %pad_add_fusion.place_ref, ...), custom_call_target="tpu_custom_call", output_to_operand_aliasing={{0}: (11, {}), {1}: (12, {}), {2}: (13, {}), {3}: (14, {}),... | custom-call | flops 5000000000 | bytes 15000000 | tf_op jit(solution)/shard_map/project/pallas_call | solution.py:470
  139.9 19.9 %attend.1 = (f32[2048,128]{1,0:T(8,128)}, bf16[2048,128]{1,0:T(8,128)(2,1)}, f32[8,2048]{1,0:T(8,128)}) custom-call(bf16[2048,128]{1,0:T(8,128)(2,1)} %get-tuple-element.89.q_ref, bf16[2048,128]{1,0:T(8,128)(2,1)} %and_convert_fusion.member_ref, bf16[2048,256]{1,0:T(8,128)(2,1)} %get-tuple-element.90.k_ref, bf16[128,2048]{1,0:T(8,128)(2,1)} %get-tuple-element.91.vt_ref), custom_call_target="tpu_custom_call" | custom-call | flops 17999998976 | bytes 54000000 | tf_op jit(solution)/shard_map/attend/pallas_call | solution.py:527
  169.7 5.7 %all-to-all-done.3.mine_ref = bf16[8,256,128]{2,1,0:T(8,128)(2,1)S(1)} async-done(((bf16[8,256,128]{2,1,0:T(8,128)(2,1)}), bf16[8,256,128]{2,1,0:T(8,128)(2,1)S(1)}, u32[]{:S(2)}, u32[]{:S(2)}) %all-to-all-start.3) | async-done | bytes 524320 | tf_op jit(solution)/shard_map/all_to_all | solution.py:356
  176.3 20.8 %middle.1 = (bf16[256,1024]{1,0:T(8,128)(2,1)}, f32[256,1024]{1,0:T(8,128)}, bf16[8,256,128]{2,1,0:T(8,128)(2,1)}, f32[16,4096]{1,0:T(8,128)}, bf16[4096,256]{1,0:T(8,128)(2,1)}, /*index=5*/bf16[256,4096]{1,0:T(8,128)(2,1)}) custom-call(bf16[8,256,128]{2,1,0:T(8,128)(2,1)} %copy-done.17, bf16[256,1024]{1,0:T(8,128)(2,1)} %bitcast.114, ...), custom_call_target="tpu_custom_call" | custom-call | flops 20000000000 | bytes 60000000 | tf_op jit(solution)/shard_map/middle/pallas_call | solution.py:764
  197.1 5.6 %collective-permute-done.13 = bf16[8,768,128]{2,1,0:T(8,128)(2,1)S(1)} collective-permute-done((bf16[8,768,128]{2,1,0:T(8,128)(2,1)}, bf16[8,768,128]{2,1,0:T(8,128)(2,1)S(1)}, u32[]{:S(2)}, u32[]{:S(2)}) %collective-permute-start.13) | collective-permute-done | bytes 1572896 | tf_op jit(solution)/shard_map/ppermute | solution.py:352
  206.4 5.4 %all-to-all-start.4 = ((bf16[8,256,128]{2,1,0:T(8,128)(2,1)}), bf16[8,256,128]{2,1,0:T(8,128)(2,1)S(1)}, u32[]{:S(2)}, u32[]{:S(2)}) async-start(bf16[8,256,128]{2,1,0:T(8,128)(2,1)} %get-tuple-element.97), calls=%async_computation.4 | async-start | bytes 1048576 | tf_op jit(solution)/shard_map/all_to_all | solution.py:356
  214.2 8.7 %weight_grads.1 = (bf16[8,512,128]{2,1,0:T(8,128)(2,1)}, bf16[8,512,128]{2,1,0:T(8,128)(2,1)}, bf16[2,4,768,128]{3,2,1,0:T(8,128)(2,1)}, bf16[2,4,768,128]{3,2,1,0:T(8,128)(2,1)}) custom-call(s32[3]{0:T(128)} %pad_add_fusion.1.place_ref, bf16[4096,256]{1,0:T(8,128)(2,1)} %get-tuple-element.99.down_l.up_l.out_l, ...), custom_call_target="tpu_custom_call" | custom-call | flops 8999999488 | bytes 27000000 | tf_op jit(solution)/shard_map/weight_grads/pallas_call | solution.py:835
  225.6 28.5 %attend_back.1 = bf16[2048,384]{1,0:T(8,128)(2,1)} custom-call(bf16[2048,128]{1,0:T(8,128)(2,1)} %get-tuple-element.89.q_ref, bf16[2048,128]{1,0:T(8,128)(2,1)} %and_convert_fusion.member_ref, bf16[2048,128]{1,0:T(8,128)(2,1)} %bitcast.130, f32[2048,128]{1,0:T(8,128)} %get-tuple-element.106.att_ref, f32[8,2048]{1,0:T(8,128)} %get-tuple-element.107.log_ref, ...), custom_call_target="tpu_custom_call" | custom-call | flops 27000000512 | bytes 81000000 | tf_op jit(solution)/shard_map/attend_back/pallas_call | solution.py:594
  254.1 5.0 %convolution_convert_fusion = bf16[1024,384]{1,0:T(8,128)(2,1)S(1)} fusion(bf16[2048,1024]{1,0:T(8,128)(2,1)} %get-tuple-element.113, bf16[2048,384]{1,0:T(8,128)(2,1)} %attend_back.1), kind=kOutput, calls=%fused_computation.9 | convolution fusion | flops 1611005952 | bytes 6553600 | tf_op jit(solution)/shard_map/dot_general | solution.py:29
  264.1 5.4 %all-to-all-start.5 = ((bf16[8,256,384]{2,1,0:T(8,128)(2,1)}), bf16[8,256,384]{2,1,0:T(8,128)(2,1)S(1)}, u32[]{:S(2)}, u32[]{:S(2)}) async-start(bf16[8,256,384]{2,1,0:T(8,128)(2,1)} %bitcast.30), calls=%async_computation.5 | async-start | bytes 3145728 | tf_op jit(solution)/shard_map/all_to_all | solution.py:356
  277.8 21.1 %collective-permute-done.25 = bf16[4,512,128]{2,1,0:T(8,128)(2,1)S(1)} collective-permute-done((bf16[4,512,128]{2,1,0:T(8,128)(2,1)S(1)}, bf16[4,512,128]{2,1,0:T(8,128)(2,1)S(1)}, u32[]{:S(2)}, u32[]{:S(2)}) %collective-permute-start.25) | collective-permute-done | bytes 524320 | tf_op jit(solution)/shard_map/ppermute | solution.py:352
  303.7 5.6 %all-to-all-done.5.own_ref = bf16[8,256,384]{2,1,0:T(8,128)(2,1)S(1)} async-done(((bf16[8,256,384]{2,1,0:T(8,128)(2,1)}), bf16[8,256,384]{2,1,0:T(8,128)(2,1)S(1)}, u32[]{:S(2)}, u32[]{:S(2)}) %all-to-all-start.5) | async-done | bytes 1572896 | tf_op jit(solution)/shard_map/all_to_all | solution.py:356
  318.7 6.7 %last.1 = (bf16[256,1024]{1,0:T(8,128)(2,1)}, f32[16,2048]{1,0:T(8,128)S(1)}) custom-call(s32[3]{0:T(128)S(1)} %copy-done.5, bf16[8,256,384]{2,1,0:T(8,128)(2,1)S(1)} %all-to-all-done.5.own_ref, bf16[256,1024]{1,0:T(8,128)(2,1)S(1)} %bitcast.118, f32[256,1024]{1,0:T(8,128)S(1)} %copy-done.8, bf16[256,128]{1,0:T(8,128)(2,1)S(1)} %copy-done.2, ...), custom_call_target="tpu_custom_call" | custom-call | flops 4000000000 | bytes 12000000 | tf_op jit(solution)/shard_map/last/pallas_call | solution.py:889
  333.8 9.5 %collective-permute-done.21 = bf16[768,128]{1,0:T(8,128)(2,1)S(1)} collective-permute-done((bf16[768,128]{1,0:T(8,128)(2,1)S(1)}, bf16[768,128]{1,0:T(8,128)(2,1)S(1)}, u32[]{:S(2)}, u32[]{:S(2)}) %collective-permute-start.21) | collective-permute-done | bytes 196640 | tf_op jit(solution)/shard_map/ppermute | solution.py:352
  345.8 6.1 %all_gather.12 = f32[64,768]{1,0:T(8,128)S(1)} all-gather(f32[16,768]{1,0:T(8,128)S(1)} %reduce_sum.39), channel_id=1, replica_groups=mesh['seq'=8,'batch'=4] {'batch'}, dimensions={0}, use_global_device_ids=true | all-gather | bytes 245760 | tf_op jit(solution)/shard_map/all_gather | solution.py:1048
  (197 shorter events, 94.0 us)
Async XLA Ops:
  7.3 168.2 %all-gather.3.cloned.1.call-start = ((), (), s32[]{:S(2)}) async-start(), calls=%async_computation.7 | async-start | bytes 10813440 | tf_op jit(solution)/shard_map/all_gather | solution.py:940
  17.6 23.3 %collective-permute-start.6 = (bf16[256,384]{1,0:T(8,128)(2,1)S(1)}, bf16[256,384]{1,0:T(8,128)(2,1)S(1)}, u32[]{:S(2)}, u32[]{:S(2)}) collective-permute-start(bf16[256,384]{1,0:T(8,128)(2,1)S(1)} %pad_maximum_fusion.6), channel_id=1, source_target_pairs={{0,1},{1,0},{2,3},{3,2},{4,5},{5,4},{6,7},{7,6},{8,9},{9,8},{10,11... | collective-permute-start | bytes 589832 | tf_op jit(solution)/shard_map/ppermute | solution.py:352
  30.1 30.4 %collective-permute-start.1 = (bf16[256,1024]{1,0:T(8,128)(2,1)S(1)}, bf16[256,1024]{1,0:T(8,128)(2,1)S(1)}, u32[]{:S(2)}, u32[]{:S(2)}) collective-permute-start(bf16[256,1024]{1,0:T(8,128)(2,1)S(1)} %bitcast.115), channel_id=1, source_target_pairs={{0,8},{4,12},{8,0},{12,4},{16,24},{20,28},{24,16},{28,20},{1,9},{5... | collective-permute-start | bytes 1572872 | tf_op jit(solution)/shard_map/ppermute | solution.py:352
  30.4 29.8 %collective-permute-start.3 = (bf16[256,1024]{1,0:T(8,128)(2,1)S(1)}, bf16[256,1024]{1,0:T(8,128)(2,1)}, u32[]{:S(2)}, u32[]{:S(2)}) collective-permute-start(bf16[256,1024]{1,0:T(8,128)(2,1)S(1)} %bitcast.116), channel_id=1, source_target_pairs={{0,16},{4,20},{8,24},{12,28},{16,0},{20,4},{24,8},{28,12},{1,17},{... | collective-permute-start | bytes 1572872 | tf_op jit(solution)/shard_map/ppermute | solution.py:352
  34.0 56.0 %collective-permute-start = (bf16[256,1024]{1,0:T(8,128)(2,1)S(1)}, bf16[256,1024]{1,0:T(8,128)(2,1)S(1)}, u32[]{:S(2)}, u32[]{:S(2)}) collective-permute-start(bf16[256,1024]{1,0:T(8,128)(2,1)S(1)} %bitcast.117), channel_id=1, source_target_pairs={{0,4},{4,0},{8,12},{12,8},{16,20},{20,16},{24,28},{28,24},{1,5},{5... | collective-permute-start | bytes 1572872 | tf_op jit(solution)/shard_map/ppermute | solution.py:352
  35.5 53.3 %all-to-all-start.2 = ((f32[8,16,768]{2,1,0:T(8,128)}), f32[8,16,768]{2,1,0:T(8,128)S(1)}, u32[]{:S(2)}, u32[]{:S(2)}) async-start(f32[8,16,768]{2,1,0:T(8,128)} %broadcast_in_dim.21), calls=%async_computation.2 | async-start | bytes 786432 | tf_op jit(solution)/shard_map/all_to_all | solution.py:356
  60.2 40.4 %collective-permute-start.4 = (bf16[256,1024]{1,0:T(8,128)(2,1)}, bf16[256,1024]{1,0:T(8,128)(2,1)}, u32[]{:S(2)}, u32[]{:S(2)}) collective-permute-start(bf16[256,1024]{1,0:T(8,128)(2,1)} %collective-permute-done.3.c_ref), channel_id=1, source_target_pairs={{0,4},{4,0},{8,12},{12,8},{16,20},{20,16},{24,28},{28,24},{1,5},{5... | collective-permute-start | bytes 1572872 | tf_op jit(solution)/shard_map/ppermute | solution.py:352
  60.5 27.1 %collective-permute-start.5 = (bf16[256,1024]{1,0:T(8,128)(2,1)}, bf16[256,1024]{1,0:T(8,128)(2,1)}, u32[]{:S(2)}, u32[]{:S(2)}) collective-permute-start(bf16[256,1024]{1,0:T(8,128)(2,1)} %collective-permute-done.3.c_ref), channel_id=1, source_target_pairs={{0,8},{4,12},{8,0},{12,4},{16,24},{20,28},{24,16},{28,20},{1,9},{5... | collective-permute-start | bytes 1572872 | tf_op jit(solution)/shard_map/ppermute | solution.py:352
  60.5 30.8 %collective-permute-start.2 = (bf16[256,1024]{1,0:T(8,128)(2,1)S(1)}, bf16[256,1024]{1,0:T(8,128)(2,1)}, u32[]{:S(2)}, u32[]{:S(2)}) collective-permute-start(bf16[256,1024]{1,0:T(8,128)(2,1)S(1)} %collective-permute-done.1.b_ref), channel_id=1, source_target_pairs={{0,4},{4,0},{8,12},{12,8},{16,20},{20,16},{24,28},{28,24},{1,5},{5... | collective-permute-start | bytes 1572872 | tf_op jit(solution)/shard_map/ppermute | solution.py:352
  87.6 43.3 %collective-permute-start.8 = (bf16[256,1024]{1,0:T(8,128)(2,1)}, bf16[256,1024]{1,0:T(8,128)(2,1)}, u32[]{:S(2)}, u32[]{:S(2)}) collective-permute-start(bf16[256,1024]{1,0:T(8,128)(2,1)} %collective-permute-done.5.d_ref), channel_id=1, source_target_pairs={{0,4},{4,0},{8,12},{12,8},{16,20},{20,16},{24,28},{28,24},{1,5},{5... | collective-permute-start | bytes 1572872 | tf_op jit(solution)/shard_map/ppermute | solution.py:352
  91.3 39.6 %collective-permute-start.11 = (bf16[768,128]{1,0:T(8,128)(2,1)S(1)}, bf16[768,128]{1,0:T(8,128)(2,1)S(1)}, u32[]{:S(2)}, u32[]{:S(2)}) collective-permute-start(bf16[768,128]{1,0:T(8,128)(2,1)S(1)} %pad_maximum_fusion.7), channel_id=1, source_target_pairs={{0,24},{4,28},{8,16},{12,20},{16,8},{20,12},{24,0},{28,4},{1,25},{... | collective-permute-start | bytes 589832 | tf_op jit(solution)/shard_map/ppermute | solution.py:352
  131.0 28.8 %collective-permute-start.12 = (bf16[4,768,128]{2,1,0:T(8,128)(2,1)S(1)}, bf16[4,768,128]{2,1,0:T(8,128)(2,1)S(1)}, u32[]{:S(2)}, u32[]{:S(2)}) collective-permute-start(bf16[4,768,128]{2,1,0:T(8,128)(2,1)S(1)} %pad_maximum_fusion.1), channel_id=1, source_target_pairs={{0,4},{4,0},{8,12},{12,8},{16,20},{20,16},{24,28},{28,24},{1,5},{5... | collective-permute-start | bytes 2359304 | tf_op jit(solution)/shard_map/ppermute | solution.py:352
  168.7 34.0 %collective-permute-start.13 = (bf16[8,768,128]{2,1,0:T(8,128)(2,1)}, bf16[8,768,128]{2,1,0:T(8,128)(2,1)S(1)}, u32[]{:S(2)}, u32[]{:S(2)}) collective-permute-start(bf16[8,768,128]{2,1,0:T(8,128)(2,1)} %get-tuple-element.127), channel_id=1, source_target_pairs={{0,2},{1,3},{2,0},{3,1},{4,6},{5,7},{6,4},{7,5},{8,10},{9,11},{10,... | collective-permute-start | bytes 4718600 | tf_op jit(solution)/shard_map/ppermute | solution.py:352
  213.1 64.7 %collective-permute-start.16 = (bf16[16,768,128]{2,1,0:T(8,128)(2,1)}, bf16[16,768,128]{2,1,0:T(8,128)(2,1)}, u32[]{:S(2)}, u32[]{:S(2)}) collective-permute-start(bf16[16,768,128]{2,1,0:T(8,128)(2,1)} %constant_dynamic-update-slice_fusion.5.refs_0_), channel_id=1, source_target_pairs={{0,1},{1,0},{2,3},{3,2},{4,5},{5,4},{6,7},{7,6},{8,9},{9,8},{10,11... | collective-permute-start | bytes 9437192 | tf_op jit(solution)/shard_map/ppermute | solution.py:352
  224.6 48.7 %collective-permute-start.19 = (bf16[2,4,768,128]{3,2,1,0:T(8,128)(2,1)}, bf16[2,4,768,128]{3,2,1,0:T(8,128)(2,1)S(1)}, u32[]{:S(2)}, u32[]{:S(2)}) collective-permute-start(bf16[2,4,768,128]{3,2,1,0:T(8,128)(2,1)} %get-tuple-element.115), channel_id=1, source_target_pairs={{0,4},{4,0},{8,12},{12,8},{16,20},{20,16},{24,28},{28,24},{1,5},{5... | collective-permute-start | bytes 4718600 | tf_op jit(solution)/shard_map/ppermute | solution.py:352
  224.6 46.7 %collective-permute-start.24 = (bf16[8,512,128]{2,1,0:T(8,128)(2,1)}, bf16[8,512,128]{2,1,0:T(8,128)(2,1)}, u32[]{:S(2)}, u32[]{:S(2)}) collective-permute-start(bf16[8,512,128]{2,1,0:T(8,128)(2,1)} %get-tuple-element.121), channel_id=1, source_target_pairs={{0,2},{1,3},{2,0},{3,1},{4,6},{5,7},{6,4},{7,5},{8,10},{9,11},{10,... | collective-permute-start | bytes 3145736 | tf_op jit(solution)/shard_map/ppermute | solution.py:352
  264.1 45.2 %all-to-all-start.5 = ((bf16[8,256,384]{2,1,0:T(8,128)(2,1)}), bf16[8,256,384]{2,1,0:T(8,128)(2,1)S(1)}, u32[]{:S(2)}, u32[]{:S(2)}) async-start(bf16[8,256,384]{2,1,0:T(8,128)(2,1)} %bitcast.30), calls=%async_computation.5 | async-start | bytes 3145728 | tf_op jit(solution)/shard_map/all_to_all | solution.py:356
  272.9 26.0 %collective-permute-start.25 = (bf16[4,512,128]{2,1,0:T(8,128)(2,1)S(1)}, bf16[4,512,128]{2,1,0:T(8,128)(2,1)S(1)}, u32[]{:S(2)}, u32[]{:S(2)}) collective-permute-start(bf16[4,512,128]{2,1,0:T(8,128)(2,1)S(1)} %slice.129), channel_id=1, source_target_pairs={{0,4},{4,0},{8,12},{12,8},{16,20},{20,16},{24,28},{28,24},{1,5},{5... | collective-permute-start | bytes 1572872 | tf_op jit(solution)/shard_map/ppermute | solution.py:352
  273.7 28.9 %collective-permute-start.20 = (bf16[4,768,128]{2,1,0:T(8,128)(2,1)S(1)}, bf16[4,768,128]{2,1,0:T(8,128)(2,1)S(1)}, u32[]{:S(2)}, u32[]{:S(2)}) collective-permute-start(bf16[4,768,128]{2,1,0:T(8,128)(2,1)S(1)} %fusion.6), channel_id=1, source_target_pairs={{0,2},{1,3},{2,0},{3,1},{4,6},{5,7},{6,4},{7,5},{8,10},{9,11},{10,... | collective-permute-start | bytes 2359304 | tf_op jit(solution)/shard_map/ppermute | solution.py:352
  299.9 30.3 %collective-permute-start.28 = (bf16[512,128]{1,0:T(8,128)(2,1)}, bf16[512,128]{1,0:T(8,128)(2,1)S(1)}, u32[]{:S(2)}, u32[]{:S(2)}) collective-permute-start(bf16[512,128]{1,0:T(8,128)(2,1)} %get-tuple-element.129), channel_id=1, source_target_pairs={{0,24},{4,28},{8,16},{12,20},{16,8},{20,12},{24,0},{28,4},{1,25},{... | collective-permute-start | bytes 393224 | tf_op jit(solution)/shard_map/ppermute | solution.py:352
  301.1 29.4 %collective-permute-start.27 = (bf16[512,128]{1,0:T(8,128)(2,1)}, bf16[512,128]{1,0:T(8,128)(2,1)}, u32[]{:S(2)}, u32[]{:S(2)}) collective-permute-start(bf16[512,128]{1,0:T(8,128)(2,1)} %get-tuple-element.130), channel_id=1, source_target_pairs={{0,16},{4,20},{8,24},{12,28},{16,0},{20,4},{24,8},{28,12},{1,17},{... | collective-permute-start | bytes 393224 | tf_op jit(solution)/shard_map/ppermute | solution.py:352
  301.2 29.3 %collective-permute-start.26 = (bf16[512,128]{1,0:T(8,128)(2,1)}, bf16[512,128]{1,0:T(8,128)(2,1)}, u32[]{:S(2)}, u32[]{:S(2)}) collective-permute-start(bf16[512,128]{1,0:T(8,128)(2,1)} %get-tuple-element.128), channel_id=1, source_target_pairs={{0,8},{4,12},{8,0},{12,4},{16,24},{20,28},{24,16},{28,20},{1,9},{5... | collective-permute-start | bytes 393224 | tf_op jit(solution)/shard_map/ppermute | solution.py:352
  311.2 21.1 %collective-permute-start.23 = (bf16[768,128]{1,0:T(8,128)(2,1)}, bf16[768,128]{1,0:T(8,128)(2,1)S(1)}, u32[]{:S(2)}, u32[]{:S(2)}) collective-permute-start(bf16[768,128]{1,0:T(8,128)(2,1)} %get-tuple-element.124), channel_id=1, source_target_pairs={{0,24},{4,28},{8,16},{12,20},{16,8},{20,12},{24,0},{28,4},{1,25},{... | collective-permute-start | bytes 589832 | tf_op jit(solution)/shard_map/ppermute | solution.py:352
  312.5 21.3 %collective-permute-start.22 = (bf16[768,128]{1,0:T(8,128)(2,1)}, bf16[768,128]{1,0:T(8,128)(2,1)}, u32[]{:S(2)}, u32[]{:S(2)}) collective-permute-start(bf16[768,128]{1,0:T(8,128)(2,1)} %get-tuple-element.125), channel_id=1, source_target_pairs={{0,16},{4,20},{8,24},{12,28},{16,0},{20,4},{24,8},{28,12},{1,17},{... | collective-permute-start | bytes 589832 | tf_op jit(solution)/shard_map/ppermute | solution.py:352
  (41 other events, 411.6 us)
Sparse Core Ops, SparseCore 0:
  11.3 121.8 all-gather.2

commit v3 on v2

--- a/solution.py
+++ b/solution.py
@@ -356,28 +356,6 @@
     return lax.all_to_all(blocks, "seq", 0, 0, tiled=True)
 
 
-def sum_over_replicas(grad):
-    place = lax.axis_index("batch")
-    x, core = place // 2, place % 2
-    rows, cols = grad.shape[0] // REPLICAS, grad.shape[1]
-    parts = grad.reshape(2, 2, rows, cols)
-    keep = lax.dynamic_index_in_dim(parts, core, 1, False)
-    send = lax.dynamic_index_in_dim(parts, 1 - core, 1, False)
-    both = (
-        keep.astype(jnp.float32) + swap(send.astype(jnp.bfloat16), "batch", 1).astype(jnp.float32)
-    ).astype(jnp.bfloat16)
-    keep = lax.dynamic_index_in_dim(both, x, 0, False)
-    send = lax.dynamic_index_in_dim(both, 1 - x, 0, False)
-    return keep.astype(jnp.float32) + swap(send, "batch", 2).astype(jnp.float32)
-
-
-def along_z(part):
-    total = part[0].astype(jnp.float32)
-    for k in range(1, 4):
-        total = total + swap(part[k], "seq", 2 * k).astype(jnp.float32)
-    return total
-
-
 def turn(vectors, cosine, sine):
     lane = lax.broadcasted_iota(jnp.int32, vectors.shape, 1)
     first = (lane % HEAD) < HEAD // 2
@@ -491,7 +469,7 @@
         ],
         input_output_aliases={first + i: i for i in range(len(earlier))},
         compiler_params=params(VMEM_MIB),
-        cost_estimate=cost(5),
+        cost_estimate=cost(2),
         name="project",
     )(*inputs)
 
@@ -633,22 +611,34 @@
     return jnp.concatenate([ref[tile, rows, :] for tile in tiles], axis=1)
 
 
-def middle_kernel(mine_ref, x_ref, cot_ref, member_ref, clip_ref, emb_ref, tiles_ref,
-                  result_ref, grad_middle_ref, grad_att_ref, grad_emb_ref, left_ref, right_ref,
-                  out_ref, up_ref, down_ref, sems, branch_ref, low_ref, act_ref, slope_ref,
-                  wide_ref):
+def tile_index(away, apart):
+    return 16 * (away % 2) + 8 * (away // 2) + 4 * (apart % 2) + apart // 2
+
+
+def middle_kernel(mine_ref, x_ref, cot_ref, member_ref, clip_ref, emb_ref, *refs):
+    *tile_refs, result_ref, grad_middle_ref, grad_att_ref, grad_emb_ref, left_ref, right_ref = refs[:-9]
+    out_ref, up_ref, down_ref, sems, branch_ref, low_ref, act_ref, slope_ref, wide_ref = refs[-9:]
     low = jnp.bfloat16
     act_t_ref, ffn_t_ref = left_ref.at[:2 * D], left_ref.at[2 * D:3 * D]
     mine_t_ref = left_ref.at[3 * D:]
     g_ffn_ref, g_attn_ref = right_ref.at[:, :D], right_ref.at[:, 3 * D:]
     g_hidden_ref = right_ref.at[:, D:3 * D]
     pieces = ((out_ref, 0, 256), (up_ref, 256, 512), (down_ref, 768, 512))
+    for i, (ref, start, size) in enumerate(pieces):
+        first = 0
+        for tile_ref in tile_refs:
+            count = tile_ref.shape[0]
+            pltpu.make_async_copy(
+                tile_ref.at[:, pl.ds(start, size), :], ref.at[pl.ds(first, count)], sems.at[i]
+            ).start()
+            first += count
     copies = [
-        pltpu.make_async_copy(tiles_ref.at[:, pl.ds(start, size), :], ref, sems.at[i])
-        for i, (ref, start, size) in enumerate(pieces)
+        pltpu.make_async_copy(ref, ref, sems.at[i]) for i, (ref, _, _) in enumerate(pieces)
     ]
-    for copy in copies:
-        copy.start()
+
+    def tile(b, s):
+        return SEQ * b + s
+
     member = member_ref[...]
 
     def modulation(index):
@@ -668,7 +658,7 @@
     def _(n):
         total = jnp.zeros((ROWS, 256), jnp.float32)
         for b in range(REPLICAS):
-            weight = beside(out_ref, [8 * b + 2 * n, 8 * b + 2 * n + 1], every)
+            weight = beside(out_ref, [tile(b, 2 * n), tile(b, 2 * n + 1)], every)
             total = total + matmul(low_ref[:, 256 * b:256 * b + 256], weight)
         branch_ref[:, cols(n)] = total
 
@@ -688,8 +678,8 @@
     def _(n):
         hidden = jnp.zeros((ROWS, 256), jnp.float32)
         for b in range(REPLICAS):
-            tile = 8 * b + n
-            weight = jnp.concatenate([up_ref[tile, :256, :], up_ref[tile, 256:, :]], axis=1)
+            index = tile(b, n)
+            weight = jnp.concatenate([up_ref[index, :256, :], up_ref[index, 256:, :]], axis=1)
             hidden = hidden + matmul(low_ref[:, 256 * b:256 * b + 256], weight)
         root = math.sqrt(2.0 / math.pi)
         squared = hidden * hidden
@@ -709,7 +699,7 @@
     def _(n):
         total = jnp.zeros((ROWS, 256), jnp.float32)
         for b in range(REPLICAS):
-            weight = beside(down_ref, [8 * b + 2 * n, 8 * b + 2 * n + 1], every)
+            weight = beside(down_ref, [tile(b, 2 * n), tile(b, 2 * n + 1)], every)
             total = total + matmul(act_ref[:, 512 * b:512 * b + 512], weight)
         wide_ref[:, cols(n)] = total
 
@@ -719,7 +709,7 @@
 
     @pl.loop(0, REPLICAS)
     def _(b):
-        weight = beside(down_ref, [8 * b + s for s in range(SEQ)], every)
+        weight = beside(down_ref, [tile(b, s) for s in range(SEQ)], every)
         grad = dot_t(g_ffn_ref[...], weight)
         here = cols(b, 512)
         g_hidden_ref[:, here] = (grad * slope_ref[:, here]).astype(low)
@@ -727,7 +717,7 @@
     @pl.loop(0, REPLICAS)
     def _(b):
         weight = jnp.concatenate(
-            [up_ref[8 * b + s, 256 * k:256 * k + 256, :] for s in range(SEQ) for k in range(2)],
+            [up_ref[tile(b, s), 256 * k:256 * k + 256, :] for s in range(SEQ) for k in range(2)],
             axis=1,
         )
         wide_ref[:, cols(b)] = dot_t(g_hidden_ref[...], weight)
@@ -747,7 +737,7 @@
 
     @pl.loop(0, REPLICAS)
     def _(b):
-        weight = beside(out_ref, [8 * b + s for s in range(SEQ)], every)
+        weight = beside(out_ref, [tile(b, s) for s in range(SEQ)], every)
         grad = dot_t(g_attn_ref[...], weight).astype(low)
         grad_att_ref[2 * b] = grad[:, :TWO]
         grad_att_ref[2 * b + 1] = grad[:, TWO:]
@@ -763,7 +753,7 @@
     vmem = pl.BlockSpec(memory_space=pltpu.VMEM)
     return pl.pallas_call(
         middle_kernel,
-        in_specs=[vmem] * 6 + [pl.BlockSpec(memory_space=pl.ANY)],
+        in_specs=[vmem] * 6 + [pl.BlockSpec(memory_space=pl.ANY)] * len(tiles),
         out_specs=[vmem] * len(shapes),
         out_shape=[jax.ShapeDtypeStruct(shape, dtype) for shape, dtype in shapes],
         scratch_shapes=[
@@ -780,7 +770,7 @@
         compiler_params=pltpu.CompilerParams(vmem_limit_bytes=VMEM_MIB * 1024 * 1024),
         cost_estimate=cost(20),
         name="middle",
-    )(mine, x, cot, member, clip_row, emb, tiles)
+    )(mine, x, cot, member, clip_row, emb, *tiles)
 
 
 def weight_grads_kernel(place_ref, down_l, up_l, out_l, right_ref, down_o, up_o, out_o, other_ref,
@@ -848,34 +838,60 @@
     )(place, left, left, left, right, other_left, other_left, other_left, other_right)
 
 
-def last_kernel(place_ref, own_ref, x_ref, grad_middle_ref, member_ref, clip_ref, emb_ref, *refs):
-    *tile_refs, out_ref, grad_emb_ref, wide_ref = refs
+def clip_grads_kernel(place_ref, x_ref, clip_ref, g_ref, w_ref, out_ref):
+    @pl.when(pl.program_id(0) == 0)
+    def _():
+        out_ref[...] = jnp.zeros_like(out_ref)
+
+    normed, _ = standardize(x_ref[...].astype(jnp.float32))
+    grad = jnp.concatenate(
+        [dot_t(g_ref[...], w_ref[b ^ place_ref[1]]) for b in range(REPLICAS)], axis=1
+    )
+    out_ref[:, :D] += sum_of_clips(clip_ref, grad)
+    out_ref[:, D:] += sum_of_clips(clip_ref, grad * normed)
+
+
+def clip_grads(places, x, clip_row, g_heads, heads_w):
+    frames = x.shape[0]
+    return pl.pallas_call(
+        clip_grads_kernel,
+        grid=(frames // ROWS,),
+        in_specs=[pl.BlockSpec(memory_space=pltpu.SMEM), rows_spec(D), cols_spec(1),
+                  rows_spec(3 * TWO),
+                  pl.BlockSpec((REPLICAS, ROWS, 3 * TWO), lambda i: (0, 0, 0))],
+        out_specs=whole_spec(CLIPS, 2 * D),
+        out_shape=jax.ShapeDtypeStruct((CLIPS, 2 * D), jnp.float32),
+        compiler_params=params(VMEM_MIB),
+        cost_estimate=cost(9),
+        name="clip_grads",
+    )(places, x, clip_row, g_heads, heads_w)
+
+
+def last_kernel(place_ref, own_ref, x_ref, grad_middle_ref, member_ref, emb_ref, *refs):
+    *tile_refs, out_ref, wide_ref = refs
     grads = jnp.concatenate([own_ref[place_ref[2] ^ s] for s in range(SEQ)], axis=1)
 
-    def tile(apart, s):
-        index = apart * SEQ + (s % 2) * 4 + s // 2
+    def tile(away, apart):
+        index = tile_index(away, apart)
         for ref in tile_refs:
             if index < ref.shape[0]:
-                return ref[index]
+                return ref[index, ref.shape[1] - 768:, :]
             index -= ref.shape[0]
 
-    for apart in range(REPLICAS):
+    for away in range(REPLICAS):
         weight = jnp.concatenate(
             [
-                tile(apart, s)[256 * k:256 * k + 256, :]
+                tile(away, s)[256 * k:256 * k + 256, :]
                 for s in range(SEQ)
                 for k in range(3)
             ],
             axis=1,
         )
-        b = (2 * place_ref[0] + place_ref[1]) ^ ((apart % 2) * 2 + apart // 2)
+        b = (2 * place_ref[0] + place_ref[1]) ^ away
         wide_ref[:, pl.ds(pl.multiple_of(b * 256, 256), 256)] = dot_t(grads, weight)
 
     normed, inverse = standardize(x_ref[...].astype(jnp.float32))
-    grad_input = wide_ref[...]
-    grad_emb_ref[:, :D] = sum_of_clips(clip_ref, grad_input)
-    grad_emb_ref[:, D:] = sum_of_clips(clip_ref, grad_input * normed)
-    spread = grad_input * (1.0 + matmul(member_ref[...], emb_ref[:, D:2 * D]))
+    spread = wide_ref[...] * (1.0 + matmul(member_ref[...], emb_ref[:, D:2 * D]))
     grad = grad_middle_ref[...] + inverse * (
         spread
         - jnp.mean(spread, axis=1, keepdims=True)
@@ -884,21 +900,18 @@
     out_ref[...] = grad.astype(jnp.bfloat16)
 
 
-def last_part(place, own, x, grad_middle, member, clip_row, emb, tiles):
+def last_part(place, own, x, grad_middle, member, emb, tiles):
     vmem = pl.BlockSpec(memory_space=pltpu.VMEM)
     return pl.pallas_call(
         last_kernel,
-        in_specs=[pl.BlockSpec(memory_space=pltpu.SMEM)] + [vmem] * (6 + len(tiles)),
-        out_specs=[vmem, vmem],
-        out_shape=[
-            jax.ShapeDtypeStruct((ROWS, D), jnp.bfloat16),
-            jax.ShapeDtypeStruct((CLIPS, 2 * D), jnp.float32),
-        ],
+        in_specs=[pl.BlockSpec(memory_space=pltpu.SMEM)] + [vmem] * (5 + len(tiles)),
+        out_specs=vmem,
+        out_shape=jax.ShapeDtypeStruct((ROWS, D), jnp.bfloat16),
         scratch_shapes=[pltpu.VMEM((ROWS, D), jnp.float32)],
         compiler_params=pltpu.CompilerParams(vmem_limit_bytes=30 * 1024 * 1024),
         cost_estimate=cost(4),
         name="last",
-    )(place, own, x, grad_middle, member, clip_row, emb, *tiles)
+    )(place, own, x, grad_middle, member, emb, *tiles)
 
 
 def after(value, *others):
@@ -934,32 +947,39 @@
     frames = frame_count * SEQ
     segment = segments[0]
 
-    mine_w = jnp.concatenate(
-        [w_out, w_up[:, :128], w_up[:, 128:], w_down], axis=0
-    ).astype(low)
-    tiles = lax.all_gather(mine_w, ("batch", "seq"), axis=0)
-
-    own_codes = segment * 2 + (validity[0] == 1)
-    codes = exchange(jnp.broadcast_to(own_codes[None], (SEQ, frame_count))).reshape(frames)
+    seat = lax.axis_index("seq").astype(jnp.int32)
+    z, y = seat // 2, seat % 2
+    place = jnp.stack([replica // 2, replica % 2, seat]).astype(jnp.int32)
+    mine_w = jnp.concatenate([w_out, w_up[:, :128], w_up[:, 128:], w_down], axis=0).astype(low)
+
+    z1, z2, y0 = swap(x, "seq", 2), swap(x, "seq", 4), swap(x, "seq", 1)
     times = lax.all_gather(timesteps[0], "batch", axis=0, tiled=True)
     silu_all = jax.nn.silu(time_embedding(times)).astype(low)
     depth = w_ada.shape[0]
     silu_part = lax.dynamic_slice_in_dim(silu_all, replica * depth, depth, 1)
     emb_part = matmul(silu_part, w_ada.astype(low)).reshape(REPLICAS, CLIPS, -1)
     emb_cols = lax.all_to_all(emb_part, "batch", 0, 0, tiled=True)
-    start = after(x, emb_part, codes)
-    z1, z2, y0 = swap(start, "seq", 2), swap(start, "seq", 4), swap(start, "seq", 1)
     emb_cols = jnp.sum(emb_cols, axis=0)
-    emb = exchange(jnp.broadcast_to(emb_cols[None], (SEQ,) + emb_cols.shape))
-    z1 = after(z1, emb_cols)
-    y1 = swap(z1, "seq", 1)
-    z2 = after(z2, emb_cols)
-    y2, z3 = swap(z2, "seq", 1), swap(z2, "seq", 2)
+    own_codes = (segment * 2 + (validity[0] == 1)).astype(wide)
+    cols = emb_cols.shape[1]
+    own_codes = jnp.pad(own_codes, (0, 8 * cols - frame_count)).reshape(8, cols)
+    packed = jnp.concatenate([emb_cols, own_codes])
+    packed = jnp.broadcast_to(packed[None], (SEQ,) + packed.shape)
     heads_w = jnp.concatenate([w_query, w_key, w_value], axis=1).astype(low)
     heads_w = jnp.stack([heads_w, swap(heads_w, "batch", 1)])
-    heads_w = jnp.concatenate([heads_w, swap(after(heads_w, z1), "batch", 2)])
-    codes = after(codes, z2)
+    z1, z2, y0, packed, heads_w, mine_w = together(z1, z2, y0, packed, heads_w, mine_w)
+    tiles_w = (lax.all_gather(mine_w, ("batch", "seq"), axis=0),)
+    packed = exchange(packed)
+    z3 = swap(z2, "seq", 2)
+    y1, y2 = swap(z1, "seq", 1), swap(z2, "seq", 1)
+    heads_x = swap(heads_w, "batch", 2)
+    z3, y1, y2, heads_x = together(z3, y1, y2, heads_x)
+    y3 = swap(z3, "seq", 1)
+    heads_w = jnp.concatenate([heads_w, heads_x])
+    emb = packed[:, :CLIPS]
+    codes = packed[:, CLIPS:].reshape(SEQ, -1)[:, :frame_count].reshape(frames).astype(jnp.int32)
     clip = codes // 2
+    clip_row = clip[None, :]
     tri = jnp.arange(frame_count)[:, None] > jnp.arange(frame_count)[None, :]
     ids = jnp.arange(CLIPS, dtype=jnp.int32)
     one_hot = (clip.reshape(SEQ, frame_count)[:, :, None] == ids).astype(low)
@@ -975,78 +995,90 @@
     allowed = clip_lanes(jnp.where(codes % 2 == 1, clip, -1), 1)
     inside = jnp.arange(TWO, dtype=jnp.int32)[None, :] < CLIPS
     bar = jnp.where(inside & ~allowed, -BIG, 0.0).astype(low)
-    z3 = after(z3, member, bar, cosine, sine, heads_w)
-    y3 = swap(z3, "seq", 1)
-    mine_h = jnp.concatenate([w_query, w_key, w_value], axis=0).astype(low)
-    mine_h = after(mine_h, z3)
-    tiles_z = [swap(mine_h, "seq", 2 * k) for k in range(1, 4)]
-    line, other = (x, z1, z2, z3), (y0, y1, y2, y3)
-    emb = after(emb, z3)
+    emb = after(emb, heads_w, member, cosine)
     emb = emb.transpose(1, 0, 2).reshape(CLIPS, -1)
     emb = jnp.concatenate(
         [t.astype(low) for t in three_terms(emb)] + [jnp.zeros((TWO - 3 * CLIPS, 6 * D), low)],
         axis=0,
     )
 
-    seat = lax.axis_index("seq").astype(jnp.int32)
     tables = (member, bar, cosine, sine, emb[:, :2 * D], heads_w)
     places = jnp.stack([seat, replica.astype(jnp.int32)])
-    earlier = project(places, 0, line, *tables, ())
-    *other, tiles_1, tiles_2, tiles_3 = together(*other, *tiles_z)
-    tiles_z = [tiles_1, tiles_2, tiles_3]
-    x_all, attn_input, q, k, kt, v, vt = project(places, 1, other, *tables, earlier)
-    tiles_z = jnp.stack([mine_h] + tiles_z)
-    tiles_y = swap(tiles_z, "seq", 1)
-    attended, attended_low, log_total = attend(after(q, tiles_z), member, k, vt)
-    attended_low, tiles_y = together(attended_low, tiles_y)
-    tiles_zy = jnp.concatenate([tiles_z, tiles_y])
-    tiles_x = swap(tiles_zy, "batch", 2)
+    earlier = project(places, 0, (x, z1, z2, z3), *tables, ())
+    y3, earlier = together(y3, earlier)
+    mine_h = jnp.concatenate([w_query, w_key, w_value], axis=0).astype(low)
+    mine_h = after(mine_h, y3)
+    x_all, attn_input, q, k, kt, v, vt = project(places, 1, (y0, y1, y2, y3), *tables, earlier)
+    h_z1, h_z2 = swap(mine_h, "seq", 2), swap(mine_h, "seq", 4)
+    attended, attended_low, log_total = attend(q, member, k, vt)
+    attended_low, h_z1, h_z2 = together(attended_low, h_z1, h_z2)
+    h_z3 = swap(h_z2, "seq", 2)
     mine = exchange(attended_low.reshape(SEQ, frame_count, TWO))
-    mine = after(mine, tiles_zy)
+    mine, h_z3 = together(mine, h_z3)
+    h_z = jnp.stack([mine_h, h_z1, h_z2, h_z3])
+    h_y, h_x = swap(h_z, "seq", 1), swap(h_z, "batch", 2)
 
     own_member = clip_lanes(segment, 3).astype(low)
     result, grad_middle, grad_att, grad_emb, left, right = middle_part(
-        mine, x, cotangent[0], own_member, segment[None, :], emb, tiles
-    )
-    place = jnp.stack([replica // 2, replica % 2, seat]).astype(jnp.int32)
-    left, tiles_x = together(left, tiles_x)
+        mine, x, cotangent[0], own_member, segment[None, :], emb, tiles_w
+    )
+    left, h_y, h_x = together(left, h_y, h_x)
+    h_yx = swap(h_y, "batch", 2)
     other_left, other_right = swap(left, "batch", 1), swap(right, "batch", 1)
     away_d, keep_d, away_u, keep_u = weight_grads(place, left, right, other_left, other_right)
     grad_heads = exchange(grad_att).reshape(frames, TWO)
     grad_heads, away_d, away_u = together(grad_heads, away_d, away_u)
     from_x = swap(away_d, "batch", 2)
     from_y = swap(away_u, "seq", 1)
-    tiles_zyx = jnp.concatenate([tiles_zy, tiles_x])
-    grad_heads = after(grad_heads, tiles_zyx)
-    tiles_c = swap(tiles_zyx, "batch", 1)
 
     g_heads = attend_back(
         q, member, grad_heads, attended, log_total, cosine, sine, k, kt, v
     )
     own = exchange(g_heads.reshape(SEQ, frame_count, 3 * TWO))
-    from_x, from_y, tiles_c = after(from_x, g_heads), after(from_y, g_heads), after(tiles_c, g_heads)
-    near_d = plus(keep_d, from_x)
+    near_d = plus(keep_d, after(from_x, g_heads))
     from_y_d = swap(near_d[4:].astype(low), "seq", 1)
-    near_u = plus(keep_u, from_y)
+    near_u = plus(keep_u, after(from_y, near_d, h_yx))
     from_x_u = swap(near_u[1].astype(low), "batch", 2)
-    part_d = plus(near_d[:4], from_y_d).astype(low)
-    part_u = after(plus(near_u[0], from_x_u).astype(low), own)
-    final_d = along_z(part_d)
-    final_uo = along_z(part_u)
+    g_heads = after(g_heads, near_d, near_u)
+    late = clip_grads(places, x_all, clip_row, g_heads, heads_w)
+    grad_heads_w = matmul(attn_input.T, g_heads).astype(low).reshape(2, 2, ROWS, 3 * TWO)
+    h_first = jnp.concatenate([after(h_z, near_u), h_y, h_x])
+    h_first_core = swap(h_first, "batch", 1)
+    late, grad_heads_w, from_y_d, from_x_u, h_first, h_first_core = together(
+        late, grad_heads_w, from_y_d, from_x_u, h_first, h_first_core
+    )
+    part = jnp.concatenate(
+        [plus(near_u[0], from_x_u).astype(low), plus(near_d[:4], from_y_d).astype(low)], axis=1
+    )
+    late, own = together(late, own)
+    grad_emb = jnp.concatenate([late, grad_emb], axis=1)
+    grad_emb = grad_emb.reshape(CLIPS, 4, 2, -1).transpose(2, 1, 0, 3)
+    keep_e = lax.dynamic_index_in_dim(grad_emb, y, 0, False)
+    other_e = swap(lax.dynamic_index_in_dim(grad_emb, 1 - y, 0, False), "seq", 1)
+    x_place, core_place = replica // 2, replica % 2
+    grad_emb = keep_e + other_e
+    from_z_e = [
+        swap(lax.dynamic_index_in_dim(grad_emb, z ^ k, 0, False), "seq", 2 * k) for k in range(1, 4)
+    ]
+    grad_emb = plus(lax.dynamic_index_in_dim(grad_emb, z, 0, False), *from_z_e)
+    keep_h = lax.dynamic_index_in_dim(grad_heads_w, core_place, 1, False)
+    other_h = swap(lax.dynamic_index_in_dim(grad_heads_w, 1 - core_place, 1, False), "batch", 1)
+    h_yx_core = swap(after(h_yx, part), "batch", 1)
+    from_z = [swap(part[k], "seq", 2 * k) for k in range(1, 4)]
+    both_h = plus(keep_h, other_h).astype(low)
+    away_h = swap(lax.dynamic_index_in_dim(both_h, 1 - x_place, 0, False), "batch", 2)
+
+    grad_tokens = last_part(place, own, x, grad_middle, own_member, emb,
+        (h_first, h_yx, h_first_core, h_yx_core),
+    )
+    grad_emb = lax.all_gather(grad_emb, "batch", axis=0, tiled=True)
+    final_a = jnp.dot(silu_part.astype(wide).T, grad_emb, precision=highest)
+    grad_tokens, final_a, away_h, *from_z = together(grad_tokens, final_a, away_h, *from_z)
+    final_heads = plus(lax.dynamic_index_in_dim(both_h, x_place, 0, False), away_h)
+    total = plus(part[0], *from_z)
+    final_uo, final_d = total[:768], total[768:]
     final_o = final_uo[:256]
     final_u = jnp.concatenate([final_uo[256:512], final_uo[512:]], axis=1)
-
-    grad_heads_w = matmul(attn_input.T, g_heads).astype(low)
-    final_heads = sum_over_replicas(grad_heads_w)
-    grad_tokens, late = last_part(
-        place, own, x, grad_middle, own_member, segment[None, :], emb,
-        (tiles_zyx, tiles_c),
-    )
-    grad_emb = jnp.concatenate([late, grad_emb], axis=1)
-    grad_emb = grad_emb.reshape(CLIPS, SEQ, -1).transpose(1, 0, 2)
-    grad_emb = jnp.sum(exchange(grad_emb), axis=0)
-    grad_emb = lax.all_gather(grad_emb, "batch", axis=0, tiled=True)
-    final_a = jnp.dot(silu_part.astype(wide).T, grad_emb, precision=highest)
     width = w_query.shape[1]
     return (
         result[None],

time: 364 us -> 324 us (0.89)
  waiting for transfers between devices: 118 us -> 58.7 us
  Pallas kernels: 102 us -> 112 us
  starting transfers between devices: 63.4 us -> 68.9 us
    ppermute x29 -> x32, waiting for transfers between devices: 105 us -> 53.2 us  [swap(): return lax.ppermute(part, axis, [(i, i ^ distance) for i in range(size)])]
    ppermute x29 -> x32, starting transfers between devices: 29.3 us -> 42.8 us  [swap(): return lax.ppermute(part, axis, [(i, i ^ distance) for i in range(size)])]
    pallas_call x0 -> x1, Pallas kernels: none -> 10.9 us  [clip_grads(): pl.pallas_call(clip_grads_kernel, grid=(frames // ROWS,), in_specs=[pl.Bl...]
    all_to_all x6 -> x4, waiting for transfers between devices: 12.3 us -> 2.16 us  [exchange(): return lax.all_to_all(blocks, 'seq', 0, 0, tiled=True)]
    all_to_all x6 -> x4, starting transfers between devices: 30.1 us -> 21.6 us  [exchange(): return lax.all_to_all(blocks, 'seq', 0, 0, tiled=True)]
    add x2 -> x5, other arithmetic: 1.86 us -> 6.75 us  [plus(): total = total + term.astype(jnp.float32)]
    unnamed x65 -> x81, local copies, waits for them, and re-layouts: 10 us -> 6.15 us
  transfers between devices with their start and end apart: 37 -> 38, of which waited for: 15 -> 12; matrix products, arithmetic and copies ran while one was open for 11% -> 16% of each run, Pallas kernels for 28% -> 35%
where the time goes in v3:
time: 324 us; the launch traced here: 323 us
  Pallas kernels  112 us (35%)
  starting transfers between devices  68.9 us (21%)
  waiting for transfers between devices  58.7 us (18%)
  other arithmetic  26.3 us (8%)
  local copies, waits for them, and re-layouts  19.5 us (6%)
  between operations  15.5 us (5%)
  blocking collectives  12.2 us (4%)
  matrix products  9.61 us (3%)
    ppermute x32, waiting for transfers between devices, swap(): return lax.ppermute(part, axis, [(i, i ^ distance) for i in range(size)])  53.2 us
    ppermute x32, starting transfers between devices, swap(): return lax.ppermute(part, axis, [(i, i ^ distance) for i in range(size)])  42.8 us
    pallas_call x1, Pallas kernels, attend_back(): pl.pallas_call(attend_back_kernel, grid=(frames // ROWS,), in_specs=[rows...  28.5 us
    all_to_all x4, starting transfers between devices, exchange(): return lax.all_to_all(blocks, 'seq', 0, 0, tiled=True)  21.6 us
    pallas_call x1, Pallas kernels, middle_part(): pl.pallas_call(middle_kernel, in_specs=[vmem] * 6 + [pl.BlockSpec(memory_...  20.8 us
    pallas_call x1, Pallas kernels, attend(): pl.pallas_call(attend_kernel, grid=(frames // ROWS,), in_specs=[rows_spec...  19.9 us
    pallas_call x2, Pallas kernels, project(): pl.pallas_call(project_kernel, grid_spec=pltpu.PrefetchScalarGridSpec(num...  17.5 us
    pallas_call x1, Pallas kernels, clip_grads(): pl.pallas_call(clip_grads_kernel, grid=(frames // ROWS,), in_specs=[pl.Bl...  10.9 us
  transfers between devices with their start and end apart: 38, of which 12 were waited for; matrix products, arithmetic and copies ran while one was open for 16% of the time, Pallas kernels for 35%

profile of v3, /device:TPU:13, one launch (start us, length us, event | category | flops | bytes accessed | tf_op | source)
XLA Modules:
  0.0 322.6 jit_solution(10332521789841667827)
XLA Ops:
  12.7 5.4 %all-reduce.1 = s32[64]{0:T(128)S(1)} all-reduce(s32[64]{0:T(128)S(1)} %bitcast_dynamic-update-slice_fusion), channel_id=2, replica_groups=mesh['seq'=8,'batch'=4] {'batch'}, use_global_device_ids=true, to_apply=%add.1 | all-reduce | flops 64 | bytes 512
  20.7 4.5 %all-to-all-start = ((f32[4,16,768]{2,1,0:T(8,128)}), f32[4,16,768]{2,1,0:T(8,128)S(1)}, u32[]{:S(2)}, u32[]{:S(2)}) async-start(f32[4,16,768]{2,1,0:T(8,128)} %bitcast.5), calls=%async_computation | async-start | bytes 393216 | tf_op jit(solution)/shard_map/all_to_all | solution.py:961
  43.2 3.9 %collective-permute-done.7 = bf16[2,256,384]{2,1,0:T(8,128)(2,1)} collective-permute-done((bf16[2,256,384]{2,1,0:T(8,128)(2,1)S(1)}, bf16[2,256,384]{2,1,0:T(8,128)(2,1)}, u32[]{:S(2)}, u32[]{:S(2)}) %collective-permute-start.7) | collective-permute-done | bytes 393248 | tf_op jit(solution)/shard_map/ppermute | solution.py:352
  47.1 15.9 %collective-permute-done.4.d_ref = bf16[256,1024]{1,0:T(8,128)(2,1)} collective-permute-done((bf16[256,1024]{1,0:T(8,128)(2,1)}, bf16[256,1024]{1,0:T(8,128)(2,1)}, u32[]{:S(2)}, u32[]{:S(2)}) %collective-permute-start.4) | collective-permute-done | bytes 524320 | tf_op jit(solution)/shard_map/ppermute | solution.py:352
  62.9 4.4 %collective-permute-done.5.b_ref = bf16[256,1024]{1,0:T(8,128)(2,1)S(1)} collective-permute-done((bf16[256,1024]{1,0:T(8,128)(2,1)}, bf16[256,1024]{1,0:T(8,128)(2,1)S(1)}, u32[]{:S(2)}, u32[]{:S(2)}) %collective-permute-start.5) | collective-permute-done | bytes 524320 | tf_op jit(solution)/shard_map/ppermute | solution.py:352
  72.4 6.3 %multiply_sine_fusion = (f32[2048,128]{1,0:T(8,128)}, f32[2048,128]{1,0:T(8,128)}) fusion(f32[128]{0:T(128)} %mul.62, f32[2048]{0:T(1024)S(1)} %bitcast.138), kind=kLoop, calls=%fused_computation.16 | loop fusion | flops 262144 | bytes 2105856 | tf_op jit(solution)/shard_map/sin | solution.py:993
  81.1 8.7 %project.2 = (bf16[2048,1024]{1,0:T(8,128)(2,1)}, bf16[2048,1024]{1,0:T(8,128)(2,1)}, bf16[2048,128]{1,0:T(8,128)(2,1)}, bf16[2048,256]{1,0:T(8,128)(2,1)}, bf16...) custom-call(s32[2]{0:T(128)} %pad_add_fusion.place_ref, bf16[256,1024]{1,0:T(8,128)(2,1)} %bitcast.117, ...), custom_call_target="tpu_custom_call" | custom-call | flops 2000000000 | bytes 6000000 | tf_op jit(solution)/shard_map/project/pallas_call | solution.py:448
  93.1 8.8 %project.3 = (bf16[2048,1024]{1,0:T(8,128)(2,1)}, bf16[2048,1024]{1,0:T(8,128)(2,1)}, bf16[2048,128]{1,0:T(8,128)(2,1)}, bf16[2048,256]{1,0:T(8,128)(2,1)}, bf16...) custom-call(s32[2]{0:T(128)} %pad_add_fusion.place_ref, ...), custom_call_target="tpu_custom_call", output_to_operand_aliasing={{0}: (11, {}), {1}: (12, {}), {2}: (13, {}), {3}: (14, {}),... | custom-call | flops 2000000000 | bytes 6000000 | tf_op jit(solution)/shard_map/project/pallas_call | solution.py:448
  101.9 19.9 %attend.1 = (f32[2048,128]{1,0:T(8,128)}, bf16[2048,128]{1,0:T(8,128)(2,1)}, f32[8,2048]{1,0:T(8,128)}) custom-call(bf16[2048,128]{1,0:T(8,128)(2,1)} %get-tuple-element.111.q_ref, bf16[2048,128]{1,0:T(8,128)(2,1)} %and_convert_fusion.member_ref, bf16[2048,256]{1,0:T(8,128)(2,1)} %get-tuple-element.112.k_ref, bf16[128,2048]{1,0:T(8,128)(2,1)} %get-tuple-element.113.vt_ref), custom_call_target="tpu_custom_call" | custom-call | flops 17999998976 | bytes 54000000 | tf_op jit(solution)/shard_map/attend/pallas_call | solution.py:505
  121.9 5.7 %all-to-all-start.2 = ((bf16[8,256,128]{2,1,0:T(8,128)(2,1)}), bf16[8,256,128]{2,1,0:T(8,128)(2,1)S(1)}, u32[]{:S(2)}, u32[]{:S(2)}) async-start(bf16[8,256,128]{2,1,0:T(8,128)(2,1)} %bitcast.127), calls=%async_computation.2 | async-start | bytes 1048576 | tf_op jit(solution)/shard_map/all_to_all | solution.py:356
  128.6 6.7 %collective-permute-done.11 = bf16[768,128]{1,0:T(8,128)(2,1)S(1)} collective-permute-done((bf16[768,128]{1,0:T(8,128)(2,1)S(1)}, bf16[768,128]{1,0:T(8,128)(2,1)S(1)}, u32[]{:S(2)}, u32[]{:S(2)}) %collective-permute-start.11) | collective-permute-done | bytes 196640 | tf_op jit(solution)/shard_map/ppermute | solution.py:352
  136.9 20.8 %middle.1 = (bf16[256,1024]{1,0:T(8,128)(2,1)}, f32[256,1024]{1,0:T(8,128)}, bf16[8,256,128]{2,1,0:T(8,128)(2,1)}, f32[16,4096]{1,0:T(8,128)}, bf16[4096,256]{1,0:T(8,128)(2,1)}, /*index=5*/bf16[256,4096]{1,0:T(8,128)(2,1)}) custom-call(bf16[8,256,128]{2,1,0:T(8,128)(2,1)} %copy-done.16, bf16[256,1024]{1,0:T(8,128)(2,1)} %bitcast.118, ...), custom_call_target="tpu_custom_call" | custom-call | flops 20000000000 | bytes 60000000 | tf_op jit(solution)/shard_map/middle/pallas_call | solution.py:754
  157.8 9.9 %collective-permute-start.14 = (bf16[4096,256]{1,0:T(8,128)(2,1)}, bf16[4096,256]{1,0:T(8,128)(2,1)}, u32[]{:S(2)}, u32[]{:S(2)}) collective-permute-start(bf16[4096,256]{1,0:T(8,128)(2,1)} %get-tuple-element.126.down_l.up_l.out_l), channel_id=1, source_target_pairs={{0,1},{1,0},{2,3},{3,2},{4,5},{5,4},{6,7},{7,6},{8,9},{9,8},{10,11... | collective-permute-start | bytes 6291464 | tf_op jit(solution)/shard_map/ppermute | solution.py:352
  167.7 5.9 %all-to-all-start.3 = ((bf16[8,256,128]{2,1,0:T(8,128)(2,1)}), bf16[8,256,128]{2,1,0:T(8,128)(2,1)S(1)}, u32[]{:S(2)}, u32[]{:S(2)}) async-start(bf16[8,256,128]{2,1,0:T(8,128)(2,1)} %get-tuple-element.122), calls=%async_computation.3 | async-start | bytes 1048576 | tf_op jit(solution)/shard_map/all_to_all | solution.py:356
  174.8 8.6 %weight_grads.1 = (bf16[8,512,128]{2,1,0:T(8,128)(2,1)}, bf16[8,512,128]{2,1,0:T(8,128)(2,1)}, bf16[2,4,768,128]{3,2,1,0:T(8,128)(2,1)}, bf16[2,4,768,128]{3,2,1,0:T(8,128)(2,1)}) custom-call(s32[3]{0:T(128)} %pad_add_fusion.1.place_ref, bf16[4096,256]{1,0:T(8,128)(2,1)} %get-tuple-element.126.down_l.up_l.out_l, ...), custom_call_target="tpu_custom_call" | custom-call | flops 8999999488 | bytes 27000000 | tf_op jit(solution)/shard_map/weight_grads/pallas_call | solution.py:825
  186.3 28.5 %attend_back.1.g_ref = bf16[2048,384]{1,0:T(8,128)(2,1)} custom-call(bf16[2048,128]{1,0:T(8,128)(2,1)} %get-tuple-element.111.q_ref, bf16[2048,128]{1,0:T(8,128)(2,1)} %and_convert_fusion.member_ref, bf16[2048,128]{1,0:T(8,128)(2,1)} %bitcast.126, f32[2048,128]{1,0:T(8,128)} %get-tuple-element.131.att_ref, f32[8,2048]{1,0:T(8,128)} %get-tuple-element.132.log_ref, ...), custom_call_target="tpu_custom_call" | custom-call | flops 27000000512 | bytes 81000000 | tf_op jit(solution)/shard_map/attend_back/pallas_call | solution.py:572
  214.8 6.3 %all-to-all-start.4 = ((bf16[8,256,384]{2,1,0:T(8,128)(2,1)}), bf16[8,256,384]{2,1,0:T(8,128)(2,1)S(1)}, u32[]{:S(2)}, u32[]{:S(2)}) async-start(bf16[8,256,384]{2,1,0:T(8,128)(2,1)} %bitcast.120), calls=%async_computation.4 | async-start | bytes 3145728 | tf_op jit(solution)/shard_map/all_to_all | solution.py:356
  239.8 10.9 %clip_grads.1 = f32[16,2048]{1,0:T(8,128)} custom-call(s32[2]{0:T(128)} %pad_add_fusion.place_ref, bf16[2048,1024]{1,0:T(8,128)(2,1)} %get-tuple-element.121.x_ref, s32[1,2048]{1,0:T(1,128)} %and_select_fusion.clip_ref, bf16[2048,384]{1,0:T(8,128)(2,1)} %attend_back.1.g_ref, bf16[4,256,384]{2,1,0:T(8,128)(2,1)} %copy-done.7), custom_call_target="tpu_custom_call" | custom-call | flops 8999999488 | bytes 27000000 | tf_op jit(solution)/shard_map/clip_grads/pallas_call | solution.py:856
  250.7 6.0 %convolution_convert_fusion = bf16[1024,384]{1,0:T(8,128)(2,1)} fusion(bf16[2048,1024]{1,0:T(8,128)(2,1)} %get-tuple-element.143, bf16[2048,384]{1,0:T(8,128)(2,1)} %attend_back.1.g_ref), kind=kOutput, calls=%fused_computation.18 | convolution fusion | flops 1611005952 | bytes 6553600 | tf_op jit(solution)/shard_map/dot_general | solution.py:29
  266.8 5.6 %collective-permute-start.29 = (bf16[1280,128]{1,0:T(8,128)(2,1)S(1)}, bf16[1280,128]{1,0:T(8,128)(2,1)S(1)}, u32[]{:S(2)}, u32[]{:S(2)}) collective-permute-start(bf16[1280,128]{1,0:T(8,128)(2,1)S(1)} %get-tuple-element.165), channel_id=1, source_target_pairs={{0,8},{4,12},{8,0},{12,4},{16,24},{20,28},{24,16},{28,20},{1,9},{5... | collective-permute-start | bytes 983048 | tf_op jit(solution)/shard_map/ppermute | solution.py:352
  275.9 5.6 %last.1 = bf16[256,1024]{1,0:T(8,128)(2,1)} custom-call(s32[3]{0:T(128)S(1)} %copy-done.3, bf16[8,256,384]{2,1,0:T(8,128)(2,1)S(1)} %all-to-all-done.4.own_ref, bf16[256,1024]{1,0:T(8,128)(2,1)S(1)} %bitcast.119, f32[256,1024]{1,0:T(8,128)S(1)} %copy-done.5, bf16[256,128]{1,0:T(8,128)(2,1)S(1)} %copy-done.2, bf16[128,6144]{1,0:T(8,128)(2,1)S(1)} %copy-done.1, ...), custom_call_target="tpu_custom_call" | custom-call | flops 4000000000 | bytes 12000000 | tf_op jit(solution)/shard_map/last/pallas_call | solution.py:905
  285.4 6.8 %all_gather.15 = f32[64,768]{1,0:T(8,128)S(1)} all-gather(f32[16,768]{1,0:T(8,128)S(1)} %fusion.28), channel_id=1, replica_groups=mesh['seq'=8,'batch'=4] {'batch'}, dimensions={0}, use_global_device_ids=true | all-gather | bytes 245760 | tf_op jit(solution)/shard_map/all_gather | solution.py:1074
  295.2 9.5 %collective-permute-done.30 = bf16[1280,128]{1,0:T(8,128)(2,1)S(1)} collective-permute-done((bf16[1280,128]{1,0:T(8,128)(2,1)S(1)}, bf16[1280,128]{1,0:T(8,128)(2,1)S(1)}, u32[]{:S(2)}, u32[]{:S(2)}) %collective-permute-start.30) | collective-permute-done | bytes 327712 | tf_op jit(solution)/shard_map/ppermute | solution.py:352
  304.7 8.6 %collective-permute-done.31 = bf16[1280,128]{1,0:T(8,128)(2,1)S(1)} collective-permute-done((bf16[1280,128]{1,0:T(8,128)(2,1)S(1)}, bf16[1280,128]{1,0:T(8,128)(2,1)S(1)}, u32[]{:S(2)}, u32[]{:S(2)}) %collective-permute-start.31) | collective-permute-done | bytes 327712 | tf_op jit(solution)/shard_map/ppermute | solution.py:352
  (223 shorter events, 84.0 us)
Async XLA Ops:
  7.2 22.6 %collective-permute-start = (bf16[256,1024]{1,0:T(8,128)(2,1)}, bf16[256,1024]{1,0:T(8,128)(2,1)S(1)}, u32[]{:S(2)}, u32[]{:S(2)}) collective-permute-start(bf16[256,1024]{1,0:T(8,128)(2,1)} %bitcast.114), channel_id=1, source_target_pairs={{0,8},{4,12},{8,0},{12,4},{16,24},{20,28},{24,16},{28,20},{1,9},{5... | collective-permute-start | bytes 1572872 | tf_op jit(solution)/shard_map/ppermute | solution.py:352
  7.5 25.2 %collective-permute-start.1 = (bf16[256,1024]{1,0:T(8,128)(2,1)}, bf16[256,1024]{1,0:T(8,128)(2,1)}, u32[]{:S(2)}, u32[]{:S(2)}) collective-permute-start(bf16[256,1024]{1,0:T(8,128)(2,1)} %bitcast.115), channel_id=1, source_target_pairs={{0,16},{4,20},{8,24},{12,28},{16,0},{20,4},{24,8},{28,12},{1,17},{... | collective-permute-start | bytes 1572872 | tf_op jit(solution)/shard_map/ppermute | solution.py:352
  9.8 22.9 %collective-permute-start.2 = (bf16[256,1024]{1,0:T(8,128)(2,1)}, bf16[256,1024]{1,0:T(8,128)(2,1)S(1)}, u32[]{:S(2)}, u32[]{:S(2)}) collective-permute-start(bf16[256,1024]{1,0:T(8,128)(2,1)} %bitcast.116), channel_id=1, source_target_pairs={{0,4},{4,0},{8,12},{12,8},{16,20},{20,16},{24,28},{28,24},{1,5},{5... | collective-permute-start | bytes 1572872 | tf_op jit(solution)/shard_map/ppermute | solution.py:352
  25.2 111.7 %all-gather.4.cloned.1.call-start = ((), (), s32[]{:S(2)}) async-start(), calls=%async_computation.5 | async-start | bytes 10813440 | tf_op jit(solution)/shard_map/all_gather | solution.py:971
  33.6 36.4 %all-to-all-start.1 = ((f32[8,24,768]{2,1,0:T(8,128)}), f32[8,24,768]{2,1,0:T(8,128)S(1)}, u32[]{:S(2)}, u32[]{:S(2)}) async-start(f32[8,24,768]{2,1,0:T(8,128)} %broadcast_in_dim.16), calls=%async_computation.1 | async-start | bytes 1179648 | tf_op jit(solution)/shard_map/all_to_all | solution.py:356
  37.8 25.1 %collective-permute-start.4 = (bf16[256,1024]{1,0:T(8,128)(2,1)}, bf16[256,1024]{1,0:T(8,128)(2,1)}, u32[]{:S(2)}, u32[]{:S(2)}) collective-permute-start(bf16[256,1024]{1,0:T(8,128)(2,1)} %collective-permute-done.1.c_ref), channel_id=1, source_target_pairs={{0,8},{4,12},{8,0},{12,4},{16,24},{20,28},{24,16},{28,20},{1,9},{5... | collective-permute-start | bytes 1572872 | tf_op jit(solution)/shard_map/ppermute | solution.py:352
  38.1 29.2 %collective-permute-start.6 = (bf16[256,1024]{1,0:T(8,128)(2,1)}, bf16[256,1024]{1,0:T(8,128)(2,1)S(1)}, u32[]{:S(2)}, u32[]{:S(2)}) collective-permute-start(bf16[256,1024]{1,0:T(8,128)(2,1)} %collective-permute-done.1.c_ref), channel_id=1, source_target_pairs={{0,4},{4,0},{8,12},{12,8},{16,20},{20,16},{24,28},{28,24},{1,5},{5... | collective-permute-start | bytes 1572872 | tf_op jit(solution)/shard_map/ppermute | solution.py:352
  38.1 29.2 %collective-permute-start.5 = (bf16[256,1024]{1,0:T(8,128)(2,1)}, bf16[256,1024]{1,0:T(8,128)(2,1)S(1)}, u32[]{:S(2)}, u32[]{:S(2)}) collective-permute-start(bf16[256,1024]{1,0:T(8,128)(2,1)} %copy-done.32), channel_id=1, source_target_pairs={{0,4},{4,0},{8,12},{12,8},{16,20},{20,16},{24,28},{28,24},{1,5},{5... | collective-permute-start | bytes 1572872 | tf_op jit(solution)/shard_map/ppermute | solution.py:352
  67.3 22.6 %collective-permute-start.8 = (bf16[256,1024]{1,0:T(8,128)(2,1)}, bf16[256,1024]{1,0:T(8,128)(2,1)}, u32[]{:S(2)}, u32[]{:S(2)}) collective-permute-start(bf16[256,1024]{1,0:T(8,128)(2,1)} %collective-permute-done.4.d_ref), channel_id=1, source_target_pairs={{0,4},{4,0},{8,12},{12,8},{16,20},{20,16},{24,28},{28,24},{1,5},{5... | collective-permute-start | bytes 1572872 | tf_op jit(solution)/shard_map/ppermute | solution.py:352
  89.9 31.9 %collective-permute-start.9 = (bf16[768,128]{1,0:T(8,128)(2,1)S(1)}, bf16[768,128]{1,0:T(8,128)(2,1)S(1)}, u32[]{:S(2)}, u32[]{:S(2)}) collective-permute-start(bf16[768,128]{1,0:T(8,128)(2,1)S(1)} %pad_maximum_fusion.7), channel_id=1, source_target_pairs={{0,8},{4,12},{8,0},{12,4},{16,24},{20,28},{24,16},{28,20},{1,9},{5... | collective-permute-start | bytes 589832 | tf_op jit(solution)/shard_map/ppermute | solution.py:352
  93.1 28.8 %collective-permute-start.10 = (bf16[768,128]{1,0:T(8,128)(2,1)S(1)}, bf16[768,128]{1,0:T(8,128)(2,1)S(1)}, u32[]{:S(2)}, u32[]{:S(2)}) collective-permute-start(bf16[768,128]{1,0:T(8,128)(2,1)S(1)} %pad_maximum_fusion.7), channel_id=1, source_target_pairs={{0,16},{4,20},{8,24},{12,28},{16,0},{20,4},{24,8},{28,12},{1,17},{... | collective-permute-start | bytes 589832 | tf_op jit(solution)/shard_map/ppermute | solution.py:352
  135.5 22.3 %collective-permute-start.12 = (bf16[4,768,128]{2,1,0:T(8,128)(2,1)S(1)}, bf16[4,768,128]{2,1,0:T(8,128)(2,1)}, u32[]{:S(2)}, u32[]{:S(2)}) collective-permute-start(bf16[4,768,128]{2,1,0:T(8,128)(2,1)S(1)} %pad_maximum_fusion.1), channel_id=1, source_target_pairs={{0,4},{4,0},{8,12},{12,8},{16,20},{20,16},{24,28},{28,24},{1,5},{5... | collective-permute-start | bytes 2359304 | tf_op jit(solution)/shard_map/ppermute | solution.py:352
  135.7 22.1 %collective-permute-start.13 = (bf16[4,768,128]{2,1,0:T(8,128)(2,1)S(1)}, bf16[4,768,128]{2,1,0:T(8,128)(2,1)S(1)}, u32[]{:S(2)}, u32[]{:S(2)}) collective-permute-start(bf16[4,768,128]{2,1,0:T(8,128)(2,1)S(1)} %pad_maximum_fusion.1), channel_id=1, source_target_pairs={{0,2},{1,3},{2,0},{3,1},{4,6},{5,7},{6,4},{7,5},{8,10},{9,11},{10,... | collective-permute-start | bytes 2359304 | tf_op jit(solution)/shard_map/ppermute | solution.py:352
  174.2 50.2 %collective-permute-start.18 = (bf16[4,768,128]{2,1,0:T(8,128)(2,1)}, bf16[4,768,128]{2,1,0:T(8,128)(2,1)S(1)}, u32[]{:S(2)}, u32[]{:S(2)}) collective-permute-start(bf16[4,768,128]{2,1,0:T(8,128)(2,1)} %collective-permute-done.12), channel_id=1, source_target_pairs={{0,2},{1,3},{2,0},{3,1},{4,6},{5,7},{6,4},{7,5},{8,10},{9,11},{10,... | collective-permute-start | bytes 2359304 | tf_op jit(solution)/shard_map/ppermute | solution.py:352
  185.6 35.6 %collective-permute-start.16 = (bf16[8,512,128]{2,1,0:T(8,128)(2,1)}, bf16[8,512,128]{2,1,0:T(8,128)(2,1)}, u32[]{:S(2)}, u32[]{:S(2)}) collective-permute-start(bf16[8,512,128]{2,1,0:T(8,128)(2,1)} %get-tuple-element.136), channel_id=1, source_target_pairs={{0,2},{1,3},{2,0},{3,1},{4,6},{5,7},{6,4},{7,5},{8,10},{9,11},{10,... | collective-permute-start | bytes 3145736 | tf_op jit(solution)/shard_map/ppermute | solution.py:352
  185.6 38.8 %collective-permute-start.17 = (bf16[2,4,768,128]{3,2,1,0:T(8,128)(2,1)}, bf16[2,4,768,128]{3,2,1,0:T(8,128)(2,1)}, u32[]{:S(2)}, u32[]{:S(2)}) collective-permute-start(bf16[2,4,768,128]{3,2,1,0:T(8,128)(2,1)} %get-tuple-element.139), channel_id=1, source_target_pairs={{0,4},{4,0},{8,12},{12,8},{16,20},{20,16},{24,28},{28,24},{1,5},{5... | collective-permute-start | bytes 4718600 | tf_op jit(solution)/shard_map/ppermute | solution.py:352
  214.8 42.4 %all-to-all-start.4 = ((bf16[8,256,384]{2,1,0:T(8,128)(2,1)}), bf16[8,256,384]{2,1,0:T(8,128)(2,1)S(1)}, u32[]{:S(2)}, u32[]{:S(2)}) async-start(bf16[8,256,384]{2,1,0:T(8,128)(2,1)} %bitcast.120), calls=%async_computation.4 | async-start | bytes 3145728 | tf_op jit(solution)/shard_map/all_to_all | solution.py:356
  231.7 25.4 %collective-permute-start.21 = (bf16[12,768,128]{2,1,0:T(8,128)(2,1)}, bf16[12,768,128]{2,1,0:T(8,128)(2,1)}, u32[]{:S(2)}, u32[]{:S(2)}) collective-permute-start(bf16[12,768,128]{2,1,0:T(8,128)(2,1)} %constant_dynamic-update-slice_fusion.2.refs_0_), channel_id=1, source_target_pairs={{0,1},{1,0},{2,3},{3,2},{4,5},{5,4},{6,7},{7,6},{8,9},{9,8},{10,11... | collective-permute-start | bytes 7077896 | tf_op jit(solution)/shard_map/ppermute | solution.py:352
  234.1 40.8 %collective-permute-start.22 = (bf16[4,768,128]{2,1,0:T(8,128)(2,1)S(1)}, bf16[4,768,128]{2,1,0:T(8,128)(2,1)S(1)}, u32[]{:S(2)}, u32[]{:S(2)}) collective-permute-start(bf16[4,768,128]{2,1,0:T(8,128)(2,1)S(1)} %collective-permute-done.18.refs_1_), channel_id=1, source_target_pairs={{0,1},{1,0},{2,3},{3,2},{4,5},{5,4},{6,7},{7,6},{8,9},{9,8},{10,11... | collective-permute-start | bytes 2359304 | tf_op jit(solution)/shard_map/ppermute | solution.py:352
  235.4 21.3 %collective-permute-start.19 = (bf16[4,512,128]{2,1,0:T(8,128)(2,1)S(1)}, bf16[4,512,128]{2,1,0:T(8,128)(2,1)}, u32[]{:S(2)}, u32[]{:S(2)}) collective-permute-start(bf16[4,512,128]{2,1,0:T(8,128)(2,1)S(1)} %slice.171), channel_id=1, source_target_pairs={{0,4},{4,0},{8,12},{12,8},{16,20},{20,16},{24,28},{28,24},{1,5},{5... | collective-permute-start | bytes 1572872 | tf_op jit(solution)/shard_map/ppermute | solution.py:352
  262.0 30.2 %collective-permute-start.27 = (bf16[2,256,384]{2,1,0:T(8,128)(2,1)S(1)}, bf16[2,256,384]{2,1,0:T(8,128)(2,1)S(1)}, u32[]{:S(2)}, u32[]{:S(2)}) collective-permute-start(bf16[2,256,384]{2,1,0:T(8,128)(2,1)S(1)} %dynamic-slice_bitcast_fusion), channel_id=1, source_target_pairs={{0,1},{1,0},{2,3},{3,2},{4,5},{5,4},{6,7},{7,6},{8,9},{9,8},{10,11... | collective-permute-start | bytes 1179656 | tf_op jit(solution)/shard_map/ppermute | solution.py:352
  266.8 28.4 %collective-permute-start.29 = (bf16[1280,128]{1,0:T(8,128)(2,1)S(1)}, bf16[1280,128]{1,0:T(8,128)(2,1)S(1)}, u32[]{:S(2)}, u32[]{:S(2)}) collective-permute-start(bf16[1280,128]{1,0:T(8,128)(2,1)S(1)} %get-tuple-element.165), channel_id=1, source_target_pairs={{0,8},{4,12},{8,0},{12,4},{16,24},{20,28},{24,16},{28,20},{1,9},{5... | collective-permute-start | bytes 983048 | tf_op jit(solution)/shard_map/ppermute | solution.py:352
  281.5 23.2 %collective-permute-start.30 = (bf16[1280,128]{1,0:T(8,128)(2,1)S(1)}, bf16[1280,128]{1,0:T(8,128)(2,1)S(1)}, u32[]{:S(2)}, u32[]{:S(2)}) collective-permute-start(bf16[1280,128]{1,0:T(8,128)(2,1)S(1)} %get-tuple-element.164), channel_id=1, source_target_pairs={{0,16},{4,20},{8,24},{12,28},{16,0},{20,4},{24,8},{28,12},{1,17},{... | collective-permute-start | bytes 983048 | tf_op jit(solution)/shard_map/ppermute | solution.py:352
  284.1 29.2 %collective-permute-start.31 = (bf16[1280,128]{1,0:T(8,128)(2,1)S(1)}, bf16[1280,128]{1,0:T(8,128)(2,1)S(1)}, u32[]{:S(2)}, u32[]{:S(2)}) collective-permute-start(bf16[1280,128]{1,0:T(8,128)(2,1)S(1)} %get-tuple-element.163), channel_id=1, source_target_pairs={{0,24},{4,28},{8,16},{12,20},{16,8},{20,12},{24,0},{28,4},{1,25},{... | collective-permute-start | bytes 983048 | tf_op jit(solution)/shard_map/ppermute | solution.py:352
  (47 other events, 526.9 us)
Sparse Core Ops, SparseCore 0:
  33.7 98.6 all-gather.3
